TPU v7x, 32 devices: a whole 2x2x4 slice. The times are simulated.
32 devices in a mesh: case: 2 (over x), wide: 16 (over z, y, core).
Axes of the slice: x: 2, y: 2, z: 4, core: 2. Of those that a mesh axis runs over, the one named last changes fastest.
Arguments:
- flow: bfloat16 [5, 16, 65536], P(None, None, ('case', 'wide')), parts along dimension 2, may hold values from -6 to 6
- positions: bfloat16 [3, 65536], P(None, ('case', 'wide')), parts along dimension 1, may hold values from -1.1953125 to 1.1953125
- normals: bfloat16 [3, 65536], P(None, ('case', 'wide')), parts along dimension 1, may hold values from -6 to 6
- panel_ids: int32 [65536], P(('case', 'wide')), parts along dimension 0, may hold values from 0 to 32767, as said below
- observers: float32 [2, 512], P(None, ('case', 'wide')), parts along dimension 1, may hold values from -6 to 6
Outputs:
- panel_spectra: bfloat16 [32, 65536], P(None, ('case', 'wide')), parts along dimension 1
- pressure: float32 [512, 8], P(('case', 'wide')), parts along dimension 0
There are 2 independent parts, one for each index of `case`. A program takes and returns all parts, laid end to end along the dimension named above; each array names one. Nothing has to cross between parts.
Inputs may be any that keep to these rules, and one draw needn't show every extreme that they name: `panel_ids`: every number 0 to 32767 appears exactly once; panel g belongs to device g // 2048 of wide at local position g % 2048, so every device owns exactly 2048 panels. The 2048 columns of one device name each owner at most 256 times, and every device names some owner exactly 256 times.
All inputs are finite; a program needn't handle non-finite values.
Results may differ from a plain program's by a relative error of at most 0.0034.
Values may be sent and summed in bfloat16 or wider, within the bound.
No kernel may reach another device: no remote copies, remote signals or barrier semaphores. Data moves between devices by JAX's collectives and lax.ppermute only.
A program may use at most 192 MiB of HBM per device.

v0:
```python
import math

import jax
import jax.numpy as jnp
from jax import lax
from jax.sharding import PartitionSpec as P

NT = 16
HARM = 4


WAVENUMBER = 2.0
GROUND = 3.0


def dft_table():
    samples = jnp.arange(NT, dtype=jnp.float32)[:, None]
    harmonic = jnp.arange(1, HARM + 1, dtype=jnp.float32)[None, :]
    angle = 2.0 * math.pi / NT * samples * harmonic
    table = jnp.stack([jnp.cos(angle), -jnp.sin(angle)], axis=2) * (2.0 / NT)
    return table.reshape(NT, 2 * HARM)


def spectra_of(flow, normals):
    values = flow.astype(jnp.float32)
    normal_vec = normals.astype(jnp.float32)[:, None, :]
    density = 1.0 + 0.2 * values[0]
    velocity = 0.5 * values[1:4]
    fluctuation = values[4]
    normal_vel = jnp.sum(velocity * normal_vec, axis=0)
    source = density * normal_vel
    loads = fluctuation[None] * normal_vec + density[None] * velocity * normal_vel[None]
    quantities = jnp.concatenate([source[None], loads], axis=0)
    spectra = jnp.einsum("qtp,tc->qcp", quantities, dft_table(), precision=lax.Precision.HIGHEST)
    return spectra.reshape(8 * HARM, -1).astype(jnp.bfloat16)


def pressure_sums(spectra, positions, listeners):
    parts = spectra.astype(jnp.float32).reshape(4, HARM, 2, -1)
    place = positions.astype(jnp.float32)
    delta_x = listeners[0][:, None] - place[0][None, :]
    delta_y = listeners[1][:, None] - place[1][None, :]
    delta_z = -GROUND - place[2][None, :]
    distance = jnp.sqrt(delta_x * delta_x + delta_y * delta_y + delta_z * delta_z)
    inverse = 1.0 / distance
    unit_x = delta_x * inverse
    unit_y = delta_y * inverse
    unit_z = delta_z * inverse
    columns = []
    for harmonic in range(HARM):
        wavenum = WAVENUMBER * (harmonic + 1)
        source_re = parts[0, harmonic, 0][None, :]
        source_im = parts[0, harmonic, 1][None, :]
        along_re = (
            parts[1, harmonic, 0][None, :] * unit_x
            + parts[2, harmonic, 0][None, :] * unit_y
            + parts[3, harmonic, 0][None, :] * unit_z
        )
        along_im = (
            parts[1, harmonic, 1][None, :] * unit_x
            + parts[2, harmonic, 1][None, :] * unit_y
            + parts[3, harmonic, 1][None, :] * unit_z
        )
        bracket_re = -wavenum * source_im + along_re * inverse - wavenum * along_im
        bracket_im = wavenum * source_re + along_im * inverse + wavenum * along_re
        phase = wavenum * distance
        cosine = jnp.cos(phase)
        sine = jnp.sin(phase)
        columns.append(jnp.sum((cosine * bracket_re + sine * bracket_im) * inverse, axis=1))
        columns.append(jnp.sum((cosine * bracket_im - sine * bracket_re) * inverse, axis=1))
    return jnp.stack(columns, axis=1)


def shards(flow, positions, normals, panel_ids, observers):
    owned = flow.shape[2]
    nwide = lax.axis_size("wide")
    capacity = 2 * owned // nwide
    total = nwide * capacity
    owner = panel_ids // owned
    local = panel_ids - owner * owned
    onehot = (owner[:, None] == jnp.arange(nwide, dtype=jnp.int32)[None, :]).astype(jnp.int32)
    rank = jnp.sum(jnp.cumsum(onehot, axis=0) * onehot, axis=1) - 1
    slot = owner * capacity + rank

    def pack(columns, filler):
        empty = jnp.full(columns.shape[:-1] + (total,), filler, columns.dtype)
        return empty.at[:, slot].set(columns)

    slot_local = pack(local[None, :], owned)
    received = (
        lax.all_to_all(
            pack(flow.reshape(5 * NT, owned), 0), "wide", split_axis=1, concat_axis=1, tiled=True
        ),
        lax.all_to_all(pack(positions, 0), "wide", split_axis=1, concat_axis=1, tiled=True),
        lax.all_to_all(pack(normals, 0), "wide", split_axis=1, concat_axis=1, tiled=True),
        lax.all_to_all(slot_local, "wide", split_axis=1, concat_axis=1, tiled=True),
    )
    slot_spectra = spectra_of(received[0].reshape(5, NT, total), received[2])
    slot_place = received[1]
    slot_index = received[3][0]
    panel_spectra = (
        jnp.zeros((8 * HARM, owned), jnp.bfloat16).at[:, slot_index].set(slot_spectra, mode="drop")
    )
    owned_place = jnp.zeros((3, owned), jnp.bfloat16).at[:, slot_index].set(slot_place, mode="drop")
    scale = 2.0 / math.sqrt(owned * nwide)
    listeners = observers.shape[1]
    initial = jnp.zeros((listeners, 2 * HARM), jnp.float32)
    spectra = lax.all_gather(panel_spectra, "wide", axis=1, tiled=True)
    place = lax.all_gather(owned_place, "wide", axis=1, tiled=True)
    count = spectra.shape[1]
    width = math.gcd(count, 16384)

    def step(index, acc):
        part_spec = lax.dynamic_slice_in_dim(spectra, index * width, width, 1)
        part_place = lax.dynamic_slice_in_dim(place, index * width, width, 1)
        return acc + pressure_sums(part_spec, part_place, observers)

    summed = lax.fori_loop(0, count // width, step, initial)
    pressure = summed * scale
    return (panel_spectra, pressure)


def solution(mesh):
    placed = (
        P(None, None, ("case", "wide")),
        P(None, ("case", "wide")),
        P(None, ("case", "wide")),
        P(("case", "wide")),
        P(None, ("case", "wide")),
    )
    return jax.shard_map(
        shards,
        mesh=mesh,
        in_specs=placed,
        out_specs=(P(None, ("case", "wide")), P(("case", "wide"), None)),
        check_vma=False,
    )
```

profile of v0, /device:TPU:0, one launch (start us, length us, event | category | flops | bytes accessed | tf_op | source)
XLA Modules:
  0.0 312.7 jit_solution(13018767336382383730)
XLA Ops:
  7.2 0.8 add_select_fusion
  7.9 4.5 %reduce-window.6 = s32[16,16,128]{2,1,0:T(8,128)S(1)} reduce-window(s32[16,16,128]{2,1,0:T(8,128)S(1)} %fusion.60, s32[]{:T(128)} %constant.139.clone.1), window={size=1x1x128 pad=0_0x0_0x127_0}, to_apply=%region_0.1 | reduce-window | flops 4161536 | bytes 262148 | tf_op jit(solution)/shard_map/reduce-window
  12.5 0.4 slice_reduce_fusion
  13.3 0.7 multiply_subtract_fusion.4
  14.0 8.6 %scatter_custom_fusion = s32[4096]{0:T(1024)} fusion(s32[2048]{0:T(1024)S(1)} %get-tuple-element.218, s32[2048]{0:T(1024)S(1)} %get-tuple-element.217, s32[]{:T(128)} %constant.137.clone.1), kind=kCustom, calls=%fused_computation.129 | custom fusion | bytes 16388 | tf_op jit(solution)/shard_map/scatter | solution.py:87
  22.6 7.4 %all-to-all-start = ((s32[1,16,256]{2,0,1:T(1,128)}), s32[1,16,256]{2,0,1:T(1,128)S(1)}, u32[]{:S(2)}, u32[]{:S(2)}) async-start(s32[1,16,256]{2,0,1:T(1,128)} %bitcast.2), calls=%async_computation | async-start | bytes 32768 | tf_op jit(solution)/shard_map/all_to_all | solution.py:96
  30.1 1.0 copy.70
  31.2 6.1 %scatter_custom_fusion.2 = bf16[3,4096]{0,1:T(8,128)(2,1)S(1)} fusion(s32[2048]{0:T(1024)S(1)} %get-tuple-element.218, bf16[2048,3]{1,0:T(8,128)(2,1)S(1)} %copy.70, bf16[]{:T(256)} %constant.136.clone.1), kind=kCustom, calls=%fused_computation.102 | custom fusion | bytes 24578 | tf_op jit(solution)/shard_map/scatter | solution.py:87
  37.2 1.0 copy.71
  38.3 6.0 %all-to-all-start.2 = ((bf16[3,16,256]{2,0,1:T(4,128)(2,1)}), bf16[3,16,256]{2,0,1:T(4,128)(2,1)S(1)}, u32[]{:S(2)}, u32[]{:S(2)}) async-start(bf16[3,16,256]{2,0,1:T(4,128)(2,1)} %copy.71), calls=%async_computation.2 | async-start | bytes 65536 | tf_op jit(solution)/shard_map/all_to_all | solution.py:95
  44.6 6.1 %scatter_custom_fusion.1 = bf16[80,4096]{0,1:T(8,128)(2,1)S(1)} fusion(s32[2048]{0:T(1024)S(1)} %get-tuple-element.218, bf16[80,2048]{0,1:T(8,128)(2,1)S(1)} %copy.66, bf16[]{:T(256)} %constant.136.clone.1), kind=kCustom, calls=%fused_computation.98 | custom fusion | bytes 1179650 | tf_op jit(solution)/shard_map/scatter | solution.py:87
  50.6 1.2 copy.67
  51.9 6.0 %all-to-all-start.1 = ((bf16[80,16,256]{2,0,1:T(8,128)(2,1)}), bf16[80,16,256]{2,0,1:T(8,128)(2,1)S(1)}, u32[]{:S(2)}, u32[]{:S(2)}) async-start(bf16[80,16,256]{2,0,1:T(8,128)(2,1)} %copy.67), calls=%async_computation.1 | async-start | bytes 1310720 | tf_op jit(solution)/shard_map/all_to_all | solution.py:91
  58.0 16.5 %all-to-all-done.1 = bf16[80,16,256]{2,0,1:T(8,128)(2,1)S(1)} async-done(((bf16[80,16,256]{2,0,1:T(8,128)(2,1)}), bf16[80,16,256]{2,0,1:T(8,128)(2,1)S(1)}, u32[]{:S(2)}, u32[]{:S(2)}) %all-to-all-start.1) | async-done | bytes 655392 | tf_op jit(solution)/shard_map/all_to_all | solution.py:91
  74.6 0.5 copy.69
  75.9 0.6 fusion.41
  76.5 0.5 copy.73
  77.0 11.5 %scatter_custom_fusion.3 = bf16[32,2048]{0,1:T(8,128)(2,1)} fusion(s32[4096]{0:T(1024)S(1)} %bitcast.251, bf16[32,4096]{0,1:T(8,128)(2,1)S(1)} %copy.73, bf16[]{:T(256)} %constant.136.clone.1), kind=kCustom, calls=%fused_computation.94 | custom fusion | bytes 1179650 | tf_op jit(solution)/shard_map/scatter | solution.py:102
  88.8 6.1 %scatter_custom_fusion.4 = bf16[3,4096]{0,1:T(8,128)(2,1)S(1)} fusion(s32[2048]{0:T(1024)S(1)} %get-tuple-element.218, bf16[2048,3]{1,0:T(8,128)(2,1)S(1)} %copy.74, bf16[]{:T(256)} %constant.136.clone.1), kind=kCustom, calls=%fused_computation.100 | custom fusion | bytes 24578 | tf_op jit(solution)/shard_map/scatter | solution.py:87
  94.9 1.0 copy.75
  95.9 4.8 %all-to-all-start.3 = ((bf16[3,16,256]{2,0,1:T(4,128)(2,1)}), bf16[3,16,256]{2,0,1:T(4,128)(2,1)S(1)}, u32[]{:S(2)}, u32[]{:S(2)}) async-start(bf16[3,16,256]{2,0,1:T(4,128)(2,1)} %copy.75), calls=%async_computation.3 | async-start | bytes 65536 | tf_op jit(solution)/shard_map/all_to_all | solution.py:94
  100.7 7.2 %all-to-all-done.3 = bf16[3,16,256]{2,0,1:T(4,128)(2,1)S(1)} async-done(((bf16[3,16,256]{2,0,1:T(4,128)(2,1)}), bf16[3,16,256]{2,0,1:T(4,128)(2,1)S(1)}, u32[]{:S(2)}, u32[]{:S(2)}) %all-to-all-start.3) | async-done | bytes 24608 | tf_op jit(solution)/shard_map/all_to_all | solution.py:94
  107.9 0.5 copy.76
  108.4 10.9 %scatter_custom_fusion.5 = bf16[3,2048]{0,1:T(8,128)(2,1)S(1)} fusion(s32[4096]{0:T(1024)S(1)} %bitcast.252, bf16[4096,3]{1,0:T(8,128)(2,1)S(1)} %copy.76, bf16[]{:T(256)} %constant.136.clone.1), kind=kCustom, calls=%fused_computation.109 | custom fusion | bytes 12290 | tf_op jit(solution)/shard_map/scatter | solution.py:104
  119.4 111.1 %all_gather.6 = bf16[3,32768]{0,1:T(8,128)(2,1)} all-gather(bf16[3,2048]{0,1:T(8,128)(2,1)S(1)} %scatter_custom_fusion.5), channel_id=1, replica_groups=mesh['case'=2,'wide'=16] {'wide'}, dimensions={1}, use_global_device_ids=true | all-gather | bytes 208896 | tf_op jit(solution)/shard_map/all_gather | solution.py:109
  230.4 6.5 %copy.77 = bf16[3,32768]{1,0:T(4,128)(2,1)S(1)} copy(bf16[3,32768]{0,1:T(8,128)(2,1)} %all_gather.6) | data formatting | bytes 393216
  237.0 0.8 copy.79
  237.8 6.9 %copy.78 = bf16[32,32768]{1,0:T(8,128)(2,1)S(1)} copy(bf16[32,32768]{0,1:T(8,128)(2,1)} %all-gather.2.cloned.1.call-done) | data formatting | bytes 4194304
  244.7 60.5 %while.14 = (s32[]{:T(128)}, f32[16,8]{0,1:T(8,128)S(1)}, f32[2,16]{1,0:T(2,128)S(1)}, bf16[3,32768]{1,0:T(4,128)(2,1)S(1)}, bf16[32,32768]{1,0:T(8,128)(2,1)S(1...) while((s32[]{:T(128)}, f32[16,8]{0,1:T(8,128)S(1)}, f32[2,16]{1,0:T(2,128)S(1)}, ...), condition=%wide.region_19.20_spmd.clone, body=%wide.region_10.19_spmd.clone.sunk | while | flops 41631876 | bytes 32215004 | solution.py:118
  244.8 1.3 copy-done
  246.1 1.4 dynamic-slice_convert_fusion.4
  247.5 2.5 reshape.394
  250.0 0.7 slice_multiply_fusion.11
  251.0 5.7 %multiply_reduce_fusion.13 = (f32[16]{0:T(128)S(1)}, f32[16]{0:T(128)S(1)}) fusion(f32[16384]{0:T(1024)S(1)} %bitcast.232, f32[16384]{0:T(1024)S(1)} %bitcast.233, f32[16384]{0:T(1024)S(1)} %bitcast.234, f32[16384]{0:T(1024)S(1)} %bitcast.235, f32[16384]{0:T(1024)S(1)} %bitcast.200, f32[16384]{0:T(1024)S(1)} %bitcast.236, f32[16384]{0:T(1024)S(1)} %bitcast.237, ...), kind=kLoop, calls=%fused_computation.70.clone.1 | loop fusion | flops 10223584 | bytes 786688 | tf_op jit(solution)/shard_map/while/body/eval_jaxpr/reduce_sum | solution.py:70
  256.6 1.3 slice_multiply_fusion.12
  257.9 5.7 %multiply_reduce_fusion.14 = (f32[16]{0:T(128)S(1)}, f32[16]{0:T(128)S(1)}) fusion(f32[16384]{0:T(1024)S(1)} %bitcast.224, f32[16384]{0:T(1024)S(1)} %bitcast.225, f32[16384]{0:T(1024)S(1)} %bitcast.226, f32[16384]{0:T(1024)S(1)} %bitcast.228, f32[16384]{0:T(1024)S(1)} %bitcast.229, f32[16384]{0:T(1024)S(1)} %bitcast.230, f32[16384]{0:T(1024)S(1)} %bitcast.231, ...), kind=kLoop, calls=%fused_computation.66.clone.1 | loop fusion | flops 10223584 | bytes 786688 | tf_op jit(solution)/shard_map/while/body/eval_jaxpr/reduce_sum | solution.py:70
  263.6 5.7 %multiply_reduce_fusion.15 = (f32[16]{0:T(128)S(1)}, f32[16]{0:T(128)S(1)}) fusion(f32[16384]{0:T(1024)S(1)} %bitcast.216, f32[16384]{0:T(1024)S(1)} %bitcast.217, f32[16384]{0:T(1024)S(1)} %bitcast.218, f32[16384]{0:T(1024)S(1)} %bitcast.219, f32[16384]{0:T(1024)S(1)} %bitcast.220, f32[16384]{0:T(1024)S(1)} %bitcast.221, f32[16384]{0:T(1024)S(1)} %bitcast.222, ...), kind=kLoop, calls=%fused_computation.62.clone.1 | loop fusion | flops 10223584 | bytes 786688 | tf_op jit(solution)/shard_map/while/body/eval_jaxpr/reduce_sum | solution.py:70
  269.3 5.7 %multiply_reduce_fusion.16 = (f32[16]{0:T(128)S(1)}, f32[16]{0:T(128)S(1)}) fusion(f32[16384]{0:T(1024)S(1)} %bitcast.209, f32[16384]{0:T(1024)S(1)} %bitcast.210, f32[16384]{0:T(1024)S(1)} %bitcast.211, f32[16384]{0:T(1024)S(1)} %bitcast.212, f32[16384]{0:T(1024)S(1)} %bitcast.213, f32[16384]{0:T(1024)S(1)} %bitcast.214, f32[16384]{0:T(1024)S(1)} %bitcast.215, ...), kind=kLoop, calls=%fused_computation.26.clone.1 | loop fusion | flops 10223584 | bytes 786688 | tf_op jit(solution)/shard_map/while/body/eval_jaxpr/reduce_sum | solution.py:70
  275.0 1.3 copy-done
  276.4 1.4 dynamic-slice_convert_fusion.4
  277.8 2.5 reshape.394
  280.3 0.7 slice_multiply_fusion.11
  281.2 5.7 %multiply_reduce_fusion.13 = (f32[16]{0:T(128)S(1)}, f32[16]{0:T(128)S(1)}) fusion(f32[16384]{0:T(1024)S(1)} %bitcast.232, f32[16384]{0:T(1024)S(1)} %bitcast.233, f32[16384]{0:T(1024)S(1)} %bitcast.234, f32[16384]{0:T(1024)S(1)} %bitcast.235, f32[16384]{0:T(1024)S(1)} %bitcast.200, f32[16384]{0:T(1024)S(1)} %bitcast.236, f32[16384]{0:T(1024)S(1)} %bitcast.237, ...), kind=kLoop, calls=%fused_computation.70.clone.1 | loop fusion | flops 10223584 | bytes 786688 | tf_op jit(solution)/shard_map/while/body/eval_jaxpr/reduce_sum | solution.py:70
  286.9 1.3 slice_multiply_fusion.12
  288.2 5.7 %multiply_reduce_fusion.14 = (f32[16]{0:T(128)S(1)}, f32[16]{0:T(128)S(1)}) fusion(f32[16384]{0:T(1024)S(1)} %bitcast.224, f32[16384]{0:T(1024)S(1)} %bitcast.225, f32[16384]{0:T(1024)S(1)} %bitcast.226, f32[16384]{0:T(1024)S(1)} %bitcast.228, f32[16384]{0:T(1024)S(1)} %bitcast.229, f32[16384]{0:T(1024)S(1)} %bitcast.230, f32[16384]{0:T(1024)S(1)} %bitcast.231, ...), kind=kLoop, calls=%fused_computation.66.clone.1 | loop fusion | flops 10223584 | bytes 786688 | tf_op jit(solution)/shard_map/while/body/eval_jaxpr/reduce_sum | solution.py:70
  293.9 5.7 %multiply_reduce_fusion.15 = (f32[16]{0:T(128)S(1)}, f32[16]{0:T(128)S(1)}) fusion(f32[16384]{0:T(1024)S(1)} %bitcast.216, f32[16384]{0:T(1024)S(1)} %bitcast.217, f32[16384]{0:T(1024)S(1)} %bitcast.218, f32[16384]{0:T(1024)S(1)} %bitcast.219, f32[16384]{0:T(1024)S(1)} %bitcast.220, f32[16384]{0:T(1024)S(1)} %bitcast.221, f32[16384]{0:T(1024)S(1)} %bitcast.222, ...), kind=kLoop, calls=%fused_computation.62.clone.1 | loop fusion | flops 10223584 | bytes 786688 | tf_op jit(solution)/shard_map/while/body/eval_jaxpr/reduce_sum | solution.py:70
  299.5 5.7 %multiply_reduce_fusion.16 = (f32[16]{0:T(128)S(1)}, f32[16]{0:T(128)S(1)}) fusion(f32[16384]{0:T(1024)S(1)} %bitcast.209, f32[16384]{0:T(1024)S(1)} %bitcast.210, f32[16384]{0:T(1024)S(1)} %bitcast.211, f32[16384]{0:T(1024)S(1)} %bitcast.212, f32[16384]{0:T(1024)S(1)} %bitcast.213, f32[16384]{0:T(1024)S(1)} %bitcast.214, f32[16384]{0:T(1024)S(1)} %bitcast.215, ...), kind=kLoop, calls=%fused_computation.26.clone.1 | loop fusion | flops 10223584 | bytes 786688 | tf_op jit(solution)/shard_map/while/body/eval_jaxpr/reduce_sum | solution.py:70
  305.3 0.6 broadcast_multiply_fusion.1
  (54 shorter events, 2.5 us)
Async XLA Ops:
  7.2 37.1 %copy-start.3 = (bf16[5,16,2048]{2,1,0:T(8,128)(2,1)S(1)}, bf16[5,16,2048]{2,1,0:T(8,128)(2,1)}, u32[]{:S(2)}) copy-start(bf16[5,16,2048]{2,1,0:T(8,128)(2,1)} %param.7) | copy-start | bytes 983044
  22.6 15.7 %all-to-all-start = ((s32[1,16,256]{2,0,1:T(1,128)}), s32[1,16,256]{2,0,1:T(1,128)S(1)}, u32[]{:S(2)}, u32[]{:S(2)}) async-start(s32[1,16,256]{2,0,1:T(1,128)} %bitcast.2), calls=%async_computation | async-start | bytes 32768 | tf_op jit(solution)/shard_map/all_to_all | solution.py:96
  38.3 13.6 %all-to-all-start.2 = ((bf16[3,16,256]{2,0,1:T(4,128)(2,1)}), bf16[3,16,256]{2,0,1:T(4,128)(2,1)S(1)}, u32[]{:S(2)}, u32[]{:S(2)}) async-start(bf16[3,16,256]{2,0,1:T(4,128)(2,1)} %copy.71), calls=%async_computation.2 | async-start | bytes 65536 | tf_op jit(solution)/shard_map/all_to_all | solution.py:95
  51.9 22.6 %all-to-all-start.1 = ((bf16[80,16,256]{2,0,1:T(8,128)(2,1)}), bf16[80,16,256]{2,0,1:T(8,128)(2,1)S(1)}, u32[]{:S(2)}, u32[]{:S(2)}) async-start(bf16[80,16,256]{2,0,1:T(8,128)(2,1)} %copy.67), calls=%async_computation.1 | async-start | bytes 1310720 | tf_op jit(solution)/shard_map/all_to_all | solution.py:91
  57.9 179.9 %all-gather.2.cloned.1.call-start = ((), (), s32[]{:S(2)}) async-start(), calls=%async_computation.4 | async-start | bytes 8912896 | tf_op jit(solution)/shard_map/all_gather | solution.py:108
  75.9 12.7 %copy-start.5 = (bf16[3,2048]{1,0:T(4,128)(2,1)S(1)}, bf16[3,2048]{1,0:T(4,128)(2,1)}, u32[]{:S(2)}) copy-start(bf16[3,2048]{1,0:T(4,128)(2,1)} %param.8) | copy-start | bytes 36868
  95.9 12.0 %all-to-all-start.3 = ((bf16[3,16,256]{2,0,1:T(4,128)(2,1)}), bf16[3,16,256]{2,0,1:T(4,128)(2,1)S(1)}, u32[]{:S(2)}, u32[]{:S(2)}) async-start(bf16[3,16,256]{2,0,1:T(4,128)(2,1)} %copy.75), calls=%async_computation.3 | async-start | bytes 65536 | tf_op jit(solution)/shard_map/all_to_all | solution.py:94
  230.4 6.5 %copy-start.2 = (bf16[32,2048]{0,1:T(8,128)(2,1)S(1)}, bf16[32,2048]{0,1:T(8,128)(2,1)}, u32[]{:S(2)}) copy-start(bf16[32,2048]{0,1:T(8,128)(2,1)} %scatter_custom_fusion.3) | copy-start | bytes 393220
  237.8 6.9 %copy-start.4 = (f32[2,16]{1,0:T(2,128)S(1)}, f32[2,16]{1,0:T(2,128)}, u32[]{:S(2)}) copy-start(f32[2,16]{1,0:T(2,128)} %param.11) | copy-start | bytes 388
  244.7 1.4 copy-start
  257.9 17.0 %copy-start.1 = (bf16[32,32768]{1,0:T(8,128)(2,1)S(1)}, bf16[32,32768]{1,0:T(8,128)(2,1)}, u32[]{:S(2)}) copy-start(bf16[32,32768]{1,0:T(8,128)(2,1)} %copy-done) | copy-start | bytes 6291460 | tf_op jit(solution)/shard_map/while
  275.0 1.4 copy-start
  288.2 17.0 %copy-start.1 = (bf16[32,32768]{1,0:T(8,128)(2,1)S(1)}, bf16[32,32768]{1,0:T(8,128)(2,1)}, u32[]{:S(2)}) copy-start(bf16[32,32768]{1,0:T(8,128)(2,1)} %copy-done) | copy-start | bytes 6291460 | tf_op jit(solution)/shard_map/while
Sparse Core Ops, SparseCore 0:
  88.6 123.3 all-gather.1
where the time goes:
time: 313 us
  blocking collectives  111 us (35%)
  local copies, waits for them, and re-layouts  78.5 us (25%)
  other arithmetic  60.1 us (19%)
  starting transfers between devices  24.2 us (8%)
  waiting for transfers between devices  23.7 us (8%)
  between operations  14.4 us (5%)
    all_gather x1, blocking collectives, shards(): place = lax.all_gather(owned_place, 'wide', axis=1, tiled=True)  111 us
    reduce_sum x8, other arithmetic, pressure_sums(): jnp.sum((cosine * bracket_im - sine * bracket_re) * inverse, axis=1)  45.3 us
    scatter x4, local copies, waits for them, and re-layouts, pack(): return empty.at[:, slot].set(columns)  26.8 us
    all_to_all x1, waiting for transfers between devices, shards(): lax.all_to_all(pack(flow.reshape(5 * NT, owned), 0), 'wide', split_axis=1...  16.5 us
    unnamed x13, local copies, waits for them, and re-layouts  15.6 us
    scatter x1, local copies, waits for them, and re-layouts, shards(): jnp.zeros((8 * HARM, owned), jnp.bfloat16).at[:, slot_index]  11.5 us
    scatter x1, local copies, waits for them, and re-layouts, shards(): jnp.zeros((3, owned), jnp.bfloat16).at[:, slot_index]  10.9 us
    all_to_all x1, starting transfers between devices, shards(): lax.all_to_all(slot_local, 'wide', split_axis=1, concat_axis=1, tiled=True)  7.39 us
  transfers between devices with their start and end apart: 5, of which 2 were waited for; matrix products, arithmetic and copies ran while one was open for 13% of the time, Pallas kernels for 0%

commit v1 on v0

v1 whole, which is shorter than its diff:
```python
import math

import jax
import jax.numpy as jnp
import numpy as np
from jax import lax
from jax.experimental import pallas as pl
from jax.experimental.pallas import tpu as pltpu
from jax.sharding import PartitionSpec as P

NT = 16
HARM = 4
ROWS = 8 * HARM
WAVENUMBER = 2.0
GROUND = 3.0
LOW = 256
F32 = jnp.float32
BF16 = jnp.bfloat16
NT_DIMS = (((1,), (1,)), ((), ()))


def dft_split():
    samples = np.arange(NT)[:, None]
    harmonic = np.arange(1, HARM + 1)[None, :]
    angle = 2.0 * np.pi / NT * samples * harmonic
    table = np.stack([np.cos(angle), -np.sin(angle)], axis=2) * (2.0 / NT)
    table = table.reshape(NT, 2 * HARM).T
    block = np.kron(np.eye(4), table).astype(np.float32)
    high = block.astype(jnp.bfloat16)
    low = (block - high.astype(np.float32)).astype(jnp.bfloat16)
    return np.concatenate([high, high, low, low], axis=1)


def pack_shape(nwide, owned):
    capacity = 2 * owned // nwide
    lanes = min(capacity, 128)
    subs = capacity // lanes
    return capacity, lanes, subs, ROWS * subs + 16


def source_kernel(nwide, flow_ref, normals_ref, ids_ref, table_ref, spectra_ref, packed_ref, left, right):
    owned = flow_ref.shape[2]
    capacity, lanes, subs, _ = pack_shape(nwide, owned)
    step = min(256, owned)
    table = table_ref[...]
    upper = (
        lax.broadcasted_iota(jnp.int32, (step, step), 0)
        < lax.broadcasted_iota(jnp.int32, (step, step), 1)
    ).astype(F32).astype(BF16)
    ids = ids_ref[...]
    owner = ids // owned
    local = ids - owner * owned
    high = local // LOW
    code_high = (high + 1).astype(F32)
    code_low = (local - high * LOW).astype(F32)
    carry = jnp.zeros((nwide, 1), F32)
    which = lax.broadcasted_iota(jnp.int32, (nwide, step), 0)
    slots = lax.broadcasted_iota(jnp.int32, (capacity, step), 0).astype(F32)
    codes_row = lax.broadcasted_iota(jnp.int32, (8, step), 0)
    for start in range(0, owned, step):
        cols = slice(start, start + step)
        normal = normals_ref[:, cols].astype(F32)
        n0, n1, n2 = normal[0:1], normal[1:2], normal[2:3]
        density = 1.0 + 0.2 * flow_ref[0, :, cols].astype(F32)
        v0 = 0.5 * flow_ref[1, :, cols].astype(F32)
        v1 = 0.5 * flow_ref[2, :, cols].astype(F32)
        v2 = 0.5 * flow_ref[3, :, cols].astype(F32)
        fluct = flow_ref[4, :, cols].astype(F32)
        across = v0 * n0 + v1 * n1 + v2 * n2
        source = density * across
        parts = jnp.concatenate(
            [source, fluct * n0 + v0 * source, fluct * n1 + v1 * source, fluct * n2 + v2 * source], axis=0
        )
        top = parts.astype(BF16)
        rest = (parts - top.astype(F32)).astype(BF16)
        both = jnp.concatenate([top, rest, top, rest], axis=0)
        spectra = jnp.dot(table, both, preferred_element_type=F32).astype(BF16)
        spectra_ref[:, cols] = spectra

        own = which == owner[:, cols]
        ownf = own.astype(F32)
        before = jnp.dot(ownf.astype(BF16), upper, preferred_element_type=F32) + carry
        rank = jnp.sum(before * ownf, axis=0, keepdims=True)
        carry = before[:, step - 1 : step] + ownf[:, step - 1 : step]
        right[:, cols] = (slots == rank).astype(F32).astype(BF16)
        codes = jnp.where(codes_row == 0, code_high[:, cols], jnp.where(codes_row == 1, code_low[:, cols], 0.0))
        codes = jnp.concatenate([codes, jnp.zeros_like(codes)], axis=0).astype(BF16)
        values = jnp.concatenate([spectra, codes], axis=0)
        for o in range(nwide):
            left[48 * o : 48 * o + 48, cols] = jnp.where(owner[:, cols] == o, values, jnp.zeros_like(values))
    packed = lax.dot_general(left[...], right[...], NT_DIMS, preferred_element_type=F32)
    for o in range(nwide):
        block = packed[48 * o : 48 * o + 48]
        pieces = [block[:ROWS, lanes * s : lanes * s + lanes] for s in range(subs)]
        pieces += [block[ROWS : ROWS + 8, lanes * s : lanes * s + lanes] for s in range(subs)]
        if subs == 1:
            pieces.append(jnp.zeros((8, lanes), F32))
        packed_ref[o] = jnp.concatenate(pieces, axis=0).astype(BF16)


def sources(flow, normals, ids, nwide):
    owned = flow.shape[2]
    capacity, lanes, subs, depth = pack_shape(nwide, owned)
    vmem = pl.BlockSpec(memory_space=pltpu.VMEM)
    table = jnp.asarray(dft_split())

    def body(*refs):
        source_kernel(nwide, *refs)

    return pl.pallas_call(
        body,
        out_shape=(
            jax.ShapeDtypeStruct((ROWS, owned), BF16),
            jax.ShapeDtypeStruct((nwide, depth, lanes), BF16),
        ),
        in_specs=[vmem] * 4,
        out_specs=(vmem, vmem),
        scratch_shapes=[
            pltpu.VMEM((48 * nwide, owned), BF16),
            pltpu.VMEM((capacity, owned), BF16),
        ],
        compiler_params=pltpu.CompilerParams(vmem_limit_bytes=48 * 2**20),
    )(flow, normals, ids.reshape(1, owned), table)


def place_kernel(received_ref, spectra_ref):
    nwide, depth, lanes = received_ref.shape
    owned = spectra_ref.shape[1]
    subs = (depth - 16) // ROWS
    heights = owned // LOW
    group = max(1, 256 // (lanes * subs))
    width = lanes * subs * group
    lows = lax.broadcasted_iota(jnp.int32, (LOW, width), 0).astype(F32)
    total = jnp.zeros((heights * ROWS, LOW), F32)
    for first in range(0, nwide, group):
        blocks, high, low = [], [], []
        for o in range(first, first + group):
            codes = received_ref[o, ROWS * subs : ROWS * subs + 16, :].astype(F32)
            for s in range(subs):
                blocks.append(received_ref[o, ROWS * s : ROWS * s + ROWS, :])
                high.append(codes[8 * s : 8 * s + 1])
                low.append(codes[8 * s + 1 : 8 * s + 2])
        values = jnp.concatenate(blocks, axis=1)
        high = jnp.concatenate(high, axis=1)
        low = jnp.concatenate(low, axis=1)
        spread = (lows == low).astype(F32).astype(BF16)
        picked = jnp.concatenate(
            [jnp.where(high == h + 1.0, values, jnp.zeros_like(values)) for h in range(heights)], axis=0
        )
        total = total + lax.dot_general(picked, spread, NT_DIMS, preferred_element_type=F32)
    for h in range(heights):
        spectra_ref[:, LOW * h : LOW * h + LOW] = total[ROWS * h : ROWS * h + ROWS].astype(BF16)


def place(received, owned):
    vmem = pl.BlockSpec(memory_space=pltpu.VMEM)
    return pl.pallas_call(
        place_kernel,
        out_shape=jax.ShapeDtypeStruct((ROWS, owned), BF16),
        in_specs=[vmem],
        out_specs=vmem,
        compiler_params=pltpu.CompilerParams(vmem_limit_bytes=48 * 2**20),
    )(received)


def fit(function, degree):
    nodes = np.cos(np.pi * (np.arange(64) + 0.5) / 64) * 0.5
    squares = nodes * nodes
    powers = np.stack([squares**d for d in range(degree + 1)], axis=1)
    return [float(c) for c in np.linalg.lstsq(powers, function(nodes), rcond=None)[0]]


COS = fit(lambda f: 2.0 * np.cos(2.0 * np.pi * f), 5)
SIN = fit(lambda f: np.sin(2.0 * np.pi * f) / f, 4)


def horner(coefficients, x):
    value = coefficients[-1]
    for c in coefficients[-2::-1]:
        value = value * x + c
    return value


KINDS = 4
COLS = 16


def sums_kernel(spectra_ref, place_ref, over_ref, sums_ref, weights):
    owned = spectra_ref.shape[1]
    count = over_ref.shape[0]
    step = min(256, owned)
    tile = 64
    steps = owned // step

    place_all = place_ref[...].astype(F32)
    px, py, pz = place_all[0:1], place_all[1:2], place_all[2:3]
    for h in range(HARM):
        def row(a, c):
            r = 2 * HARM * a + 2 * h + c
            return spectra_ref[r : r + 1, :].astype(F32)

        qr, qi = row(0, 0), row(0, 1)
        xr, xi, yr, yi, zr, zi = row(1, 0), row(1, 1), row(2, 0), row(2, 1), row(3, 0), row(3, 1)
        tr = -GROUND * zr - (px * xr + py * yr + pz * zr)
        ti = -GROUND * zi - (px * xi + py * yi + pz * zi)
        trh = tr.astype(BF16).astype(F32)
        tih = ti.astype(BF16).astype(F32)
        trl, til = tr - trh, ti - tih
        zero = jnp.zeros_like(qr)
        six = [zero] * 6
        blocks = [
            [-qi, qr] + [zero] * 8,
            [qr, qi] + [zero] * 8,
            [zero, zero, trh, tih, trl, til, xr, xi, yr, yi],
            [zero, zero, -tih, trh, -til, trl, -xi, xr, -yi, yr],
        ]
        for kind, rows in enumerate(blocks):
            value = jnp.concatenate(rows + [zero] * (COLS - len(rows)), axis=0).astype(BF16)
            for i in range(steps):
                weights[i, h, :, kind * step : kind * step + step] = value[:, i * step : i * step + step]

    for o in range(0, count, tile):
        ox = over_ref[o : o + tile, 0:1]
        oy = over_ref[o : o + tile, 1:2]
        ox2, oy2 = -2.0 * ox, -2.0 * oy
        oc = ox * ox + oy * oy + GROUND * GROUND
        acc = [jnp.zeros((tile, COLS), F32) for _ in range(HARM)]
        for i in range(steps):
            cols = slice(i * step, i * step + step)
            pxs, pys, pzs = px[:, cols], py[:, cols], pz[:, cols]
            pc = pxs * pxs + pys * pys + pzs * pzs + (2.0 * GROUND) * pzs
            square = (oc + pc) + ox2 * pxs + oy2 * pys
            inv = lax.rsqrt(square)
            turns = (square * inv) * (WAVENUMBER / (2.0 * math.pi))
            frac = turns - jnp.round(turns)
            fsq = frac * frac
            twoc = horner(COS, fsq)
            sine = horner(SIN, fsq) * frac
            c_prev, s_prev = inv, None
            c_now, s_now = (0.5 * inv) * twoc, inv * sine
            for h in range(HARM):
                wavenum = WAVENUMBER * (h + 1)
                ratio = inv * (1.0 / wavenum)
                d, e = inv * c_now, inv * s_now
                g_re = ratio * d + e
                g_im = d - ratio * e
                g = jnp.concatenate(
                    [c_now.astype(BF16), s_now.astype(BF16), g_re.astype(BF16), g_im.astype(BF16)], axis=1
                )
                acc[h] = acc[h] + lax.dot_general(g, weights[i, h], NT_DIMS, preferred_element_type=F32)
                if h < HARM - 1:
                    c_next = twoc * c_now - c_prev
                    s_next = twoc * s_now - s_prev if h else twoc * s_now
                    c_prev, s_prev, c_now, s_now = c_now, s_now, c_next, s_next
        outs = []
        for h in range(HARM):
            wavenum = WAVENUMBER * (h + 1)
            a = acc[h]
            for c in range(2):
                outs.append(
                    wavenum
                    * (a[:, c : c + 1] + a[:, 2 + c : 3 + c] + a[:, 4 + c : 5 + c] + ox * a[:, 6 + c : 7 + c] + oy * a[:, 8 + c : 9 + c])
                )
        sums_ref[o : o + tile, :] = jnp.concatenate(outs, axis=1)


def pressure_sums(spectra, positions, over):
    owned = spectra.shape[1]
    count = over.shape[0]
    step = min(256, owned)
    vmem = pl.BlockSpec(memory_space=pltpu.VMEM)
    return pl.pallas_call(
        sums_kernel,
        out_shape=jax.ShapeDtypeStruct((count, 2 * HARM), F32),
        in_specs=[vmem] * 3,
        out_specs=vmem,
        scratch_shapes=[pltpu.VMEM((owned // step, HARM, COLS, KINDS * step), BF16)],
        compiler_params=pltpu.CompilerParams(vmem_limit_bytes=48 * 2**20),
    )(spectra, positions, over)


def shards(flow, positions, normals, panel_ids, observers):
    owned = flow.shape[2]
    nwide = lax.axis_size("wide")
    listeners = observers.shape[1]
    mine = jnp.broadcast_to(observers.T[None], (nwide, listeners, 2))
    over = lax.all_to_all(mine, "wide", split_axis=0, concat_axis=0, tiled=True)
    spectra, packed = sources(flow, normals, panel_ids, nwide)
    received = lax.all_to_all(packed, "wide", split_axis=0, concat_axis=0, tiled=True)
    sums = pressure_sums(spectra, positions, over.reshape(nwide * listeners, 2))
    shares = lax.all_to_all(
        sums.reshape(nwide, listeners, 2 * HARM), "wide", split_axis=0, concat_axis=0, tiled=True
    )
    panel_spectra = place(received, owned)
    pressure = jnp.sum(shares, axis=0) * (2.0 / math.sqrt(owned * nwide))
    return (panel_spectra, pressure)


def solution(mesh):
    placed = (
        P(None, None, ("case", "wide")),
        P(None, ("case", "wide")),
        P(None, ("case", "wide")),
        P(("case", "wide")),
        P(None, ("case", "wide")),
    )
    return jax.shard_map(
        shards,
        mesh=mesh,
        in_specs=placed,
        out_specs=(P(None, ("case", "wide")), P(("case", "wide"), None)),
        check_vma=False,
    )
```

time: 313 us -> 50.6 us (0.16)
  blocking collectives: 111 us -> 9.46 us
  local copies, waits for them, and re-layouts: 78.5 us -> 3.95 us
  other arithmetic: 60.1 us -> 0.69 us
  between operations: 14.4 us -> 0.72 us
  starting transfers between devices: 24.2 us -> 11.1 us
  Pallas kernels: 0 us -> 11.9 us
  waiting for transfers between devices: 23.7 us -> 12.3 us
    all_gather x1 -> x0, blocking collectives: 111 us -> none  [shards(): place = lax.all_gather(owned_place, 'wide', axis=1, tiled=True)]
    scatter x6 -> x0, local copies, waits for them, and re-layouts: 49.3 us -> none  [the longest x4 26.8 us: pack(): return empty.at[:, slot].set(columns)]
    reduce_sum x10 -> x1, other arithmetic: 45.4 us -> 0.02 us  [shards(): pressure = jnp.sum(shares, axis=0) * (2.0 / math.sqrt(owned * nwide))]
    all_to_all x4 -> x2, starting transfers between devices: 24.2 us -> 11.1 us  [the longest x1 7.52 us: shards(): over = lax.all_to_all(mine, 'wide', split_axis=0, concat_axis=0, tiled=True)]
    unnamed x13 -> x16, local copies, waits for them, and re-layouts: 15.6 us -> 2.58 us
    pallas_call x0 -> x3, Pallas kernels: none -> 11.9 us  [the longest x1 8.36 us: pressure_sums(): pl.pallas_call(sums_kernel, out_shape=jax.ShapeDtypeStruct((count, 2 * HA...]
    all_to_all x4 -> x2, waiting for transfers between devices: 23.7 us -> 12.3 us  [the longest x1 9.02 us: shards(): lax.all_to_all(packed, 'wide', split_axis=0, concat_axis=0, tiled=True)]
    all_to_all x0 -> x1, blocking collectives: none -> 9.46 us  [shards(): lax.all_to_all(sums.reshape(nwide, listeners, 2 * HARM), 'wide', split_ax...]
  transfers between devices with their start and end apart: 5 -> 2, of which waited for: 2 -> 2; matrix products, arithmetic and copies ran while one was open for 13% -> 4% of each run, Pallas kernels for 0% -> 4%
where the time goes in v1:
time: 50.6 us; the launch traced here: 50.2 us
  waiting for transfers between devices  12.3 us (24%)
  Pallas kernels  11.9 us (24%)
  starting transfers between devices  11.1 us (22%)
  blocking collectives  9.46 us (19%)
  local copies, waits for them, and re-layouts  3.95 us (8%)
  between operations  0.72 us (1%)
  other arithmetic  0.69 us (1%)
    all_to_all x1, blocking collectives, shards(): lax.all_to_all(sums.reshape(nwide, listeners, 2 * HARM), 'wide', split_ax...  9.46 us
    all_to_all x1, waiting for transfers between devices, shards(): lax.all_to_all(packed, 'wide', split_axis=0, concat_axis=0, tiled=True)  9.02 us
    pallas_call x1, Pallas kernels, pressure_sums(): pl.pallas_call(sums_kernel, out_shape=jax.ShapeDtypeStruct((count, 2 * HA...  8.36 us
    all_to_all x1, starting transfers between devices, shards(): over = lax.all_to_all(mine, 'wide', split_axis=0, concat_axis=0, tiled=True)  7.52 us
    all_to_all x1, starting transfers between devices, shards(): lax.all_to_all(packed, 'wide', split_axis=0, concat_axis=0, tiled=True)  3.54 us
    all_to_all x1, waiting for transfers between devices, shards(): over = lax.all_to_all(mine, 'wide', split_axis=0, concat_axis=0, tiled=True)  3.31 us
    unnamed x16, local copies, waits for them, and re-layouts  2.58 us
    pallas_call x1, Pallas kernels, sources(): pl.pallas_call(body, out_shape=(jax.ShapeDtypeStruct((ROWS, owned), BF16)...  2.18 us
  transfers between devices with their start and end apart: 2, of which 2 were waited for; matrix products, arithmetic and copies ran while one was open for 4% of the time, Pallas kernels for 4%

profile of v1, /device:TPU:0, one launch (start us, length us, event | category | flops | bytes accessed | tf_op | source)
XLA Modules:
  0.0 50.2 jit_solution(2705103998772492255)
XLA Ops:
  0.6 0.0 copy-start.5
  0.6 0.7 %copy-done.5 = f32[2,16]{1,0:T(2,128)S(1)} copy-done((f32[2,16]{1,0:T(2,128)S(1)}, f32[2,16]{1,0:T(2,128)}, u32[]{:S(2)}) %copy-start.5) | copy-done | bytes 152
  1.3 0.0 copy-start.4
  1.3 0.6 %broadcast_in_dim.2 = f32[16,16,2]{1,2,0:T(2,128)} broadcast(f32[16,2]{0,1:T(2,128)S(1)} %bitcast.11), dimensions={1,2} | broadcast | bytes 2176 | tf_op jit(solution)/shard_map/broadcast_in_dim | solution.py:286
  1.9 0.0 copy-start.1
  1.9 0.0 copy-start.3
  1.9 7.5 %all-to-all-start.1 = ((f32[16,16,2]{1,2,0:T(2,128)}), f32[16,16,2]{1,2,0:T(2,128)S(1)}, u32[]{:S(2)}, u32[]{:S(2)}) async-start(f32[16,16,2]{1,2,0:T(2,128)} %broadcast_in_dim.2), calls=%async_computation.1 | async-start | bytes 32768 | tf_op jit(solution)/shard_map/all_to_all | solution.py:287
  9.5 0.0 copy-done.4
  9.5 0.0 copy-done.1
  9.5 0.0 copy-done.3
  9.5 0.0 copy-start
  9.5 1.0 %copy-done = bf16[5,16,2048]{2,1,0:T(8,128)(2,1)S(1)} copy-done((bf16[5,16,2048]{2,1,0:T(8,128)(2,1)S(1)}, bf16[5,16,2048]{2,1,0:T(8,128)(2,1)}, u32[]{:S(2)}) %copy-start) | copy-done | bytes 327704
  10.5 2.2 %shard_map.77 = (bf16[32,2048]{1,0:T(8,128)(2,1)S(1)}, bf16[16,80,128]{2,1,0:T(8,128)(2,1)}) custom-call(bf16[5,16,2048]{2,1,0:T(8,128)(2,1)S(1)} %copy-done, bf16[3,2048]{1,0:T(4,128)(2,1)S(1)} %copy-done.1, s32[1,2048]{1,0:T(1,128)S(1)} %bitcast.9, bf16[32,256]{1,0:T(8,128)(2,1)S(1)} %copy-done.3), custom_call_target="tpu_custom_call" | custom-call | tf_op jit(solution)/shard_map/pallas_call | solution.py:110
  12.6 0.0 copy-start.2
  12.6 3.3 %all-to-all-done.1 = f32[16,16,2]{1,2,0:T(2,128)S(1)} async-done(((f32[16,16,2]{1,2,0:T(2,128)}), f32[16,16,2]{1,2,0:T(2,128)S(1)}, u32[]{:S(2)}, u32[]{:S(2)}) %all-to-all-start.1) | async-done | bytes 2080 | tf_op jit(solution)/shard_map/all_to_all | solution.py:287
  15.9 0.2 copy.9
  16.1 0.0 copy-done.2
  16.1 8.4 %shard_map.79 = f32[256,8]{1,0:T(8,128)S(1)} custom-call(bf16[32,2048]{1,0:T(8,128)(2,1)S(1)} %get-tuple-element.5.spectra_ref, bf16[3,2048]{1,0:T(4,128)(2,1)S(1)} %copy-done.2, f32[256,2]{1,0:T(8,128)S(1)} %bitcast.7), custom_call_target="tpu_custom_call" | custom-call | tf_op jit(solution)/shard_map/pallas_call | solution.py:272
  24.5 0.1 copy.10
  24.6 0.1 reshape.17
  24.7 9.5 %all_to_all.15 = f32[16,1,128]{2,1,0:T(1,128)S(1)} all-to-all(f32[16,1,128]{2,1,0:T(1,128)S(1)} %reshape.17), channel_id=1, replica_groups=mesh['case'=2,'wide'=16] {'wide'}, dimensions={0} | all-to-all | bytes 16384 | tf_op jit(solution)/shard_map/all_to_all | solution.py:291
  34.1 3.5 %all-to-all-start = ((bf16[16,80,128]{2,1,0:T(8,128)(2,1)}), bf16[16,80,128]{2,1,0:T(8,128)(2,1)S(1)}, u32[]{:S(2)}, u32[]{:S(2)}) async-start(bf16[16,80,128]{2,1,0:T(8,128)(2,1)} %get-tuple-element.4), calls=%async_computation | async-start | bytes 655360 | tf_op jit(solution)/shard_map/all_to_all | solution.py:289
  37.7 0.5 %broadcast.1 = f32[]{:T(128)} broadcast(f32[]{:T(128)} %constant.8), dimensions={} | broadcast | bytes 8 | tf_op jit(solution)/shard_map/all_to_all | solution.py:291
  38.2 0.7 %reduce = f32[16,128]{1,0:T(8,128)S(1)} reduce(f32[16,1,128]{2,1,0:T(1,128)S(1)} %all_to_all.15, f32[]{:T(128)} %broadcast.1), dimensions={1}, to_apply=%all_to_all.11.reduce_sub_computation | reduce | bytes 16388 | tf_op jit(solution)/shard_map/all_to_all | solution.py:291
  38.9 0.1 reshape.18
  39.0 0.1 copy.13
  39.1 0.7 %copy.12 = f32[16,8]{0,1:T(8,128)} copy(f32[16,8]{1,0:T(8,128)S(1)} %broadcast_multiply_fusion) | data formatting | bytes 1024
  39.7 9.0 %all-to-all-done.received_ref = bf16[16,80,128]{2,1,0:T(8,128)(2,1)S(1)} async-done(((bf16[16,80,128]{2,1,0:T(8,128)(2,1)}), bf16[16,80,128]{2,1,0:T(8,128)(2,1)S(1)}, u32[]{:S(2)}, u32[]{:S(2)}) %all-to-all-start) | async-done | bytes 327712 | tf_op jit(solution)/shard_map/all_to_all | solution.py:289
  48.7 1.4 %shard_map.78 = bf16[32,2048]{1,0:T(8,128)(2,1)} custom-call(bf16[16,80,128]{2,1,0:T(8,128)(2,1)S(1)} %all-to-all-done.received_ref), custom_call_target="tpu_custom_call" | custom-call | tf_op jit(solution)/shard_map/pallas_call | solution.py:157
  (2 shorter events, 0.0 us)
Async XLA Ops:
  0.6 0.7 %copy-start.5 = (f32[2,16]{1,0:T(2,128)S(1)}, f32[2,16]{1,0:T(2,128)}, u32[]{:S(2)}) copy-start(f32[2,16]{1,0:T(2,128)} %param.10) | copy-start | bytes 388
  1.3 8.1 %copy-start.4 = (s32[2048]{0:T(1024)S(1)}, s32[2048]{0:T(1024)}, u32[]{:S(2)}) copy-start(s32[2048]{0:T(1024)} %param.9) | copy-start | bytes 24580
  1.9 7.5 %copy-start.1 = (bf16[3,2048]{1,0:T(4,128)(2,1)S(1)}, bf16[3,2048]{1,0:T(4,128)(2,1)}, u32[]{:S(2)}) copy-start(bf16[3,2048]{1,0:T(4,128)(2,1)} %refs_1_.1) | copy-start | bytes 36868
  1.9 7.5 %copy-start.3 = (bf16[32,256]{1,0:T(8,128)(2,1)S(1)}, bf16[32,256]{1,0:T(8,128)(2,1)}, u32[]{:S(2)}) copy-start(bf16[32,256]{1,0:T(8,128)(2,1)} %constant.6.clone.refs_3_) | copy-start | bytes 49156
  1.9 14.0 %all-to-all-start.1 = ((f32[16,16,2]{1,2,0:T(2,128)}), f32[16,16,2]{1,2,0:T(2,128)S(1)}, u32[]{:S(2)}, u32[]{:S(2)}) async-start(f32[16,16,2]{1,2,0:T(2,128)} %broadcast_in_dim.2), calls=%async_computation.1 | async-start | bytes 32768 | tf_op jit(solution)/shard_map/all_to_all | solution.py:287
  9.5 1.0 %copy-start = (bf16[5,16,2048]{2,1,0:T(8,128)(2,1)S(1)}, bf16[5,16,2048]{2,1,0:T(8,128)(2,1)}, u32[]{:S(2)}) copy-start(bf16[5,16,2048]{2,1,0:T(8,128)(2,1)} %refs_0_.1) | copy-start | bytes 983044
  12.6 3.5 %copy-start.2 = (bf16[3,2048]{1,0:T(4,128)(2,1)S(1)}, bf16[3,2048]{1,0:T(4,128)(2,1)}, u32[]{:S(2)}) copy-start(bf16[3,2048]{1,0:T(4,128)(2,1)} %place_ref.1) | copy-start | bytes 36868
  34.1 14.6 %all-to-all-start = ((bf16[16,80,128]{2,1,0:T(8,128)(2,1)}), bf16[16,80,128]{2,1,0:T(8,128)(2,1)S(1)}, u32[]{:S(2)}, u32[]{:S(2)}) async-start(bf16[16,80,128]{2,1,0:T(8,128)(2,1)} %get-tuple-element.4), calls=%async_computation | async-start | bytes 655360 | tf_op jit(solution)/shard_map/all_to_all | solution.py:289

commit v2 on v1

v2 whole, which is shorter than its diff:
```python
import math

import jax
import jax.numpy as jnp
import numpy as np
from jax import lax
from jax.experimental import pallas as pl
from jax.experimental.pallas import tpu as pltpu
from jax.sharding import PartitionSpec as P

NT = 16
HARM = 4
ROWS = 8 * HARM
WAVENUMBER = 2.0
GROUND = 3.0
LOW = 256
F32 = jnp.float32
BF16 = jnp.bfloat16
NT_DIMS = (((1,), (1,)), ((), ()))


def fit(function, degree):
    nodes = np.cos(np.pi * (np.arange(64) + 0.5) / 64) * 0.5
    squares = nodes * nodes
    powers = np.stack([squares**d for d in range(degree + 1)], axis=1)
    return [float(c) for c in np.linalg.lstsq(powers, function(nodes), rcond=None)[0]]


TURN = WAVENUMBER / (2.0 * math.pi)
HALF_SINE = fit(lambda f: math.sqrt(2.0) * np.sin(np.pi * f) / f, 4)


def horner(coefficients, x):
    value = coefficients[-1]
    for c in coefficients[-2::-1]:
        value = value * x + c
    return value


def thirds(x):
    first = x.astype(BF16).astype(F32)
    second = (x - first).astype(BF16).astype(F32)
    return [first, second, x - first - second]


def dft_split():
    samples = np.arange(NT)[:, None]
    harmonic = np.arange(1, HARM + 1)[None, :]
    angle = 2.0 * np.pi / NT * samples * harmonic
    table = np.stack([np.cos(angle), -np.sin(angle)], axis=2) * (2.0 / NT)
    table = table.reshape(NT, 2 * HARM).T
    block = np.kron(np.eye(4), table).astype(np.float32)
    order = [8 * a + 2 * h + c for h in range(HARM) for a in range(4) for c in range(2)]
    block = np.concatenate([block, block[order]], axis=0)
    high = block.astype(jnp.bfloat16)
    low = (block - high.astype(np.float32)).astype(jnp.bfloat16)
    return np.concatenate([high, high, low, low], axis=1)


def pack_shape(nwide, owned):
    capacity = 2 * owned // nwide
    lanes = min(capacity, 128)
    subs = capacity // lanes
    return capacity, lanes, subs, ROWS * subs + 16


def source_kernel(
    flow_hbm, normals_hbm, place_hbm, table_hbm, spectra_ref, weights_ref, points_ref,
    flow_ref, normals_ref, place_ref, table_ref, sems,
):
    owned = flow_ref.shape[2]
    step = min(256, owned)
    pieces = 4
    wide = owned // pieces
    copies = [
        pltpu.make_async_copy(normals_hbm, normals_ref, sems.at[0]),
        pltpu.make_async_copy(place_hbm, place_ref, sems.at[1]),
        pltpu.make_async_copy(table_hbm, table_ref, sems.at[2]),
    ]
    flows = [
        pltpu.make_async_copy(
            flow_hbm.at[:, :, wide * p : wide * p + wide], flow_ref.at[:, :, wide * p : wide * p + wide], sems.at[3 + p]
        )
        for p in range(pieces)
    ]
    for copy in copies + flows:
        copy.start()
    for copy in copies:
        copy.wait()
    table = table_ref[...]
    scale = TURN * TURN
    for start in range(0, owned, step):
        if start % wide == 0:
            flows[start // wide].wait()
        cols = slice(start, start + step)
        normal = normals_ref[:, cols].astype(F32)
        n0, n1, n2 = normal[0:1], normal[1:2], normal[2:3]
        density = 1.0 + 0.2 * flow_ref[0, :, cols].astype(F32)
        v0 = 0.5 * flow_ref[1, :, cols].astype(F32)
        v1 = 0.5 * flow_ref[2, :, cols].astype(F32)
        v2 = 0.5 * flow_ref[3, :, cols].astype(F32)
        fluct = flow_ref[4, :, cols].astype(F32)
        across = v0 * n0 + v1 * n1 + v2 * n2
        source = density * across
        parts = jnp.concatenate(
            [source, fluct * n0 + v0 * source, fluct * n1 + v1 * source, fluct * n2 + v2 * source], axis=0
        )
        top = parts.astype(BF16)
        rest = (parts - top.astype(F32)).astype(BF16)
        both = jnp.concatenate([top, rest, top, rest], axis=0)
        spectra = jnp.dot(table, both, preferred_element_type=F32).astype(BF16)
        spectra_ref[:, cols] = spectra[:ROWS]
        by_harmonic = spectra[ROWS:].astype(F32)
        place = place_ref[:, cols].astype(F32)
        px, py, pz = place[0:1], place[1:2], place[2:3]
        down = pz + GROUND
        none = jnp.zeros_like(px)
        factors = jnp.concatenate([none, none, px, px, py, py, down, down], axis=0)
        for h in range(HARM):
            group = by_harmonic[8 * h : 8 * h + 8]
            shares = group * factors
            along = -(shares[2:4] + shares[4:6] + shares[6:8])
            along_high = along.astype(BF16).astype(F32)
            weights_ref[h, :, cols] = jnp.concatenate(
                [group, along_high, along - along_high, jnp.zeros((4, step), F32)], axis=0
            ).astype(BF16)
        here = scale * (px * px + py * py + pz * pz + (2.0 * GROUND) * pz)
        one = jnp.ones_like(here)
        points = jnp.concatenate([px] * 3 + [py] * 3 + [one] * 3 + thirds(here) + [none] * 4, axis=0)
        points_ref[cols, :] = points.T.astype(BF16)


def sources(flow, normals, positions):
    owned = flow.shape[2]
    vmem = pl.BlockSpec(memory_space=pltpu.VMEM)
    anywhere = pl.BlockSpec(memory_space=pl.ANY)
    table = jnp.asarray(dft_split())
    return pl.pallas_call(
        source_kernel,
        out_shape=(
            jax.ShapeDtypeStruct((ROWS, owned), BF16),
            jax.ShapeDtypeStruct((HARM, 16, owned), BF16),
            jax.ShapeDtypeStruct((owned, 16), BF16),
        ),
        in_specs=[anywhere] * 4,
        out_specs=(vmem,) * 3,
        scratch_shapes=[
            pltpu.VMEM(flow.shape, BF16),
            pltpu.VMEM(normals.shape, BF16),
            pltpu.VMEM(positions.shape, BF16),
            pltpu.VMEM(table.shape, BF16),
            pltpu.SemaphoreType.DMA((7,)),
        ],
        compiler_params=pltpu.CompilerParams(vmem_limit_bytes=32 * 2**20),
    )(flow, normals, positions, table)


def pack_kernel(nwide, spectra_ref, ids_ref, packed_ref, codes_ref, left, right):
    owned = spectra_ref.shape[1]
    capacity, lanes, subs, _ = pack_shape(nwide, owned)
    step = min(256, owned)
    upper = (
        lax.broadcasted_iota(jnp.int32, (step, step), 0)
        < lax.broadcasted_iota(jnp.int32, (step, step), 1)
    ).astype(F32).astype(BF16)
    ids = ids_ref[...]
    owner = ids // owned
    local = ids - owner * owned
    high = local // LOW
    code_high = (high + 1).astype(F32)
    code_low = (local - high * LOW).astype(F32)
    carry = jnp.zeros((nwide, 1), F32)
    which = lax.broadcasted_iota(jnp.int32, (nwide, step), 0)
    slots = lax.broadcasted_iota(jnp.int32, (capacity, step), 0).astype(F32)
    codes_row = lax.broadcasted_iota(jnp.int32, (8, step), 0)
    for start in range(0, owned, step):
        cols = slice(start, start + step)
        own = which == owner[:, cols]
        ownf = own.astype(F32)
        before = jnp.dot(ownf.astype(BF16), upper, preferred_element_type=F32) + carry
        rank = jnp.sum(before * ownf, axis=0, keepdims=True)
        carry = before[:, step - 1 : step] + ownf[:, step - 1 : step]
        right[:, cols] = (slots == rank).astype(F32).astype(BF16)
        codes = jnp.where(codes_row == 0, code_high[:, cols], jnp.where(codes_row == 1, code_low[:, cols], 0.0))
        codes = jnp.concatenate([codes, jnp.zeros_like(codes)], axis=0).astype(BF16)
        values = jnp.concatenate([spectra_ref[:, cols], codes], axis=0)
        for o in range(nwide):
            left[48 * o : 48 * o + 48, cols] = jnp.where(owner[:, cols] == o, values, jnp.zeros_like(values))
    packed = lax.dot_general(left[...], right[...], NT_DIMS, preferred_element_type=F32)
    for o in range(nwide):
        block = packed[48 * o : 48 * o + 48]
        for s in range(subs):
            packed_ref[o, ROWS * s : ROWS * s + ROWS, :] = block[:ROWS, lanes * s : lanes * s + lanes].astype(BF16)
        codes = [block[ROWS : ROWS + 2, lanes * s : lanes * s + lanes] for s in range(subs)]
        codes_ref[o] = jnp.concatenate(codes + [jnp.zeros((8 - 2 * subs, lanes), F32)], axis=0)


def pack(spectra, ids, nwide):
    owned = spectra.shape[1]
    capacity, lanes, subs, depth = pack_shape(nwide, owned)
    vmem = pl.BlockSpec(memory_space=pltpu.VMEM)

    def body(*refs):
        pack_kernel(nwide, *refs)

    return pl.pallas_call(
        body,
        out_shape=(
            jax.ShapeDtypeStruct((nwide, depth, lanes), BF16),
            jax.ShapeDtypeStruct((nwide, 8, lanes), F32),
        ),
        in_specs=[vmem] * 2,
        out_specs=(vmem, vmem),
        scratch_shapes=[
            pltpu.VMEM((48 * nwide, owned), BF16),
            pltpu.VMEM((capacity, owned), BF16),
        ],
        compiler_params=pltpu.CompilerParams(vmem_limit_bytes=40 * 2**20),
    )(spectra, ids.reshape(1, owned))


def place_kernel(scale, received_ref, spectra_ref, pressure_ref):
    nwide, depth, lanes = received_ref.shape
    owned = spectra_ref.shape[1]
    listeners = pressure_ref.shape[1]
    subs = (depth - 16) // ROWS
    heights = owned // LOW
    group = max(1, 256 // (lanes * subs))
    width = lanes * subs * group
    lows = lax.broadcasted_iota(jnp.int32, (LOW, width), 0).astype(F32)
    total = jnp.zeros((heights * ROWS, LOW), F32)
    sums = jnp.zeros((2 * HARM, lanes), F32)
    for first in range(0, nwide, group):
        blocks, high, low = [], [], []
        for o in range(first, first + group):
            codes = received_ref[o, ROWS * subs : ROWS * subs + 16, :].astype(F32)
            sums = sums + codes[8:16]
            for s in range(subs):
                blocks.append(received_ref[o, ROWS * s : ROWS * s + ROWS, :])
                high.append(codes[2 * s : 2 * s + 1])
                low.append(codes[2 * s + 1 : 2 * s + 2])
        values = jnp.concatenate(blocks, axis=1)
        high = jnp.concatenate(high, axis=1)
        low = jnp.concatenate(low, axis=1)
        spread = (lows == low).astype(F32).astype(BF16)
        picked = jnp.concatenate(
            [jnp.where(high == h + 1.0, values, jnp.zeros_like(values)) for h in range(heights)], axis=0
        )
        total = total + lax.dot_general(picked, spread, NT_DIMS, preferred_element_type=F32)
    for h in range(heights):
        spectra_ref[:, LOW * h : LOW * h + LOW] = total[ROWS * h : ROWS * h + ROWS].astype(BF16)
    third = [sums[:, listeners * p : listeners * p + listeners] for p in range(3)]
    pressure_ref[...] = scale * ((third[2] + third[1]) + third[0])


def place(received, owned, listeners):
    nwide = received.shape[0]
    vmem = pl.BlockSpec(memory_space=pltpu.VMEM)
    scale = 2.0 / math.sqrt(owned * nwide)

    def body(*refs):
        place_kernel(scale, *refs)

    return pl.pallas_call(
        body,
        out_shape=(
            jax.ShapeDtypeStruct((ROWS, owned), BF16),
            jax.ShapeDtypeStruct((2 * HARM, listeners), F32),
        ),
        in_specs=[vmem],
        out_specs=(vmem, vmem),
        compiler_params=pltpu.CompilerParams(vmem_limit_bytes=40 * 2**20),
    )(received)


def sums_kernel(far, near, me_ref, weights_ref, points_ref, codes_ref, *refs):
    over = refs[:near]
    packed_hbm, tail, sem = refs[near + 1 :]
    owned = weights_ref.shape[2]
    listeners = over[0].shape[1]
    nwide, _, lanes = codes_ref.shape
    depth = packed_hbm.shape[1]
    step = min(256, owned)
    scale = TURN * TURN

    over_x = jnp.concatenate([over[n][2 * z : 2 * z + 1, :] for z in range(far) for n in range(near)], axis=1)
    over_y = jnp.concatenate([over[n][2 * z + 1 : 2 * z + 2, :] for z in range(far) for n in range(near)], axis=1)
    there = scale * (over_x * over_x + over_y * over_y + GROUND * GROUND)
    one, zero = jnp.ones_like(there), jnp.zeros_like(there)
    views = jnp.concatenate(
        thirds((-2.0 * scale) * over_x) + thirds((-2.0 * scale) * over_y) + thirds(there) + [one] * 3 + [zero] * 4,
        axis=0,
    ).astype(BF16)

    count = far * near * listeners
    width = min(256, count)
    for left in range(0, count, width):
        view = views[:, left : left + width]
        totals = [[None] * 4 for _ in range(HARM)]
        for start in range(0, owned, step):
            square = jnp.dot(points_ref[start : start + step, :], view, preferred_element_type=F32)
            inv = lax.rsqrt(square)
            turns = square * inv
            frac = turns - jnp.round(turns)
            half = horner(HALF_SINE, frac * frac) * frac
            versine = half * half
            cosine = 1.0 - versine
            twoc = cosine + cosine
            rest = jnp.maximum(2.0 - versine, 1e-30)
            c_prev, s_prev = inv, None
            c_now = inv * cosine
            s_now = (inv * half) * (rest * lax.rsqrt(rest))
            for h in range(HARM):
                ratio = inv * (TURN / (WAVENUMBER * (h + 1)))
                d, e = inv * c_now, inv * s_now
                part = weights_ref[h, :, start : start + step]
                for m, value in enumerate((c_now, s_now, ratio * d + e, d - ratio * e)):
                    product = jnp.dot(part, value.astype(BF16), preferred_element_type=F32)
                    totals[h][m] = product if start == 0 else totals[h][m] + product
                if h < HARM - 1:
                    c_next = twoc * c_now - c_prev
                    s_next = twoc * s_now - s_prev if h else twoc * s_now
                    c_prev, s_prev, c_now, s_now = c_now, s_now, c_next, s_next
        ox, oy = over_x[:, left : left + width], over_y[:, left : left + width]
        lines = []
        for h in range(HARM):
            factor = WAVENUMBER * (h + 1) * TURN
            cos_sum, sin_sum = totals[h][0], totals[h][1]

            def loads(m):
                t = totals[h][m]
                return [
                    ox * t[2 + c : 3 + c] + oy * t[4 + c : 5 + c] + (t[8 + c : 9 + c] + t[10 + c : 11 + c])
                    for c in (0, 1)
                ]

            (re_re, re_im), (im_re, im_im) = loads(2), loads(3)
            lines.append(factor * (sin_sum[0:1] - cos_sum[1:2] + TURN * (re_re - im_im)))
            lines.append(factor * (cos_sum[0:1] + sin_sum[1:2] + TURN * (re_im + im_re)))
        split = thirds(jnp.concatenate(lines, axis=0))
        for j in range(width // listeners):
            owner = me_ref[0] ^ (left // listeners + j)
            cells = [value[:, listeners * j : listeners * j + listeners] for value in split]
            cells.append(jnp.zeros((2 * HARM, lanes - 3 * listeners), F32))
            cells = jnp.concatenate(cells, axis=1)
            tail[owner] = jnp.concatenate([codes_ref[owner], cells], axis=0).astype(BF16)
    copy = pltpu.make_async_copy(tail, packed_hbm.at[:, depth - 16 : depth, :], sem)
    copy.start()
    copy.wait()


def pressure_sums(weights, points, codes, over, packed, far):
    near = len(over)
    listeners = over[0].shape[1]
    owned = weights.shape[2]
    nwide, depth, lanes = packed.shape
    vmem = pl.BlockSpec(memory_space=pltpu.VMEM)
    me = lax.axis_index("wide").reshape(1)

    def body(*refs):
        sums_kernel(far, near, *refs)

    return pl.pallas_call(
        body,
        out_shape=jax.ShapeDtypeStruct(packed.shape, BF16),
        in_specs=[pl.BlockSpec(memory_space=pltpu.SMEM)] + [vmem] * (3 + near) + [pl.BlockSpec(memory_space=pl.ANY)],
        out_specs=pl.BlockSpec(memory_space=pl.ANY),
        input_output_aliases={4 + near: 0},
        scratch_shapes=[pltpu.VMEM((nwide, 16, lanes), BF16), pltpu.SemaphoreType.DMA],
        compiler_params=pltpu.CompilerParams(vmem_limit_bytes=40 * 2**20),
        cost_estimate=pl.CostEstimate(
            flops=far * near * listeners * owned * 2000,
            bytes_accessed=owned * 70,
            transcendentals=far * near * listeners * owned,
        ),
    )(me, weights, points, codes, *over, packed)


def swap(x, nwide, bits):
    return lax.ppermute(x, "wide", [(i, i ^ bits) for i in range(nwide)])


def shards(flow, positions, normals, panel_ids, observers):
    owned = flow.shape[2]
    nwide = lax.axis_size("wide")
    listeners = observers.shape[1]
    far = 4
    near = nwide // far
    lines = jnp.concatenate([observers] + [swap(observers, nwide, near * z) for z in range(1, far)], axis=0)
    spectra, weights, points = sources(flow, normals, positions)
    lines, spectra = lax.optimization_barrier((lines, spectra))
    over = [lines] + [swap(lines, nwide, n) for n in range(1, near)]
    packed, codes = pack(spectra, panel_ids, nwide)
    packed = pressure_sums(weights, points, codes, over, packed, far)
    received = lax.all_to_all(packed, "wide", split_axis=0, concat_axis=0, tiled=True)
    panel_spectra, pressure = place(received, owned, listeners)
    return (panel_spectra, pressure.T)


def solution(mesh):
    placed = (
        P(None, None, ("case", "wide")),
        P(None, ("case", "wide")),
        P(None, ("case", "wide")),
        P(("case", "wide")),
        P(None, ("case", "wide")),
    )
    return jax.shard_map(
        shards,
        mesh=mesh,
        in_specs=placed,
        out_specs=(P(None, ("case", "wide")), P(("case", "wide"), None)),
        check_vma=False,
    )
```

time: 50.6 us -> 40.2 us (0.79)
  waiting for transfers between devices: 12.3 us -> 1.61 us
  blocking collectives: 9.46 us -> 15.9 us
  starting transfers between devices: 11.1 us -> 7.6 us
  Pallas kernels: 11.9 us -> 10.9 us
  local copies, waits for them, and re-layouts: 3.95 us -> 3.17 us
  other arithmetic: 0.69 us -> 0.01 us
    all_to_all x2 -> x0, waiting for transfers between devices: 12.3 us -> none  [the longest x1 9.02 us: shards(): lax.all_to_all(packed, 'wide', split_axis=0, concat_axis=0, tiled=True)]
    all_to_all x2 -> x0, starting transfers between devices: 11.1 us -> none  [the longest x1 7.52 us: shards(): over = lax.all_to_all(mine, 'wide', split_axis=0, concat_axis=0, tiled=True)]
    ppermute x0 -> x6, starting transfers between devices: none -> 7.6 us  [swap(): return lax.ppermute(x, 'wide', [(i, i ^ bits) for i in range(nwide)])]
    all_to_all x1, blocking collectives: 9.46 us -> 15.9 us  [shards(): lax.all_to_all(packed, 'wide', split_axis=0, concat_axis=0, tiled=True)]
    ppermute x0 -> x6, waiting for transfers between devices: none -> 1.61 us  [swap(): return lax.ppermute(x, 'wide', [(i, i ^ bits) for i in range(nwide)])]
    pallas_call x3 -> x4, Pallas kernels: 11.9 us -> 10.9 us  [the longest x1 6.92 us: pressure_sums(): pl.pallas_call(body, out_shape=jax.ShapeDtypeStruct(packed.shape, BF16),...]
    all_to_all x2 -> x0, local copies, waits for them, and re-layouts: 0.68 us -> none  [the longest x1 0.51 us: shards(): lax.all_to_all(sums.reshape(nwide, listeners, 2 * HARM), 'wide', split_ax...]
    all_to_all x1 -> x0, other arithmetic: 0.67 us -> none  [shards(): lax.all_to_all(sums.reshape(nwide, listeners, 2 * HARM), 'wide', split_ax...]
  transfers between devices with their start and end apart: 2 -> 6, of which waited for: 2 -> 2; matrix products, arithmetic and copies ran while one was open for 4% -> 0% of each run, Pallas kernels for 4% -> 6%
where the time goes in v2:
time: 40.2 us; the launch traced here: 39.9 us
  blocking collectives  15.9 us (40%)
  Pallas kernels  10.9 us (27%)
  starting transfers between devices  7.6 us (19%)
  local copies, waits for them, and re-layouts  3.17 us (8%)
  waiting for transfers between devices  1.61 us (4%)
  between operations  0.71 us (2%)
    all_to_all x1, blocking collectives, shards(): lax.all_to_all(packed, 'wide', split_axis=0, concat_axis=0, tiled=True)  15.9 us
    ppermute x6, starting transfers between devices, swap(): return lax.ppermute(x, 'wide', [(i, i ^ bits) for i in range(nwide)])  7.6 us
    pallas_call x1, Pallas kernels, pressure_sums(): pl.pallas_call(body, out_shape=jax.ShapeDtypeStruct(packed.shape, BF16),...  6.92 us
    unnamed x12, local copies, waits for them, and re-layouts  3.17 us
    ppermute x6, waiting for transfers between devices, swap(): return lax.ppermute(x, 'wide', [(i, i ^ bits) for i in range(nwide)])  1.61 us
    pallas_call x1, Pallas kernels, pack(): pl.pallas_call(body, out_shape=(jax.ShapeDtypeStruct((nwide, depth, lanes...  1.44 us
    pallas_call x1, Pallas kernels, place(): pl.pallas_call(body, out_shape=(jax.ShapeDtypeStruct((ROWS, owned), BF16)...  1.41 us
    pallas_call x1, Pallas kernels, sources(): pl.pallas_call(source_kernel, out_shape=(jax.ShapeDtypeStruct((ROWS, owne...  1.13 us
  transfers between devices with their start and end apart: 6, of which 2 were waited for; matrix products, arithmetic and copies ran while one was open for 0% of the time, Pallas kernels for 6%

profile of v2, /device:TPU:0, one launch (start us, length us, event | category | flops | bytes accessed | tf_op | source)
XLA Modules:
  0.0 39.9 jit_solution(3043512482449521503)
XLA Ops:
  0.6 4.1 %collective-permute-start.1 = (f32[2,16]{1,0:T(2,128)}, f32[2,16]{1,0:T(2,128)S(1)}, u32[]{:S(2)}, u32[]{:S(2)}) collective-permute-start(f32[2,16]{1,0:T(2,128)} %param.10), channel_id=1, source_target_pairs={{0,8},{1,9},{2,10},{3,11},{4,12},{5,13},{6,14},{7,15},{8,0},{9,1},... | collective-permute-start | bytes 392 | tf_op jit(solution)/shard_map/ppermute | solution.py:380
  4.7 1.6 %collective-permute-start = (f32[2,16]{1,0:T(2,128)}, f32[2,16]{1,0:T(2,128)S(1)}, u32[]{:S(2)}, u32[]{:S(2)}) collective-permute-start(f32[2,16]{1,0:T(2,128)} %param.10), channel_id=1, source_target_pairs={{0,4},{1,5},{2,6},{3,7},{4,0},{5,1},{6,2},{7,3},{8,12},{9,13},{10,... | collective-permute-start | bytes 392 | tf_op jit(solution)/shard_map/ppermute | solution.py:380
  6.3 0.0 collective-permute-start.2
  6.3 0.0 copy-start
  6.3 1.0 %copy-done = bf16[5,16,2048]{2,1,0:T(8,128)(2,1)S(1)} copy-done((bf16[5,16,2048]{2,1,0:T(8,128)(2,1)S(1)}, bf16[5,16,2048]{2,1,0:T(8,128)(2,1)}, u32[]{:S(2)}) %copy-start) | copy-done | bytes 327704
  7.3 0.0 copy-start.1
  7.3 0.8 %copy-done.1 = bf16[64,256]{1,0:T(8,128)(2,1)S(1)} copy-done((bf16[64,256]{1,0:T(8,128)(2,1)S(1)}, bf16[64,256]{1,0:T(8,128)(2,1)}, u32[]{:S(2)}) %copy-start.1) | copy-done | bytes 32792
  8.0 0.0 copy-start.2
  8.0 0.7 %copy-done.2 = bf16[3,2048]{1,0:T(4,128)(2,1)S(1)} copy-done((bf16[3,2048]{1,0:T(4,128)(2,1)S(1)}, bf16[3,2048]{1,0:T(4,128)(2,1)}, u32[]{:S(2)}) %copy-start.2) | copy-done | bytes 12312
  8.8 0.0 copy-start.3
  8.8 0.7 %copy-done.3 = bf16[3,2048]{1,0:T(4,128)(2,1)S(1)} copy-done((bf16[3,2048]{1,0:T(4,128)(2,1)S(1)}, bf16[3,2048]{1,0:T(4,128)(2,1)}, u32[]{:S(2)}) %copy-start.3) | copy-done | bytes 12312
  9.5 0.0 copy-start.5
  9.5 1.1 %shard_map.77 = (bf16[32,2048]{1,0:T(8,128)(2,1)S(1)}, bf16[4,16,2048]{2,1,0:T(8,128)(2,1)S(1)}, bf16[2048,16]{1,0:T(8,128)(2,1)S(1)}) custom-call(bf16[5,16,2048]{2,1,0:T(8,128)(2,1)S(1)} %copy-done, bf16[3,2048]{1,0:T(4,128)(2,1)S(1)} %copy-done.2, bf16[3,2048]{1,0:T(4,128)(2,1)S(1)} %copy-done.3, bf16[64,256]{1,0:T(8,128)(2,1)S(1)} %copy-done.1), custom_call_target="tpu_custom_call" | custom-call | tf_op jit(solution)/shard_map/pallas_call | solution.py:138
  10.6 0.0 copy-start.4
  10.6 0.0 collective-permute-done.1
  10.6 0.0 collective-permute-done
  10.6 1.2 %collective-permute-done.2 = f32[2,16]{1,0:T(2,128)S(1)} collective-permute-done((f32[2,16]{1,0:T(2,128)}, f32[2,16]{1,0:T(2,128)S(1)}, u32[]{:S(2)}, u32[]{:S(2)}) %collective-permute-start.2) | collective-permute-done | bytes 160 | tf_op jit(solution)/shard_map/ppermute | solution.py:380
  11.9 0.0 copy-done.5
  11.9 0.1 collective-permute-start.5
  12.0 1.6 %collective-permute-start.4 = (f32[8,16]{1,0:T(8,128)S(1)}, f32[8,16]{1,0:T(8,128)S(1)}, u32[]{:S(2)}, u32[]{:S(2)}) collective-permute-start(f32[8,16]{1,0:T(8,128)S(1)} %pad_maximum_fusion.refs_4_), channel_id=1, source_target_pairs={{0,2},{1,3},{2,0},{3,1},{4,6},{5,7},{6,4},{7,5},{8,10},{9,11},{10,... | collective-permute-start | bytes 1544 | tf_op jit(solution)/shard_map/ppermute | solution.py:380
  13.6 0.3 collective-permute-start.3
  13.8 0.0 copy-done.4
  13.8 1.4 %shard_map.78 = (bf16[16,80,128]{2,1,0:T(8,128)(2,1)S(1)}, f32[16,8,128]{2,1,0:T(8,128)S(1)}) custom-call(bf16[32,2048]{1,0:T(8,128)(2,1)S(1)} %get-tuple-element.14.refs_0_, s32[1,2048]{1,0:T(1,128)S(1)} %bitcast.3), custom_call_target="tpu_custom_call" | custom-call | tf_op jit(solution)/shard_map/pallas_call | solution.py:206
  15.3 0.0 collective-permute-done.5.refs_7_
  15.3 0.4 collective-permute-done.4.refs_6_
  15.7 0.0 collective-permute-done.3.refs_5_
  15.7 6.9 %shard_map.79 = bf16[16,80,128]{2,1,0:T(8,128)(2,1)S(1)} custom-call(s32[1]{0:T(128)} %bitcast.refs_0_, bf16[4,16,2048]{2,1,0:T(8,128)(2,1)S(1)} %get-tuple-element.11.refs_1_, bf16[2048,16]{1,0:T(8,128)(2,1)S(1)} %get-tuple-element.12.refs_2_, f32[16,8,128]{2,1,0:T(8,128)S(1)} %get-tuple-element.15.refs_3_, ...), custom_call_target="tpu_custom_call", output_to_operand_aliasing={{}: (8, {})} | custom-call | flops 1048576000 | bytes 143360 | tf_op jit(solution)/shard_map/pallas_call | solution.py:363
  22.6 15.9 %all_to_all.5.refs_0_ = bf16[16,80,128]{2,1,0:T(8,128)(2,1)S(1)} all-to-all(bf16[16,80,128]{2,1,0:T(8,128)(2,1)S(1)} %shard_map.79), channel_id=1, replica_groups=mesh['case'=2,'wide'=16] {'wide'}, dimensions={0} | all-to-all | bytes 655360 | tf_op jit(solution)/shard_map/all_to_all | solution.py:395
  38.4 1.4 %shard_map.80 = (bf16[32,2048]{1,0:T(8,128)(2,1)}, f32[8,16]{1,0:T(8,128)}) custom-call(bf16[16,80,128]{2,1,0:T(8,128)(2,1)S(1)} %all_to_all.5.refs_0_), custom_call_target="tpu_custom_call" | custom-call | tf_op jit(solution)/shard_map/pallas_call | solution.py:264
  (1 shorter events, 0.0 us)
Async XLA Ops:
  0.6 10.0 %collective-permute-start.1 = (f32[2,16]{1,0:T(2,128)}, f32[2,16]{1,0:T(2,128)S(1)}, u32[]{:S(2)}, u32[]{:S(2)}) collective-permute-start(f32[2,16]{1,0:T(2,128)} %param.10), channel_id=1, source_target_pairs={{0,8},{1,9},{2,10},{3,11},{4,12},{5,13},{6,14},{7,15},{8,0},{9,1},... | collective-permute-start | bytes 392 | tf_op jit(solution)/shard_map/ppermute | solution.py:380
  4.7 5.9 %collective-permute-start = (f32[2,16]{1,0:T(2,128)}, f32[2,16]{1,0:T(2,128)S(1)}, u32[]{:S(2)}, u32[]{:S(2)}) collective-permute-start(f32[2,16]{1,0:T(2,128)} %param.10), channel_id=1, source_target_pairs={{0,4},{1,5},{2,6},{3,7},{4,0},{5,1},{6,2},{7,3},{8,12},{9,13},{10,... | collective-permute-start | bytes 392 | tf_op jit(solution)/shard_map/ppermute | solution.py:380
  6.3 5.6 %collective-permute-start.2 = (f32[2,16]{1,0:T(2,128)}, f32[2,16]{1,0:T(2,128)S(1)}, u32[]{:S(2)}, u32[]{:S(2)}) collective-permute-start(f32[2,16]{1,0:T(2,128)} %param.10), channel_id=1, source_target_pairs={{0,12},{1,13},{2,14},{3,15},{4,8},{5,9},{6,10},{7,11},{8,4},{9,5},... | collective-permute-start | bytes 392 | tf_op jit(solution)/shard_map/ppermute | solution.py:380
  6.3 1.0 %copy-start = (bf16[5,16,2048]{2,1,0:T(8,128)(2,1)S(1)}, bf16[5,16,2048]{2,1,0:T(8,128)(2,1)}, u32[]{:S(2)}) copy-start(bf16[5,16,2048]{2,1,0:T(8,128)(2,1)} %flow_hbm.1) | copy-start | bytes 983044
  7.3 0.8 %copy-start.1 = (bf16[64,256]{1,0:T(8,128)(2,1)S(1)}, bf16[64,256]{1,0:T(8,128)(2,1)}, u32[]{:S(2)}) copy-start(bf16[64,256]{1,0:T(8,128)(2,1)} %constant.6.clone.table_hbm) | copy-start | bytes 98308
  8.0 0.7 %copy-start.2 = (bf16[3,2048]{1,0:T(4,128)(2,1)S(1)}, bf16[3,2048]{1,0:T(4,128)(2,1)}, u32[]{:S(2)}) copy-start(bf16[3,2048]{1,0:T(4,128)(2,1)} %normals_hbm.1) | copy-start | bytes 36868
  8.8 0.7 %copy-start.3 = (bf16[3,2048]{1,0:T(4,128)(2,1)S(1)}, bf16[3,2048]{1,0:T(4,128)(2,1)}, u32[]{:S(2)}) copy-start(bf16[3,2048]{1,0:T(4,128)(2,1)} %place_hbm.1) | copy-start | bytes 36868
  9.5 2.4 %copy-start.5 = (f32[2,16]{1,0:T(2,128)S(1)}, f32[2,16]{1,0:T(2,128)}, u32[]{:S(2)}) copy-start(f32[2,16]{1,0:T(2,128)} %param.10) | copy-start | bytes 388
  10.6 3.2 %copy-start.4 = (s32[2048]{0:T(1024)S(1)}, s32[2048]{0:T(1024)}, u32[]{:S(2)}) copy-start(s32[2048]{0:T(1024)} %param.9) | copy-start | bytes 24580
  11.9 3.4 %collective-permute-start.5 = (f32[8,16]{1,0:T(8,128)S(1)}, f32[8,16]{1,0:T(8,128)S(1)}, u32[]{:S(2)}, u32[]{:S(2)}) collective-permute-start(f32[8,16]{1,0:T(8,128)S(1)} %pad_maximum_fusion.refs_4_), channel_id=1, source_target_pairs={{0,3},{1,2},{2,1},{3,0},{4,7},{5,6},{6,5},{7,4},{8,11},{9,10},{10,... | collective-permute-start | bytes 1544 | tf_op jit(solution)/shard_map/ppermute | solution.py:380
  12.0 3.7 %collective-permute-start.4 = (f32[8,16]{1,0:T(8,128)S(1)}, f32[8,16]{1,0:T(8,128)S(1)}, u32[]{:S(2)}, u32[]{:S(2)}) collective-permute-start(f32[8,16]{1,0:T(8,128)S(1)} %pad_maximum_fusion.refs_4_), channel_id=1, source_target_pairs={{0,2},{1,3},{2,0},{3,1},{4,6},{5,7},{6,4},{7,5},{8,10},{9,11},{10,... | collective-permute-start | bytes 1544 | tf_op jit(solution)/shard_map/ppermute | solution.py:380
  13.6 2.1 %collective-permute-start.3 = (f32[8,16]{1,0:T(8,128)S(1)}, f32[8,16]{1,0:T(8,128)S(1)}, u32[]{:S(2)}, u32[]{:S(2)}) collective-permute-start(f32[8,16]{1,0:T(8,128)S(1)} %pad_maximum_fusion.refs_4_), channel_id=1, source_target_pairs={{0,1},{1,0},{2,3},{3,2},{4,5},{5,4},{6,7},{7,6},{8,9},{9,8},{10,11... | collective-permute-start | bytes 1544 | tf_op jit(solution)/shard_map/ppermute | solution.py:380

commit v3 on v2

--- a/solution.py
+++ b/solution.py
@@ -65,7 +65,8 @@
 
 
 def source_kernel(
-    flow_hbm, normals_hbm, place_hbm, table_hbm, spectra_ref, weights_ref, points_ref,
+    flow_hbm, normals_hbm, place_hbm, table_hbm, ids_hbm, over_hbm,
+    spectra_ref, weights_ref, points_ref, ids_ref, mine_ref,
     flow_ref, normals_ref, place_ref, table_ref, sems,
 ):
     owned = flow_ref.shape[2]
@@ -77,13 +78,17 @@
         pltpu.make_async_copy(place_hbm, place_ref, sems.at[1]),
         pltpu.make_async_copy(table_hbm, table_ref, sems.at[2]),
     ]
+    passed = [
+        pltpu.make_async_copy(ids_hbm, ids_ref, sems.at[3]),
+        pltpu.make_async_copy(over_hbm, mine_ref, sems.at[4]),
+    ]
     flows = [
         pltpu.make_async_copy(
-            flow_hbm.at[:, :, wide * p : wide * p + wide], flow_ref.at[:, :, wide * p : wide * p + wide], sems.at[3 + p]
+            flow_hbm.at[:, :, wide * p : wide * p + wide], flow_ref.at[:, :, wide * p : wide * p + wide], sems.at[5 + p]
         )
         for p in range(pieces)
     ]
-    for copy in copies + flows:
+    for copy in copies + flows + passed:
         copy.start()
     for copy in copies:
         copy.wait()
@@ -128,31 +133,36 @@
         one = jnp.ones_like(here)
         points = jnp.concatenate([px] * 3 + [py] * 3 + [one] * 3 + thirds(here) + [none] * 4, axis=0)
         points_ref[cols, :] = points.T.astype(BF16)
-
-
-def sources(flow, normals, positions):
+    for copy in passed:
+        copy.wait()
+
+
+def sources(flow, normals, positions, ids, observers):
     owned = flow.shape[2]
     vmem = pl.BlockSpec(memory_space=pltpu.VMEM)
     anywhere = pl.BlockSpec(memory_space=pl.ANY)
     table = jnp.asarray(dft_split())
+    arrays = (flow, normals, positions, table, ids.reshape(1, owned), observers)
     return pl.pallas_call(
         source_kernel,
         out_shape=(
             jax.ShapeDtypeStruct((ROWS, owned), BF16),
             jax.ShapeDtypeStruct((HARM, 16, owned), BF16),
             jax.ShapeDtypeStruct((owned, 16), BF16),
+            jax.ShapeDtypeStruct((1, owned), jnp.int32),
+            jax.ShapeDtypeStruct(observers.shape, F32),
         ),
-        in_specs=[anywhere] * 4,
-        out_specs=(vmem,) * 3,
+        in_specs=[anywhere] * 6,
+        out_specs=(vmem,) * 5,
         scratch_shapes=[
             pltpu.VMEM(flow.shape, BF16),
             pltpu.VMEM(normals.shape, BF16),
             pltpu.VMEM(positions.shape, BF16),
             pltpu.VMEM(table.shape, BF16),
-            pltpu.SemaphoreType.DMA((7,)),
+            pltpu.SemaphoreType.DMA((9,)),
         ],
         compiler_params=pltpu.CompilerParams(vmem_limit_bytes=32 * 2**20),
-    )(flow, normals, positions, table)
+    )(*(pltpu.with_memory_space_constraint(x, pltpu.HBM) for x in arrays))
 
 
 def pack_kernel(nwide, spectra_ref, ids_ref, packed_ref, codes_ref, left, right):
@@ -216,7 +226,7 @@
             pltpu.VMEM((capacity, owned), BF16),
         ],
         compiler_params=pltpu.CompilerParams(vmem_limit_bytes=40 * 2**20),
-    )(spectra, ids.reshape(1, owned))
+    )(spectra, ids)
 
 
 def place_kernel(scale, received_ref, spectra_ref, pressure_ref):
@@ -273,58 +283,72 @@
     )(received)
 
 
-def sums_kernel(far, near, me_ref, weights_ref, points_ref, codes_ref, *refs):
-    over = refs[:near]
-    packed_hbm, tail, sem = refs[near + 1 :]
+SUB = 64
+KINDS = 6
+
+
+def pair_sums(lines, weights_ref, points_ref):
     owned = weights_ref.shape[2]
-    listeners = over[0].shape[1]
-    nwide, _, lanes = codes_ref.shape
-    depth = packed_hbm.shape[1]
+    count = lines.shape[0] // 2
+    listeners = lines.shape[1]
     step = min(256, owned)
     scale = TURN * TURN
-
-    over_x = jnp.concatenate([over[n][2 * z : 2 * z + 1, :] for z in range(far) for n in range(near)], axis=1)
-    over_y = jnp.concatenate([over[n][2 * z + 1 : 2 * z + 2, :] for z in range(far) for n in range(near)], axis=1)
+    over_x = jnp.concatenate([lines[2 * j : 2 * j + 1] for j in range(count)], axis=1)
+    over_y = jnp.concatenate([lines[2 * j + 1 : 2 * j + 2] for j in range(count)], axis=1)
     there = scale * (over_x * over_x + over_y * over_y + GROUND * GROUND)
     one, zero = jnp.ones_like(there), jnp.zeros_like(there)
     views = jnp.concatenate(
         thirds((-2.0 * scale) * over_x) + thirds((-2.0 * scale) * over_y) + thirds(there) + [one] * 3 + [zero] * 4,
         axis=0,
     ).astype(BF16)
-
-    count = far * near * listeners
-    width = min(256, count)
-    for left in range(0, count, width):
+    width = min(256, count * listeners)
+    made = []
+    for left in range(0, count * listeners, width):
         view = views[:, left : left + width]
-        totals = [[None] * 4 for _ in range(HARM)]
+        totals = [[None] * KINDS for _ in range(HARM)]
+        pending = []
+
+        def drain(number):
+            for _ in range(min(number, len(pending))):
+                h, m, begin, pieces = pending.pop(0)
+                whole = pieces[0] if len(pieces) == 1 else jnp.concatenate(pieces, axis=0)
+                part = weights_ref[h, :, begin : begin + step]
+                product = jnp.dot(part, whole, preferred_element_type=F32)
+                totals[h][m] = product if totals[h][m] is None else totals[h][m] + product
+
         for start in range(0, owned, step):
-            square = jnp.dot(points_ref[start : start + step, :], view, preferred_element_type=F32)
-            inv = lax.rsqrt(square)
-            turns = square * inv
-            frac = turns - jnp.round(turns)
-            half = horner(HALF_SINE, frac * frac) * frac
-            versine = half * half
-            cosine = 1.0 - versine
-            twoc = cosine + cosine
-            rest = jnp.maximum(2.0 - versine, 1e-30)
-            c_prev, s_prev = inv, None
-            c_now = inv * cosine
-            s_now = (inv * half) * (rest * lax.rsqrt(rest))
-            for h in range(HARM):
-                ratio = inv * (TURN / (WAVENUMBER * (h + 1)))
-                d, e = inv * c_now, inv * s_now
-                part = weights_ref[h, :, start : start + step]
-                for m, value in enumerate((c_now, s_now, ratio * d + e, d - ratio * e)):
-                    product = jnp.dot(part, value.astype(BF16), preferred_element_type=F32)
-                    totals[h][m] = product if start == 0 else totals[h][m] + product
-                if h < HARM - 1:
-                    c_next = twoc * c_now - c_prev
-                    s_next = twoc * s_now - s_prev if h else twoc * s_now
-                    c_prev, s_prev, c_now, s_now = c_now, s_now, c_next, s_next
+            mats = [[[] for _ in range(KINDS)] for _ in range(HARM)]
+            for row in range(start, start + step, SUB):
+                square = jnp.dot(points_ref[row : row + SUB, :], view, preferred_element_type=F32)
+                inv = lax.rsqrt(square)
+                turns = square * inv
+                frac = turns - jnp.round(turns)
+                half = horner(HALF_SINE, frac * frac) * frac
+                versine = half * half
+                cosine = 1.0 - versine
+                twoc = cosine + cosine
+                rest = jnp.maximum(2.0 - versine, 1e-30)
+                inv2 = (inv * inv).astype(BF16)
+                c_prev, s_prev = inv, None
+                c_now = inv * cosine
+                s_now = (inv * half) * (rest * lax.rsqrt(rest))
+                for h in range(HARM):
+                    c_bf, s_bf = c_now.astype(BF16), s_now.astype(BF16)
+                    d, e = (inv * c_now).astype(BF16), (inv * s_now).astype(BF16)
+                    for m, value in enumerate((c_bf, s_bf, d, e, inv2 * c_bf, inv2 * s_bf)):
+                        mats[h][m].append(value)
+                    if h < HARM - 1:
+                        c_next = twoc * c_now - c_prev
+                        s_next = twoc * s_now - s_prev if h else twoc * s_now
+                        c_prev, s_prev, c_now, s_now = c_now, s_now, c_next, s_next
+                drain(HARM * KINDS * SUB // step)
+            drain(HARM * KINDS)
+            pending += [(h, m, start, mats[h][m]) for h in range(HARM) for m in range(KINDS)]
+        drain(HARM * KINDS)
         ox, oy = over_x[:, left : left + width], over_y[:, left : left + width]
-        lines = []
+        rows = []
         for h in range(HARM):
-            factor = WAVENUMBER * (h + 1) * TURN
+            wavenum = WAVENUMBER * (h + 1)
             cos_sum, sin_sum = totals[h][0], totals[h][1]
 
             def loads(m):
@@ -334,64 +358,108 @@
                     for c in (0, 1)
                 ]
 
-            (re_re, re_im), (im_re, im_im) = loads(2), loads(3)
-            lines.append(factor * (sin_sum[0:1] - cos_sum[1:2] + TURN * (re_re - im_im)))
-            lines.append(factor * (cos_sum[0:1] + sin_sum[1:2] + TURN * (re_im + im_re)))
-        split = thirds(jnp.concatenate(lines, axis=0))
-        for j in range(width // listeners):
-            owner = me_ref[0] ^ (left // listeners + j)
-            cells = [value[:, listeners * j : listeners * j + listeners] for value in split]
-            cells.append(jnp.zeros((2 * HARM, lanes - 3 * listeners), F32))
-            cells = jnp.concatenate(cells, axis=1)
-            tail[owner] = jnp.concatenate([codes_ref[owner], cells], axis=0).astype(BF16)
+            (dr, di), (er, ei), (ur, ui), (vr, vi) = loads(2), loads(3), loads(4), loads(5)
+            real = wavenum * (er - di) + TURN * (ur + vi)
+            imag = wavenum * (ei + dr) + TURN * (ui - vr)
+            rows.append(TURN * (wavenum * (sin_sum[0:1] - cos_sum[1:2]) + TURN * real))
+            rows.append(TURN * (wavenum * (cos_sum[0:1] + sin_sum[1:2]) + TURN * imag))
+        made.append(jnp.concatenate(rows, axis=0))
+    return made
+
+
+def cells_of(lines, weights_ref, points_ref, lanes):
+    listeners = lines.shape[1]
+    cells = []
+    for value in pair_sums(lines, weights_ref, points_ref):
+        split = thirds(value)
+        for j in range(value.shape[1] // listeners):
+            cell = [third[:, listeners * j : listeners * j + listeners] for third in split]
+            cell.append(jnp.zeros((2 * HARM, lanes - 3 * listeners), F32))
+            cells.append(jnp.concatenate(cell, axis=1))
+    return cells
+
+
+def first_kernel(lines_ref, weights_ref, points_ref, cells_ref):
+    for j, cell in enumerate(cells_of(lines_ref[...], weights_ref, points_ref, cells_ref.shape[2])):
+        cells_ref[j] = cell
+
+
+def second_kernel(
+    steps, me_ref, lines_ref, weights_ref, points_ref, cells_ref, codes_ref, packed_in, packed_hbm, tail, sem
+):
+    lanes = codes_ref.shape[2]
+    depth = packed_hbm.shape[1]
+    early = cells_ref.shape[0]
+    cells = [cells_ref[j] for j in range(early)]
+    cells += cells_of(lines_ref[...], weights_ref, points_ref, lanes)
+    for j, cell in enumerate(cells):
+        owner = me_ref[0] ^ steps[j]
+        tail[owner] = jnp.concatenate([codes_ref[owner], cell], axis=0).astype(BF16)
     copy = pltpu.make_async_copy(tail, packed_hbm.at[:, depth - 16 : depth, :], sem)
     copy.start()
     copy.wait()
 
 
-def pressure_sums(weights, points, codes, over, packed, far):
-    near = len(over)
-    listeners = over[0].shape[1]
+def first_sums(lines, weights, points, lanes):
+    owned = weights.shape[2]
+    devices = lines.shape[0] // 2
+    pairs = devices * lines.shape[1] * owned
+    vmem = pl.BlockSpec(memory_space=pltpu.VMEM)
+    return pl.pallas_call(
+        first_kernel,
+        out_shape=jax.ShapeDtypeStruct((devices, 2 * HARM, lanes), F32),
+        in_specs=[vmem] * 3,
+        out_specs=vmem,
+        compiler_params=pltpu.CompilerParams(vmem_limit_bytes=40 * 2**20),
+        cost_estimate=pl.CostEstimate(flops=pairs * 2000, bytes_accessed=owned * 70, transcendentals=pairs),
+    )(lines, weights, points)
+
+
+def second_sums(lines, weights, points, cells, codes, packed, steps):
     owned = weights.shape[2]
     nwide, depth, lanes = packed.shape
+    pairs = lines.shape[0] // 2 * lines.shape[1] * owned
     vmem = pl.BlockSpec(memory_space=pltpu.VMEM)
+    anywhere = pl.BlockSpec(memory_space=pl.ANY)
     me = lax.axis_index("wide").reshape(1)
 
     def body(*refs):
-        sums_kernel(far, near, *refs)
+        second_kernel(steps, *refs)
 
     return pl.pallas_call(
         body,
         out_shape=jax.ShapeDtypeStruct(packed.shape, BF16),
-        in_specs=[pl.BlockSpec(memory_space=pltpu.SMEM)] + [vmem] * (3 + near) + [pl.BlockSpec(memory_space=pl.ANY)],
-        out_specs=pl.BlockSpec(memory_space=pl.ANY),
-        input_output_aliases={4 + near: 0},
+        in_specs=[pl.BlockSpec(memory_space=pltpu.SMEM)] + [vmem] * 5 + [anywhere],
+        out_specs=anywhere,
+        input_output_aliases={6: 0},
         scratch_shapes=[pltpu.VMEM((nwide, 16, lanes), BF16), pltpu.SemaphoreType.DMA],
         compiler_params=pltpu.CompilerParams(vmem_limit_bytes=40 * 2**20),
-        cost_estimate=pl.CostEstimate(
-            flops=far * near * listeners * owned * 2000,
-            bytes_accessed=owned * 70,
-            transcendentals=far * near * listeners * owned,
-        ),
-    )(me, weights, points, codes, *over, packed)
-
-
-def swap(x, nwide, bits):
-    return lax.ppermute(x, "wide", [(i, i ^ bits) for i in range(nwide)])
+        cost_estimate=pl.CostEstimate(flops=pairs * 2000, bytes_accessed=owned * 70, transcendentals=pairs),
+    )(me, lines, weights, points, cells, codes, packed)
+
+
+def swap(x, nwide, bit):
+    return lax.ppermute(x, "wide", [(i, i ^ bit) for i in range(nwide)])
 
 
 def shards(flow, positions, normals, panel_ids, observers):
     owned = flow.shape[2]
     nwide = lax.axis_size("wide")
     listeners = observers.shape[1]
-    far = 4
-    near = nwide // far
-    lines = jnp.concatenate([observers] + [swap(observers, nwide, near * z) for z in range(1, far)], axis=0)
-    spectra, weights, points = sources(flow, normals, positions)
-    lines, spectra = lax.optimization_barrier((lines, spectra))
-    over = [lines] + [swap(lines, nwide, n) for n in range(1, near)]
-    packed, codes = pack(spectra, panel_ids, nwide)
-    packed = pressure_sums(weights, points, codes, over, packed, far)
+    near = nwide // 4
+    others = [swap(observers, nwide, n) for n in range(1, near)]
+    spectra, weights, points, ids, mine = sources(flow, normals, positions, panel_ids, observers)
+    others, spectra = lax.optimization_barrier((others, spectra))
+    lines = jnp.concatenate([mine] + others, axis=0)
+    other = swap(lines, nwide, near)
+    packed, codes = pack(spectra, ids, nwide)
+    other, packed = lax.optimization_barrier((other, packed))
+    lines = jnp.concatenate([lines, other], axis=0)
+    other = swap(lines, nwide, 2 * near)
+    cells = first_sums(lines, weights, points, packed.shape[2])
+    other, cells = lax.optimization_barrier((other, cells))
+    steps = [n ^ z for z in range(0, 4 * near, near) for n in range(near)]
+    packed = second_sums(other, weights, points, cells, codes, packed, steps)
     received = lax.all_to_all(packed, "wide", split_axis=0, concat_axis=0, tiled=True)
     panel_spectra, pressure = place(received, owned, listeners)
     return (panel_spectra, pressure.T)

time: 40.2 us -> 36.6 us (0.910)
  local copies, waits for them, and re-layouts: 3.17 us -> 0.02 us
  blocking collectives: 15.9 us -> 14.8 us
  waiting for transfers between devices: 1.61 us -> 2.34 us
    unnamed x12 -> x0, local copies, waits for them, and re-layouts: 3.17 us -> none
    all_to_all x1, blocking collectives: 15.9 us -> 14.8 us  [shards(): lax.all_to_all(packed, 'wide', split_axis=0, concat_axis=0, tiled=True)]
    pallas_call x1, Pallas kernels: 1.13 us -> 1.96 us  [sources(): pl.pallas_call(source_kernel, out_shape=(jax.ShapeDtypeStruct((ROWS, owne...]
    pallas_call x1 -> x2, Pallas kernels: 6.92 us -> 6.12 us  [the longest x1 3.08 us: second_sums(): pl.pallas_call(body, out_shape=jax.ShapeDtypeStruct(packed.shape, BF16),...]
    ppermute x6 -> x5, waiting for transfers between devices: 1.61 us -> 2.34 us  [swap(): return lax.ppermute(x, 'wide', [(i, i ^ bit) for i in range(nwide)])]
    ppermute x6 -> x5, starting transfers between devices: 7.6 us -> 7.49 us  [swap(): return lax.ppermute(x, 'wide', [(i, i ^ bit) for i in range(nwide)])]
  transfers between devices with their start and end apart: 6 -> 5, of which waited for: 2 -> 2; matrix products, arithmetic and copies ran while one was open for 0% -> 0% of each run, Pallas kernels for 6% -> 18%
where the time goes in v3:
time: 36.6 us; the launch traced here: 36.3 us
  blocking collectives  14.8 us (40%)
  Pallas kernels  10.9 us (30%)
  starting transfers between devices  7.49 us (20%)
  waiting for transfers between devices  2.34 us (6%)
  between operations  0.69 us (2%)
    all_to_all x1, blocking collectives, shards(): lax.all_to_all(packed, 'wide', split_axis=0, concat_axis=0, tiled=True)  14.8 us
    ppermute x5, starting transfers between devices, swap(): return lax.ppermute(x, 'wide', [(i, i ^ bit) for i in range(nwide)])  7.49 us
    pallas_call x1, Pallas kernels, second_sums(): pl.pallas_call(body, out_shape=jax.ShapeDtypeStruct(packed.shape, BF16),...  3.08 us
    pallas_call x1, Pallas kernels, first_sums(): pl.pallas_call(first_kernel, out_shape=jax.ShapeDtypeStruct((devices, 2 *...  3.05 us
    ppermute x5, waiting for transfers between devices, swap(): return lax.ppermute(x, 'wide', [(i, i ^ bit) for i in range(nwide)])  2.34 us
    pallas_call x1, Pallas kernels, sources(): pl.pallas_call(source_kernel, out_shape=(jax.ShapeDtypeStruct((ROWS, owne...  1.96 us
    pallas_call x1, Pallas kernels, pack(): pl.pallas_call(body, out_shape=(jax.ShapeDtypeStruct((nwide, depth, lanes...  1.44 us
    pallas_call x1, Pallas kernels, place(): pl.pallas_call(body, out_shape=(jax.ShapeDtypeStruct((ROWS, owned), BF16)...  1.41 us
  transfers between devices with their start and end apart: 5, of which 2 were waited for; matrix products, arithmetic and copies ran while one was open for 0% of the time, Pallas kernels for 18%

profile of v3, /device:TPU:0, one launch (start us, length us, event | category | flops | bytes accessed | tf_op | source)
XLA Modules:
  0.0 36.3 jit_solution(2514781932814878396)
XLA Ops:
  0.6 0.5 %collective-permute-start = (f32[2,16]{1,0:T(2,128)}, f32[2,16]{1,0:T(2,128)S(1)}, u32[]{:S(2)}, u32[]{:S(2)}) collective-permute-start(f32[2,16]{1,0:T(2,128)} %over_hbm.1), channel_id=1, source_target_pairs={{0,1},{1,0},{2,3},{3,2},{4,5},{5,4},{6,7},{7,6},{8,9},{9,8},{10,11... | collective-permute-start | bytes 392 | tf_op jit(solution)/shard_map/ppermute | solution.py:442
  1.1 2.6 %collective-permute-start.2 = (f32[2,16]{1,0:T(2,128)}, f32[2,16]{1,0:T(2,128)S(1)}, u32[]{:S(2)}, u32[]{:S(2)}) collective-permute-start(f32[2,16]{1,0:T(2,128)} %over_hbm.1), channel_id=1, source_target_pairs={{0,3},{1,2},{2,1},{3,0},{4,7},{5,6},{6,5},{7,4},{8,11},{9,10},{10,... | collective-permute-start | bytes 392 | tf_op jit(solution)/shard_map/ppermute | solution.py:442
  3.8 0.0 collective-permute-start.1
  3.8 2.0 %shard_map.77 = (bf16[32,2048]{1,0:T(8,128)(2,1)S(1)}, bf16[4,16,2048]{2,1,0:T(8,128)(2,1)S(1)}, bf16[2048,16]{1,0:T(8,128)(2,1)S(1)}, s32[1,2048]{1,0:T(1,128)S(1)}, f32[2,16]{1,0:T(2,128)S(1)}) custom-call(bf16[5,16,2048]{2,1,0:T(8,128)(2,1)} %flow_hbm.1, bf16[3,2048]{1,0:T(4,128)(2,1)} %normals_hbm.1, bf16[3,2048]{1,0:T(4,128)(2,1)} %place_hbm.1, ...), custom_call_target="tpu_custom_call" | custom-call | tf_op jit(solution)/shard_map/pallas_call | solution.py:146
  5.8 0.0 collective-permute-done
  5.8 0.0 collective-permute-done.2
  5.8 1.7 %collective-permute-done.1 = f32[2,16]{1,0:T(2,128)S(1)} collective-permute-done((f32[2,16]{1,0:T(2,128)}, f32[2,16]{1,0:T(2,128)S(1)}, u32[]{:S(2)}, u32[]{:S(2)}) %collective-permute-start.1) | collective-permute-done | bytes 160 | tf_op jit(solution)/shard_map/ppermute | solution.py:442
  7.6 1.6 %collective-permute-start.3 = (f32[8,16]{1,0:T(8,128)S(1)}, f32[8,16]{1,0:T(8,128)S(1)}, u32[]{:S(2)}, u32[]{:S(2)}) collective-permute-start(f32[8,16]{1,0:T(8,128)S(1)} %pad_maximum_fusion), channel_id=1, source_target_pairs={{0,4},{1,5},{2,6},{3,7},{4,0},{5,1},{6,2},{7,3},{8,12},{9,13},{10,... | collective-permute-start | bytes 1544 | tf_op jit(solution)/shard_map/ppermute | solution.py:442
  9.2 1.4 %shard_map.78 = (bf16[16,80,128]{2,1,0:T(8,128)(2,1)S(1)}, f32[16,8,128]{2,1,0:T(8,128)S(1)}) custom-call(bf16[32,2048]{1,0:T(8,128)(2,1)S(1)} %get-tuple-element.24.refs_0_, s32[1,2048]{1,0:T(1,128)S(1)} %get-tuple-element.25.refs_1_), custom_call_target="tpu_custom_call" | custom-call | tf_op jit(solution)/shard_map/pallas_call | solution.py:216
  10.7 0.6 %collective-permute-done.3 = f32[8,16]{1,0:T(8,128)S(1)} collective-permute-done((f32[8,16]{1,0:T(8,128)S(1)}, f32[8,16]{1,0:T(8,128)S(1)}, u32[]{:S(2)}, u32[]{:S(2)}) %collective-permute-start.3) | collective-permute-done | bytes 544 | tf_op jit(solution)/shard_map/ppermute | solution.py:442
  11.3 2.6 %collective-permute-start.4 = (f32[16,16]{1,0:T(8,128)S(1)}, f32[16,16]{1,0:T(8,128)S(1)}, u32[]{:S(2)}, u32[]{:S(2)}) collective-permute-start(f32[16,16]{1,0:T(8,128)S(1)} %concatenate.8.lines_ref), channel_id=1, source_target_pairs={{0,8},{1,9},{2,10},{3,11},{4,12},{5,13},{6,14},{7,15},{8,0},{9,1},... | collective-permute-start | bytes 3080 | tf_op jit(solution)/shard_map/ppermute | solution.py:442
  13.9 3.0 %shard_map.79.refs_4_ = f32[8,8,128]{2,1,0:T(8,128)S(1)} custom-call(f32[16,16]{1,0:T(8,128)S(1)} %concatenate.8.lines_ref, bf16[4,16,2048]{2,1,0:T(8,128)(2,1)S(1)} %get-tuple-element.28.weights_ref.refs_2_, bf16[2048,16]{1,0:T(8,128)(2,1)S(1)} %get-tuple-element.29.points_ref.refs_3_), custom_call_target="tpu_custom_call" | custom-call | flops 524288000 | bytes 143360 | tf_op jit(solution)/shard_map/pallas_call | solution.py:408
  17.0 0.0 collective-permute-done.4.refs_1_
  17.0 3.1 %shard_map.80 = bf16[16,80,128]{2,1,0:T(8,128)(2,1)S(1)} custom-call(s32[1]{0:T(128)} %bitcast.refs_0_, f32[16,16]{1,0:T(8,128)S(1)} %collective-permute-done.4.refs_1_, bf16[4,16,2048]{2,1,0:T(8,128)(2,1)S(1)} %get-tuple-element.28.weights_ref.refs_2_, bf16[2048,16]{1,0:T(8,128)(2,1)S(1)} %get-tuple-element.29.points_ref.refs_3_, ...), custom_call_target="tpu_custom_call", output_to_operand_aliasing={{}: (6, {})} | custom-call | flops 524288000 | bytes 143360 | tf_op jit(solution)/shard_map/pallas_call | solution.py:429
  20.1 14.8 %all_to_all.5.refs_0_ = bf16[16,80,128]{2,1,0:T(8,128)(2,1)S(1)} all-to-all(bf16[16,80,128]{2,1,0:T(8,128)(2,1)S(1)} %shard_map.80), channel_id=1, replica_groups=mesh['case'=2,'wide'=16] {'wide'}, dimensions={0} | all-to-all | bytes 655360 | tf_op jit(solution)/shard_map/all_to_all | solution.py:463
  34.9 1.4 %shard_map.81 = (bf16[32,2048]{1,0:T(8,128)(2,1)}, f32[8,16]{1,0:T(8,128)}) custom-call(bf16[16,80,128]{2,1,0:T(8,128)(2,1)S(1)} %all_to_all.5.refs_0_), custom_call_target="tpu_custom_call" | custom-call | tf_op jit(solution)/shard_map/pallas_call | solution.py:274
  (2 shorter events, 0.0 us)
Async XLA Ops:
  0.6 5.2 %collective-permute-start = (f32[2,16]{1,0:T(2,128)}, f32[2,16]{1,0:T(2,128)S(1)}, u32[]{:S(2)}, u32[]{:S(2)}) collective-permute-start(f32[2,16]{1,0:T(2,128)} %over_hbm.1), channel_id=1, source_target_pairs={{0,1},{1,0},{2,3},{3,2},{4,5},{5,4},{6,7},{7,6},{8,9},{9,8},{10,11... | collective-permute-start | bytes 392 | tf_op jit(solution)/shard_map/ppermute | solution.py:442
  1.1 4.7 %collective-permute-start.2 = (f32[2,16]{1,0:T(2,128)}, f32[2,16]{1,0:T(2,128)S(1)}, u32[]{:S(2)}, u32[]{:S(2)}) collective-permute-start(f32[2,16]{1,0:T(2,128)} %over_hbm.1), channel_id=1, source_target_pairs={{0,3},{1,2},{2,1},{3,0},{4,7},{5,6},{6,5},{7,4},{8,11},{9,10},{10,... | collective-permute-start | bytes 392 | tf_op jit(solution)/shard_map/ppermute | solution.py:442
  3.8 3.8 %collective-permute-start.1 = (f32[2,16]{1,0:T(2,128)}, f32[2,16]{1,0:T(2,128)S(1)}, u32[]{:S(2)}, u32[]{:S(2)}) collective-permute-start(f32[2,16]{1,0:T(2,128)} %over_hbm.1), channel_id=1, source_target_pairs={{0,2},{1,3},{2,0},{3,1},{4,6},{5,7},{6,4},{7,5},{8,10},{9,11},{10,... | collective-permute-start | bytes 392 | tf_op jit(solution)/shard_map/ppermute | solution.py:442
  7.6 3.7 %collective-permute-start.3 = (f32[8,16]{1,0:T(8,128)S(1)}, f32[8,16]{1,0:T(8,128)S(1)}, u32[]{:S(2)}, u32[]{:S(2)}) collective-permute-start(f32[8,16]{1,0:T(8,128)S(1)} %pad_maximum_fusion), channel_id=1, source_target_pairs={{0,4},{1,5},{2,6},{3,7},{4,0},{5,1},{6,2},{7,3},{8,12},{9,13},{10,... | collective-permute-start | bytes 1544 | tf_op jit(solution)/shard_map/ppermute | solution.py:442
  11.3 5.7 %collective-permute-start.4 = (f32[16,16]{1,0:T(8,128)S(1)}, f32[16,16]{1,0:T(8,128)S(1)}, u32[]{:S(2)}, u32[]{:S(2)}) collective-permute-start(f32[16,16]{1,0:T(8,128)S(1)} %concatenate.8.lines_ref), channel_id=1, source_target_pairs={{0,8},{1,9},{2,10},{3,11},{4,12},{5,13},{6,14},{7,15},{8,0},{9,1},... | collective-permute-start | bytes 3080 | tf_op jit(solution)/shard_map/ppermute | solution.py:442

commit v4 on v3

--- a/solution.py
+++ b/solution.py
@@ -27,7 +27,7 @@
 
 
 TURN = WAVENUMBER / (2.0 * math.pi)
-HALF_SINE = fit(lambda f: math.sqrt(2.0) * np.sin(np.pi * f) / f, 4)
+HALF_SINE = fit(lambda f: math.sqrt(2.0) * (1.0 - 1e-6) * np.sin(np.pi * f) / f, 4)
 
 
 def horner(coefficients, x):
@@ -61,7 +61,7 @@
     capacity = 2 * owned // nwide
     lanes = min(capacity, 128)
     subs = capacity // lanes
-    return capacity, lanes, subs, ROWS * subs + 16
+    return capacity, lanes, subs, ROWS * subs + 8
 
 
 def source_kernel(
@@ -197,17 +197,23 @@
         for o in range(nwide):
             left[48 * o : 48 * o + 48, cols] = jnp.where(owner[:, cols] == o, values, jnp.zeros_like(values))
     packed = lax.dot_general(left[...], right[...], NT_DIMS, preferred_element_type=F32)
+    lane = lax.broadcasted_iota(jnp.int32, (8, lanes), 1)
     for o in range(nwide):
         block = packed[48 * o : 48 * o + 48]
         for s in range(subs):
             packed_ref[o, ROWS * s : ROWS * s + ROWS, :] = block[:ROWS, lanes * s : lanes * s + lanes].astype(BF16)
-        codes = [block[ROWS : ROWS + 2, lanes * s : lanes * s + lanes] for s in range(subs)]
-        codes_ref[o] = jnp.concatenate(codes + [jnp.zeros((8 - 2 * subs, lanes), F32)], axis=0)
+        codes = []
+        for s in range(subs):
+            upper_half = block[ROWS : ROWS + 8, lanes * s : lanes * s + lanes]
+            lower_half = jnp.concatenate([upper_half[:, lanes // 2 :], upper_half[:, : lanes // 2]], axis=1)
+            codes += [lower_half[:2], upper_half[:2]]
+        codes = jnp.concatenate(codes + [jnp.zeros((8 - 4 * subs, lanes), F32)] * (subs == 1), axis=0)
+        codes_ref[o] = jnp.where(lane < lanes // 2, 0.0, codes)
 
 
 def pack(spectra, ids, nwide):
     owned = spectra.shape[1]
-    capacity, lanes, subs, depth = pack_shape(nwide, owned)
+    capacity, lanes, subs, _ = pack_shape(nwide, owned)
     vmem = pl.BlockSpec(memory_space=pltpu.VMEM)
 
     def body(*refs):
@@ -216,7 +222,7 @@
     return pl.pallas_call(
         body,
         out_shape=(
-            jax.ShapeDtypeStruct((nwide, depth, lanes), BF16),
+            jax.ShapeDtypeStruct((nwide, ROWS * subs, lanes), BF16),
             jax.ShapeDtypeStruct((nwide, 8, lanes), F32),
         ),
         in_specs=[vmem] * 2,
@@ -233,22 +239,24 @@
     nwide, depth, lanes = received_ref.shape
     owned = spectra_ref.shape[1]
     listeners = pressure_ref.shape[1]
-    subs = (depth - 16) // ROWS
+    subs = (depth - 8) // ROWS
     heights = owned // LOW
     group = max(1, 256 // (lanes * subs))
     width = lanes * subs * group
     lows = lax.broadcasted_iota(jnp.int32, (LOW, width), 0).astype(F32)
     total = jnp.zeros((heights * ROWS, LOW), F32)
     sums = jnp.zeros((2 * HARM, lanes), F32)
+    lower = lax.broadcasted_iota(jnp.int32, (1, lanes), 1) < lanes // 2
     for first in range(0, nwide, group):
         blocks, high, low = [], [], []
         for o in range(first, first + group):
-            codes = received_ref[o, ROWS * subs : ROWS * subs + 16, :].astype(F32)
-            sums = sums + codes[8:16]
+            codes = received_ref[o, ROWS * subs : ROWS * subs + 8, :].astype(F32)
+            sums = sums + codes
+            turned = jnp.concatenate([codes[:, lanes // 2 :], codes[:, : lanes // 2]], axis=1)
             for s in range(subs):
                 blocks.append(received_ref[o, ROWS * s : ROWS * s + ROWS, :])
-                high.append(codes[2 * s : 2 * s + 1])
-                low.append(codes[2 * s + 1 : 2 * s + 2])
+                high.append(jnp.where(lower, turned[4 * s : 4 * s + 1], codes[4 * s + 2 : 4 * s + 3]))
+                low.append(jnp.where(lower, turned[4 * s + 1 : 4 * s + 2], codes[4 * s + 3 : 4 * s + 4]))
         values = jnp.concatenate(blocks, axis=1)
         high = jnp.concatenate(high, axis=1)
         low = jnp.concatenate(low, axis=1)
@@ -259,8 +267,7 @@
         total = total + lax.dot_general(picked, spread, NT_DIMS, preferred_element_type=F32)
     for h in range(heights):
         spectra_ref[:, LOW * h : LOW * h + LOW] = total[ROWS * h : ROWS * h + ROWS].astype(BF16)
-    third = [sums[:, listeners * p : listeners * p + listeners] for p in range(3)]
-    pressure_ref[...] = scale * ((third[2] + third[1]) + third[0])
+    pressure_ref[...] = scale * (sums[:, listeners : 2 * listeners] + sums[:, :listeners])
 
 
 def place(received, owned, listeners):
@@ -327,15 +334,15 @@
                 versine = half * half
                 cosine = 1.0 - versine
                 twoc = cosine + cosine
-                rest = jnp.maximum(2.0 - versine, 1e-30)
-                inv2 = (inv * inv).astype(BF16)
+                rest = 2.0 - versine
+                inv_bf = inv.astype(BF16)
                 c_prev, s_prev = inv, None
                 c_now = inv * cosine
                 s_now = (inv * half) * (rest * lax.rsqrt(rest))
                 for h in range(HARM):
                     c_bf, s_bf = c_now.astype(BF16), s_now.astype(BF16)
                     d, e = (inv * c_now).astype(BF16), (inv * s_now).astype(BF16)
-                    for m, value in enumerate((c_bf, s_bf, d, e, inv2 * c_bf, inv2 * s_bf)):
+                    for m, value in enumerate((c_bf, s_bf, d, e, inv_bf * d, inv_bf * e)):
                         mats[h][m].append(value)
                     if h < HARM - 1:
                         c_next = twoc * c_now - c_prev
@@ -371,10 +378,11 @@
     listeners = lines.shape[1]
     cells = []
     for value in pair_sums(lines, weights_ref, points_ref):
-        split = thirds(value)
+        top = value.astype(BF16).astype(F32)
+        split = [top, value - top]
         for j in range(value.shape[1] // listeners):
-            cell = [third[:, listeners * j : listeners * j + listeners] for third in split]
-            cell.append(jnp.zeros((2 * HARM, lanes - 3 * listeners), F32))
+            cell = [half[:, listeners * j : listeners * j + listeners] for half in split]
+            cell.append(jnp.zeros((2 * HARM, lanes - 2 * listeners), F32))
             cells.append(jnp.concatenate(cell, axis=1))
     return cells
 
@@ -384,20 +392,16 @@
         cells_ref[j] = cell
 
 
-def second_kernel(
-    steps, me_ref, lines_ref, weights_ref, points_ref, cells_ref, codes_ref, packed_in, packed_hbm, tail, sem
-):
-    lanes = codes_ref.shape[2]
-    depth = packed_hbm.shape[1]
+def second_kernel(steps, me_ref, lines_ref, weights_ref, points_ref, cells_ref, codes_ref, body_ref, packed_ref):
+    nwide, rows, lanes = body_ref.shape
+    for o in range(nwide):
+        packed_ref[o, :rows, :] = body_ref[o]
     early = cells_ref.shape[0]
     cells = [cells_ref[j] for j in range(early)]
     cells += cells_of(lines_ref[...], weights_ref, points_ref, lanes)
     for j, cell in enumerate(cells):
         owner = me_ref[0] ^ steps[j]
-        tail[owner] = jnp.concatenate([codes_ref[owner], cell], axis=0).astype(BF16)
-    copy = pltpu.make_async_copy(tail, packed_hbm.at[:, depth - 16 : depth, :], sem)
-    copy.start()
-    copy.wait()
+        packed_ref[owner, rows:, :] = (codes_ref[owner] + cell).astype(BF16)
 
 
 def first_sums(lines, weights, points, lanes):
@@ -415,27 +419,24 @@
     )(lines, weights, points)
 
 
-def second_sums(lines, weights, points, cells, codes, packed, steps):
+def second_sums(lines, weights, points, cells, codes, body, steps):
     owned = weights.shape[2]
-    nwide, depth, lanes = packed.shape
+    nwide, rows, lanes = body.shape
     pairs = lines.shape[0] // 2 * lines.shape[1] * owned
     vmem = pl.BlockSpec(memory_space=pltpu.VMEM)
-    anywhere = pl.BlockSpec(memory_space=pl.ANY)
     me = lax.axis_index("wide").reshape(1)
 
-    def body(*refs):
+    def kernel(*refs):
         second_kernel(steps, *refs)
 
     return pl.pallas_call(
-        body,
-        out_shape=jax.ShapeDtypeStruct(packed.shape, BF16),
-        in_specs=[pl.BlockSpec(memory_space=pltpu.SMEM)] + [vmem] * 5 + [anywhere],
-        out_specs=anywhere,
-        input_output_aliases={6: 0},
-        scratch_shapes=[pltpu.VMEM((nwide, 16, lanes), BF16), pltpu.SemaphoreType.DMA],
+        kernel,
+        out_shape=jax.ShapeDtypeStruct((nwide, rows + 8, lanes), BF16),
+        in_specs=[pl.BlockSpec(memory_space=pltpu.SMEM)] + [vmem] * 6,
+        out_specs=vmem,
         compiler_params=pltpu.CompilerParams(vmem_limit_bytes=40 * 2**20),
         cost_estimate=pl.CostEstimate(flops=pairs * 2000, bytes_accessed=owned * 70, transcendentals=pairs),
-    )(me, lines, weights, points, cells, codes, packed)
+    )(me, lines, weights, points, cells, codes, body)
 
 
 def swap(x, nwide, bit):

time: 36.6 us -> 36 us (0.984)
  blocking collectives: 14.8 us -> 14.3 us
    all_to_all x1, blocking collectives: 14.8 us -> 14.3 us  [shards(): lax.all_to_all(packed, 'wide', split_axis=0, concat_axis=0, tiled=True)]
where the time goes in v4:
time: 36 us; the launch traced here: 35.7 us
  blocking collectives  14.3 us (40%)
  Pallas kernels  10.9 us (30%)
  starting transfers between devices  7.49 us (21%)
  waiting for transfers between devices  2.28 us (6%)
  between operations  0.68 us (2%)
    all_to_all x1, blocking collectives, shards(): lax.all_to_all(packed, 'wide', split_axis=0, concat_axis=0, tiled=True)  14.3 us
    ppermute x5, starting transfers between devices, swap(): return lax.ppermute(x, 'wide', [(i, i ^ bit) for i in range(nwide)])  7.49 us
    pallas_call x1, Pallas kernels, second_sums(): pl.pallas_call(kernel, out_shape=jax.ShapeDtypeStruct((nwide, rows + 8, l...  3 us
    pallas_call x1, Pallas kernels, first_sums(): pl.pallas_call(first_kernel, out_shape=jax.ShapeDtypeStruct((devices, 2 *...  2.99 us
    ppermute x5, waiting for transfers between devices, swap(): return lax.ppermute(x, 'wide', [(i, i ^ bit) for i in range(nwide)])  2.28 us
    pallas_call x1, Pallas kernels, sources(): pl.pallas_call(source_kernel, out_shape=(jax.ShapeDtypeStruct((ROWS, owne...  1.96 us
    pallas_call x1, Pallas kernels, pack(): pl.pallas_call(body, out_shape=(jax.ShapeDtypeStruct((nwide, ROWS * subs,...  1.51 us
    pallas_call x1, Pallas kernels, place(): pl.pallas_call(body, out_shape=(jax.ShapeDtypeStruct((ROWS, owned), BF16)...  1.48 us
  transfers between devices with their start and end apart: 5, of which 2 were waited for; matrix products, arithmetic and copies ran while one was open for 0% of the time, Pallas kernels for 18%

profile of v4, /device:TPU:0, one launch (start us, length us, event | category | flops | bytes accessed | tf_op | source)
XLA Modules:
  0.0 35.7 jit_solution(11627580690483405483)
XLA Ops:
  0.6 0.5 %collective-permute-start = (f32[2,16]{1,0:T(2,128)}, f32[2,16]{1,0:T(2,128)S(1)}, u32[]{:S(2)}, u32[]{:S(2)}) collective-permute-start(f32[2,16]{1,0:T(2,128)} %over_hbm.1), channel_id=1, source_target_pairs={{0,1},{1,0},{2,3},{3,2},{4,5},{5,4},{6,7},{7,6},{8,9},{9,8},{10,11... | collective-permute-start | bytes 392 | tf_op jit(solution)/shard_map/ppermute | solution.py:443
  1.1 2.6 %collective-permute-start.2 = (f32[2,16]{1,0:T(2,128)}, f32[2,16]{1,0:T(2,128)S(1)}, u32[]{:S(2)}, u32[]{:S(2)}) collective-permute-start(f32[2,16]{1,0:T(2,128)} %over_hbm.1), channel_id=1, source_target_pairs={{0,3},{1,2},{2,1},{3,0},{4,7},{5,6},{6,5},{7,4},{8,11},{9,10},{10,... | collective-permute-start | bytes 392 | tf_op jit(solution)/shard_map/ppermute | solution.py:443
  3.8 0.0 collective-permute-start.1
  3.8 2.0 %shard_map.77 = (bf16[32,2048]{1,0:T(8,128)(2,1)S(1)}, bf16[4,16,2048]{2,1,0:T(8,128)(2,1)S(1)}, bf16[2048,16]{1,0:T(8,128)(2,1)S(1)}, s32[1,2048]{1,0:T(1,128)S(1)}, f32[2,16]{1,0:T(2,128)S(1)}) custom-call(bf16[5,16,2048]{2,1,0:T(8,128)(2,1)} %flow_hbm.1, bf16[3,2048]{1,0:T(4,128)(2,1)} %normals_hbm.1, bf16[3,2048]{1,0:T(4,128)(2,1)} %place_hbm.1, ...), custom_call_target="tpu_custom_call" | custom-call | tf_op jit(solution)/shard_map/pallas_call | solution.py:146
  5.8 0.0 collective-permute-done
  5.8 0.0 collective-permute-done.2
  5.8 1.7 %collective-permute-done.1 = f32[2,16]{1,0:T(2,128)S(1)} collective-permute-done((f32[2,16]{1,0:T(2,128)}, f32[2,16]{1,0:T(2,128)S(1)}, u32[]{:S(2)}, u32[]{:S(2)}) %collective-permute-start.1) | collective-permute-done | bytes 160 | tf_op jit(solution)/shard_map/ppermute | solution.py:443
  7.6 1.6 %collective-permute-start.3 = (f32[8,16]{1,0:T(8,128)S(1)}, f32[8,16]{1,0:T(8,128)S(1)}, u32[]{:S(2)}, u32[]{:S(2)}) collective-permute-start(f32[8,16]{1,0:T(8,128)S(1)} %pad_maximum_fusion), channel_id=1, source_target_pairs={{0,4},{1,5},{2,6},{3,7},{4,0},{5,1},{6,2},{7,3},{8,12},{9,13},{10,... | collective-permute-start | bytes 1544 | tf_op jit(solution)/shard_map/ppermute | solution.py:443
  9.2 1.5 %shard_map.78 = (bf16[16,64,128]{2,1,0:T(8,128)(2,1)S(1)}, f32[16,8,128]{2,1,0:T(8,128)S(1)}) custom-call(bf16[32,2048]{1,0:T(8,128)(2,1)S(1)} %get-tuple-element.24.refs_0_, s32[1,2048]{1,0:T(1,128)S(1)} %get-tuple-element.25.refs_1_), custom_call_target="tpu_custom_call" | custom-call | tf_op jit(solution)/shard_map/pallas_call | solution.py:222
  10.7 0.5 %collective-permute-done.3 = f32[8,16]{1,0:T(8,128)S(1)} collective-permute-done((f32[8,16]{1,0:T(8,128)S(1)}, f32[8,16]{1,0:T(8,128)S(1)}, u32[]{:S(2)}, u32[]{:S(2)}) %collective-permute-start.3) | collective-permute-done | bytes 544 | tf_op jit(solution)/shard_map/ppermute | solution.py:443
  11.3 2.6 %collective-permute-start.4 = (f32[16,16]{1,0:T(8,128)S(1)}, f32[16,16]{1,0:T(8,128)S(1)}, u32[]{:S(2)}, u32[]{:S(2)}) collective-permute-start(f32[16,16]{1,0:T(8,128)S(1)} %concatenate.8.lines_ref), channel_id=1, source_target_pairs={{0,8},{1,9},{2,10},{3,11},{4,12},{5,13},{6,14},{7,15},{8,0},{9,1},... | collective-permute-start | bytes 3080 | tf_op jit(solution)/shard_map/ppermute | solution.py:443
  13.9 3.0 %shard_map.79.refs_4_ = f32[8,8,128]{2,1,0:T(8,128)S(1)} custom-call(f32[16,16]{1,0:T(8,128)S(1)} %concatenate.8.lines_ref, bf16[4,16,2048]{2,1,0:T(8,128)(2,1)S(1)} %get-tuple-element.28.weights_ref.refs_2_, bf16[2048,16]{1,0:T(8,128)(2,1)S(1)} %get-tuple-element.29.points_ref.refs_3_), custom_call_target="tpu_custom_call" | custom-call | flops 524288000 | bytes 143360 | tf_op jit(solution)/shard_map/pallas_call | solution.py:412
  16.9 0.0 collective-permute-done.4.refs_1_
  16.9 3.0 %shard_map.80 = bf16[16,72,128]{2,1,0:T(8,128)(2,1)S(1)} custom-call(s32[1]{0:T(128)} %bitcast.refs_0_, f32[16,16]{1,0:T(8,128)S(1)} %collective-permute-done.4.refs_1_, bf16[4,16,2048]{2,1,0:T(8,128)(2,1)S(1)} %get-tuple-element.28.weights_ref.refs_2_, bf16[2048,16]{1,0:T(8,128)(2,1)S(1)} %get-tuple-element.29.points_ref.refs_3_, ...), custom_call_target="tpu_custom_call" | custom-call | flops 524288000 | bytes 143360 | tf_op jit(solution)/shard_map/pallas_call | solution.py:432
  19.9 14.3 %all_to_all.5.refs_0_ = bf16[16,72,128]{2,1,0:T(8,128)(2,1)S(1)} all-to-all(bf16[16,72,128]{2,1,0:T(8,128)(2,1)S(1)} %shard_map.80), channel_id=1, replica_groups=mesh['case'=2,'wide'=16] {'wide'}, dimensions={0} | all-to-all | bytes 589824 | tf_op jit(solution)/shard_map/all_to_all | solution.py:464
  34.2 1.5 %shard_map.81 = (bf16[32,2048]{1,0:T(8,128)(2,1)}, f32[8,16]{1,0:T(8,128)}) custom-call(bf16[16,72,128]{2,1,0:T(8,128)(2,1)S(1)} %all_to_all.5.refs_0_), custom_call_target="tpu_custom_call" | custom-call | tf_op jit(solution)/shard_map/pallas_call | solution.py:281
  (2 shorter events, 0.0 us)
Async XLA Ops:
  0.6 5.2 %collective-permute-start = (f32[2,16]{1,0:T(2,128)}, f32[2,16]{1,0:T(2,128)S(1)}, u32[]{:S(2)}, u32[]{:S(2)}) collective-permute-start(f32[2,16]{1,0:T(2,128)} %over_hbm.1), channel_id=1, source_target_pairs={{0,1},{1,0},{2,3},{3,2},{4,5},{5,4},{6,7},{7,6},{8,9},{9,8},{10,11... | collective-permute-start | bytes 392 | tf_op jit(solution)/shard_map/ppermute | solution.py:443
  1.1 4.7 %collective-permute-start.2 = (f32[2,16]{1,0:T(2,128)}, f32[2,16]{1,0:T(2,128)S(1)}, u32[]{:S(2)}, u32[]{:S(2)}) collective-permute-start(f32[2,16]{1,0:T(2,128)} %over_hbm.1), channel_id=1, source_target_pairs={{0,3},{1,2},{2,1},{3,0},{4,7},{5,6},{6,5},{7,4},{8,11},{9,10},{10,... | collective-permute-start | bytes 392 | tf_op jit(solution)/shard_map/ppermute | solution.py:443
  3.8 3.8 %collective-permute-start.1 = (f32[2,16]{1,0:T(2,128)}, f32[2,16]{1,0:T(2,128)S(1)}, u32[]{:S(2)}, u32[]{:S(2)}) collective-permute-start(f32[2,16]{1,0:T(2,128)} %over_hbm.1), channel_id=1, source_target_pairs={{0,2},{1,3},{2,0},{3,1},{4,6},{5,7},{6,4},{7,5},{8,10},{9,11},{10,... | collective-permute-start | bytes 392 | tf_op jit(solution)/shard_map/ppermute | solution.py:443
  7.6 3.7 %collective-permute-start.3 = (f32[8,16]{1,0:T(8,128)S(1)}, f32[8,16]{1,0:T(8,128)S(1)}, u32[]{:S(2)}, u32[]{:S(2)}) collective-permute-start(f32[8,16]{1,0:T(8,128)S(1)} %pad_maximum_fusion), channel_id=1, source_target_pairs={{0,4},{1,5},{2,6},{3,7},{4,0},{5,1},{6,2},{7,3},{8,12},{9,13},{10,... | collective-permute-start | bytes 1544 | tf_op jit(solution)/shard_map/ppermute | solution.py:443
  11.3 5.6 %collective-permute-start.4 = (f32[16,16]{1,0:T(8,128)S(1)}, f32[16,16]{1,0:T(8,128)S(1)}, u32[]{:S(2)}, u32[]{:S(2)}) collective-permute-start(f32[16,16]{1,0:T(8,128)S(1)} %concatenate.8.lines_ref), channel_id=1, source_target_pairs={{0,8},{1,9},{2,10},{3,11},{4,12},{5,13},{6,14},{7,15},{8,0},{9,1},... | collective-permute-start | bytes 3080 | tf_op jit(solution)/shard_map/ppermute | solution.py:443

commit v5 on v4

--- a/solution.py
+++ b/solution.py
@@ -94,6 +94,14 @@
         copy.wait()
     table = table_ref[...]
     scale = TURN * TURN
+    for start in range(0, owned, step):
+        cols = slice(start, start + step)
+        place = place_ref[:, cols].astype(F32)
+        px, py, pz = place[0:1], place[1:2], place[2:3]
+        here = scale * (px * px + py * py + pz * pz + (2.0 * GROUND) * pz)
+        one, none = jnp.ones_like(here), jnp.zeros_like(here)
+        points = jnp.concatenate([px] * 3 + [py] * 3 + [one] * 3 + thirds(here) + [none] * 4, axis=0)
+        points_ref[cols, :] = points.T.astype(BF16)
     for start in range(0, owned, step):
         if start % wide == 0:
             flows[start // wide].wait()
@@ -129,10 +137,6 @@
             weights_ref[h, :, cols] = jnp.concatenate(
                 [group, along_high, along - along_high, jnp.zeros((4, step), F32)], axis=0
             ).astype(BF16)
-        here = scale * (px * px + py * py + pz * pz + (2.0 * GROUND) * pz)
-        one = jnp.ones_like(here)
-        points = jnp.concatenate([px] * 3 + [py] * 3 + [one] * 3 + thirds(here) + [none] * 4, axis=0)
-        points_ref[cols, :] = points.T.astype(BF16)
     for copy in passed:
         copy.wait()
 
@@ -290,8 +294,8 @@
     )(received)
 
 
-SUB = 64
-KINDS = 6
+SUB = 128
+KINDS = 3
 
 
 def pair_sums(lines, weights_ref, points_ref):
@@ -308,7 +312,7 @@
         thirds((-2.0 * scale) * over_x) + thirds((-2.0 * scale) * over_y) + thirds(there) + [one] * 3 + [zero] * 4,
         axis=0,
     ).astype(BF16)
-    width = min(256, count * listeners)
+    width = min(128, count * listeners)
     made = []
     for left in range(0, count * listeners, width):
         view = views[:, left : left + width]
@@ -342,8 +346,8 @@
                 for h in range(HARM):
                     c_bf, s_bf = c_now.astype(BF16), s_now.astype(BF16)
                     d, e = (inv * c_now).astype(BF16), (inv * s_now).astype(BF16)
-                    for m, value in enumerate((c_bf, s_bf, d, e, inv_bf * d, inv_bf * e)):
-                        mats[h][m].append(value)
+                    for m, pair in enumerate(((c_bf, s_bf), (d, e), (inv_bf * d, inv_bf * e))):
+                        mats[h][m].append(jnp.concatenate(pair, axis=1))
                     if h < HARM - 1:
                         c_next = twoc * c_now - c_prev
                         s_next = twoc * s_now - s_prev if h else twoc * s_now
@@ -356,6 +360,7 @@
         rows = []
         for h in range(HARM):
             wavenum = WAVENUMBER * (h + 1)
+            totals[h] = [half for both in totals[h] for half in (both[:, :width], both[:, width:])]
             cos_sum, sin_sum = totals[h][0], totals[h][1]
 
             def loads(m):

time: 36 us -> 35.8 us (level)
  Pallas kernels: 10.9 us -> 10.5 us
where the time goes in v5:
time: 35.8 us; the launch traced here: 35.5 us
  blocking collectives  14.6 us (41%)
  Pallas kernels  10.5 us (29%)
  starting transfers between devices  7.49 us (21%)
  waiting for transfers between devices  2.19 us (6%)
  between operations  0.68 us (2%)
    all_to_all x1, blocking collectives, shards(): lax.all_to_all(packed, 'wide', split_axis=0, concat_axis=0, tiled=True)  14.6 us
    ppermute x5, starting transfers between devices, swap(): return lax.ppermute(x, 'wide', [(i, i ^ bit) for i in range(nwide)])  7.49 us
    pallas_call x1, Pallas kernels, second_sums(): pl.pallas_call(kernel, out_shape=jax.ShapeDtypeStruct((nwide, rows + 8, l...  2.76 us
    pallas_call x1, Pallas kernels, first_sums(): pl.pallas_call(first_kernel, out_shape=jax.ShapeDtypeStruct((devices, 2 *...  2.74 us
    ppermute x5, waiting for transfers between devices, swap(): return lax.ppermute(x, 'wide', [(i, i ^ bit) for i in range(nwide)])  2.19 us
    pallas_call x1, Pallas kernels, sources(): pl.pallas_call(source_kernel, out_shape=(jax.ShapeDtypeStruct((ROWS, owne...  2.05 us
    pallas_call x1, Pallas kernels, pack(): pl.pallas_call(body, out_shape=(jax.ShapeDtypeStruct((nwide, ROWS * subs,...  1.51 us
    pallas_call x1, Pallas kernels, place(): pl.pallas_call(body, out_shape=(jax.ShapeDtypeStruct((ROWS, owned), BF16)...  1.49 us
  transfers between devices with their start and end apart: 5, of which 2 were waited for; matrix products, arithmetic and copies ran while one was open for 0% of the time, Pallas kernels for 18%

profile of v5, /device:TPU:0, one launch (start us, length us, event | category | flops | bytes accessed | tf_op | source)
XLA Modules:
  0.0 35.5 jit_solution(1093834711889055996)
XLA Ops:
  0.6 0.5 %collective-permute-start = (f32[2,16]{1,0:T(2,128)}, f32[2,16]{1,0:T(2,128)S(1)}, u32[]{:S(2)}, u32[]{:S(2)}) collective-permute-start(f32[2,16]{1,0:T(2,128)} %over_hbm.1), channel_id=1, source_target_pairs={{0,1},{1,0},{2,3},{3,2},{4,5},{5,4},{6,7},{7,6},{8,9},{9,8},{10,11... | collective-permute-start | bytes 392 | tf_op jit(solution)/shard_map/ppermute | solution.py:448
  1.1 2.6 %collective-permute-start.2 = (f32[2,16]{1,0:T(2,128)}, f32[2,16]{1,0:T(2,128)S(1)}, u32[]{:S(2)}, u32[]{:S(2)}) collective-permute-start(f32[2,16]{1,0:T(2,128)} %over_hbm.1), channel_id=1, source_target_pairs={{0,3},{1,2},{2,1},{3,0},{4,7},{5,6},{6,5},{7,4},{8,11},{9,10},{10,... | collective-permute-start | bytes 392 | tf_op jit(solution)/shard_map/ppermute | solution.py:448
  3.8 0.0 collective-permute-start.1
  3.8 2.0 %shard_map.77 = (bf16[32,2048]{1,0:T(8,128)(2,1)S(1)}, bf16[4,16,2048]{2,1,0:T(8,128)(2,1)S(1)}, bf16[2048,16]{1,0:T(8,128)(2,1)S(1)}, s32[1,2048]{1,0:T(1,128)S(1)}, f32[2,16]{1,0:T(2,128)S(1)}) custom-call(bf16[5,16,2048]{2,1,0:T(8,128)(2,1)} %flow_hbm.1, bf16[3,2048]{1,0:T(4,128)(2,1)} %normals_hbm.1, bf16[3,2048]{1,0:T(4,128)(2,1)} %place_hbm.1, ...), custom_call_target="tpu_custom_call" | custom-call | tf_op jit(solution)/shard_map/pallas_call | solution.py:150
  5.9 0.0 collective-permute-done
  5.9 0.0 collective-permute-done.2
  5.9 1.7 %collective-permute-done.1 = f32[2,16]{1,0:T(2,128)S(1)} collective-permute-done((f32[2,16]{1,0:T(2,128)}, f32[2,16]{1,0:T(2,128)S(1)}, u32[]{:S(2)}, u32[]{:S(2)}) %collective-permute-start.1) | collective-permute-done | bytes 160 | tf_op jit(solution)/shard_map/ppermute | solution.py:448
  7.6 1.6 %collective-permute-start.3 = (f32[8,16]{1,0:T(8,128)S(1)}, f32[8,16]{1,0:T(8,128)S(1)}, u32[]{:S(2)}, u32[]{:S(2)}) collective-permute-start(f32[8,16]{1,0:T(8,128)S(1)} %pad_maximum_fusion), channel_id=1, source_target_pairs={{0,4},{1,5},{2,6},{3,7},{4,0},{5,1},{6,2},{7,3},{8,12},{9,13},{10,... | collective-permute-start | bytes 1544 | tf_op jit(solution)/shard_map/ppermute | solution.py:448
  9.2 1.5 %shard_map.78 = (bf16[16,64,128]{2,1,0:T(8,128)(2,1)S(1)}, f32[16,8,128]{2,1,0:T(8,128)S(1)}) custom-call(bf16[32,2048]{1,0:T(8,128)(2,1)S(1)} %get-tuple-element.24.refs_0_, s32[1,2048]{1,0:T(1,128)S(1)} %get-tuple-element.25.refs_1_), custom_call_target="tpu_custom_call" | custom-call | tf_op jit(solution)/shard_map/pallas_call | solution.py:226
  10.7 0.5 %collective-permute-done.3 = f32[8,16]{1,0:T(8,128)S(1)} collective-permute-done((f32[8,16]{1,0:T(8,128)S(1)}, f32[8,16]{1,0:T(8,128)S(1)}, u32[]{:S(2)}, u32[]{:S(2)}) %collective-permute-start.3) | collective-permute-done | bytes 544 | tf_op jit(solution)/shard_map/ppermute | solution.py:448
  11.3 2.6 %collective-permute-start.4 = (f32[16,16]{1,0:T(8,128)S(1)}, f32[16,16]{1,0:T(8,128)S(1)}, u32[]{:S(2)}, u32[]{:S(2)}) collective-permute-start(f32[16,16]{1,0:T(8,128)S(1)} %concatenate.8.lines_ref), channel_id=1, source_target_pairs={{0,8},{1,9},{2,10},{3,11},{4,12},{5,13},{6,14},{7,15},{8,0},{9,1},... | collective-permute-start | bytes 3080 | tf_op jit(solution)/shard_map/ppermute | solution.py:448
  13.9 2.7 %shard_map.79.refs_4_ = f32[8,8,128]{2,1,0:T(8,128)S(1)} custom-call(f32[16,16]{1,0:T(8,128)S(1)} %concatenate.8.lines_ref, bf16[4,16,2048]{2,1,0:T(8,128)(2,1)S(1)} %get-tuple-element.28.weights_ref.refs_2_, bf16[2048,16]{1,0:T(8,128)(2,1)S(1)} %get-tuple-element.29.points_ref.refs_3_), custom_call_target="tpu_custom_call" | custom-call | flops 524288000 | bytes 143360 | tf_op jit(solution)/shard_map/pallas_call | solution.py:417
  16.7 0.0 collective-permute-done.4.refs_1_
  16.7 2.8 %shard_map.80 = bf16[16,72,128]{2,1,0:T(8,128)(2,1)S(1)} custom-call(s32[1]{0:T(128)} %bitcast.refs_0_, f32[16,16]{1,0:T(8,128)S(1)} %collective-permute-done.4.refs_1_, bf16[4,16,2048]{2,1,0:T(8,128)(2,1)S(1)} %get-tuple-element.28.weights_ref.refs_2_, bf16[2048,16]{1,0:T(8,128)(2,1)S(1)} %get-tuple-element.29.points_ref.refs_3_, ...), custom_call_target="tpu_custom_call" | custom-call | flops 524288000 | bytes 143360 | tf_op jit(solution)/shard_map/pallas_call | solution.py:437
  19.4 14.6 %all_to_all.5.refs_0_ = bf16[16,72,128]{2,1,0:T(8,128)(2,1)S(1)} all-to-all(bf16[16,72,128]{2,1,0:T(8,128)(2,1)S(1)} %shard_map.80), channel_id=1, replica_groups=mesh['case'=2,'wide'=16] {'wide'}, dimensions={0} | all-to-all | bytes 589824 | tf_op jit(solution)/shard_map/all_to_all | solution.py:469
  34.0 1.5 %shard_map.81 = (bf16[32,2048]{1,0:T(8,128)(2,1)}, f32[8,16]{1,0:T(8,128)}) custom-call(bf16[16,72,128]{2,1,0:T(8,128)(2,1)S(1)} %all_to_all.5.refs_0_), custom_call_target="tpu_custom_call" | custom-call | tf_op jit(solution)/shard_map/pallas_call | solution.py:285
  (2 shorter events, 0.0 us)
Async XLA Ops:
  0.6 5.3 %collective-permute-start = (f32[2,16]{1,0:T(2,128)}, f32[2,16]{1,0:T(2,128)S(1)}, u32[]{:S(2)}, u32[]{:S(2)}) collective-permute-start(f32[2,16]{1,0:T(2,128)} %over_hbm.1), channel_id=1, source_target_pairs={{0,1},{1,0},{2,3},{3,2},{4,5},{5,4},{6,7},{7,6},{8,9},{9,8},{10,11... | collective-permute-start | bytes 392 | tf_op jit(solution)/shard_map/ppermute | solution.py:448
  1.1 4.8 %collective-permute-start.2 = (f32[2,16]{1,0:T(2,128)}, f32[2,16]{1,0:T(2,128)S(1)}, u32[]{:S(2)}, u32[]{:S(2)}) collective-permute-start(f32[2,16]{1,0:T(2,128)} %over_hbm.1), channel_id=1, source_target_pairs={{0,3},{1,2},{2,1},{3,0},{4,7},{5,6},{6,5},{7,4},{8,11},{9,10},{10,... | collective-permute-start | bytes 392 | tf_op jit(solution)/shard_map/ppermute | solution.py:448
  3.8 3.8 %collective-permute-start.1 = (f32[2,16]{1,0:T(2,128)}, f32[2,16]{1,0:T(2,128)S(1)}, u32[]{:S(2)}, u32[]{:S(2)}) collective-permute-start(f32[2,16]{1,0:T(2,128)} %over_hbm.1), channel_id=1, source_target_pairs={{0,2},{1,3},{2,0},{3,1},{4,6},{5,7},{6,4},{7,5},{8,10},{9,11},{10,... | collective-permute-start | bytes 392 | tf_op jit(solution)/shard_map/ppermute | solution.py:448
  7.6 3.7 %collective-permute-start.3 = (f32[8,16]{1,0:T(8,128)S(1)}, f32[8,16]{1,0:T(8,128)S(1)}, u32[]{:S(2)}, u32[]{:S(2)}) collective-permute-start(f32[8,16]{1,0:T(8,128)S(1)} %pad_maximum_fusion), channel_id=1, source_target_pairs={{0,4},{1,5},{2,6},{3,7},{4,0},{5,1},{6,2},{7,3},{8,12},{9,13},{10,... | collective-permute-start | bytes 1544 | tf_op jit(solution)/shard_map/ppermute | solution.py:448
  11.3 5.4 %collective-permute-start.4 = (f32[16,16]{1,0:T(8,128)S(1)}, f32[16,16]{1,0:T(8,128)S(1)}, u32[]{:S(2)}, u32[]{:S(2)}) collective-permute-start(f32[16,16]{1,0:T(8,128)S(1)} %concatenate.8.lines_ref), channel_id=1, source_target_pairs={{0,8},{1,9},{2,10},{3,11},{4,12},{5,13},{6,14},{7,15},{8,0},{9,1},... | collective-permute-start | bytes 3080 | tf_op jit(solution)/shard_map/ppermute | solution.py:448

commit v6 on v4

--- a/solution.py
+++ b/solution.py
@@ -27,7 +27,7 @@
 
 
 TURN = WAVENUMBER / (2.0 * math.pi)
-HALF_SINE = fit(lambda f: math.sqrt(2.0) * (1.0 - 1e-6) * np.sin(np.pi * f) / f, 4)
+HALF_SINE = fit(lambda f: math.sqrt(2.0) * np.sin(np.pi * f) / f, 4)
 
 
 def horner(coefficients, x):
@@ -71,32 +71,23 @@
 ):
     owned = flow_ref.shape[2]
     step = min(256, owned)
-    pieces = 4
-    wide = owned // pieces
     copies = [
         pltpu.make_async_copy(normals_hbm, normals_ref, sems.at[0]),
         pltpu.make_async_copy(place_hbm, place_ref, sems.at[1]),
         pltpu.make_async_copy(table_hbm, table_ref, sems.at[2]),
+        pltpu.make_async_copy(flow_hbm, flow_ref, sems.at[5]),
     ]
     passed = [
         pltpu.make_async_copy(ids_hbm, ids_ref, sems.at[3]),
         pltpu.make_async_copy(over_hbm, mine_ref, sems.at[4]),
     ]
-    flows = [
-        pltpu.make_async_copy(
-            flow_hbm.at[:, :, wide * p : wide * p + wide], flow_ref.at[:, :, wide * p : wide * p + wide], sems.at[5 + p]
-        )
-        for p in range(pieces)
-    ]
-    for copy in copies + flows + passed:
+    for copy in copies + passed:
         copy.start()
     for copy in copies:
         copy.wait()
     table = table_ref[...]
     scale = TURN * TURN
     for start in range(0, owned, step):
-        if start % wide == 0:
-            flows[start // wide].wait()
         cols = slice(start, start + step)
         normal = normals_ref[:, cols].astype(F32)
         n0, n1, n2 = normal[0:1], normal[1:2], normal[2:3]
@@ -159,7 +150,7 @@
             pltpu.VMEM(normals.shape, BF16),
             pltpu.VMEM(positions.shape, BF16),
             pltpu.VMEM(table.shape, BF16),
-            pltpu.SemaphoreType.DMA((9,)),
+            pltpu.SemaphoreType.DMA((6,)),
         ],
         compiler_params=pltpu.CompilerParams(vmem_limit_bytes=32 * 2**20),
     )(*(pltpu.with_memory_space_constraint(x, pltpu.HBM) for x in arrays))
@@ -290,8 +281,8 @@
     )(received)
 
 
-SUB = 64
-KINDS = 6
+SUB = 128
+KINDS = 3
 
 
 def pair_sums(lines, weights_ref, points_ref):
@@ -308,7 +299,7 @@
         thirds((-2.0 * scale) * over_x) + thirds((-2.0 * scale) * over_y) + thirds(there) + [one] * 3 + [zero] * 4,
         axis=0,
     ).astype(BF16)
-    width = min(256, count * listeners)
+    width = min(128, count * listeners)
     made = []
     for left in range(0, count * listeners, width):
         view = views[:, left : left + width]
@@ -334,7 +325,7 @@
                 versine = half * half
                 cosine = 1.0 - versine
                 twoc = cosine + cosine
-                rest = 2.0 - versine
+                rest = jnp.maximum(2.0 - versine, 1e-30)
                 inv_bf = inv.astype(BF16)
                 c_prev, s_prev = inv, None
                 c_now = inv * cosine
@@ -342,8 +333,8 @@
                 for h in range(HARM):
                     c_bf, s_bf = c_now.astype(BF16), s_now.astype(BF16)
                     d, e = (inv * c_now).astype(BF16), (inv * s_now).astype(BF16)
-                    for m, value in enumerate((c_bf, s_bf, d, e, inv_bf * d, inv_bf * e)):
-                        mats[h][m].append(value)
+                    for m, pair in enumerate(((c_bf, s_bf), (d, e), (inv_bf * d, inv_bf * e))):
+                        mats[h][m].append(jnp.concatenate(pair, axis=1))
                     if h < HARM - 1:
                         c_next = twoc * c_now - c_prev
                         s_next = twoc * s_now - s_prev if h else twoc * s_now
@@ -356,6 +347,7 @@
         rows = []
         for h in range(HARM):
             wavenum = WAVENUMBER * (h + 1)
+            totals[h] = [half for both in totals[h] for half in (both[:, :width], both[:, width:])]
             cos_sum, sin_sum = totals[h][0], totals[h][1]
 
             def loads(m):

time: 36 us -> 35.8 us (level)
  Pallas kernels: 10.9 us -> 10.1 us
  waiting for transfers between devices: 2.28 us -> 2.64 us
    ppermute x5, waiting for transfers between devices: 2.28 us -> 2.64 us  [swap(): return lax.ppermute(x, 'wide', [(i, i ^ bit) for i in range(nwide)])]
    pallas_call x1, Pallas kernels: 1.96 us -> 1.6 us  [sources(): pl.pallas_call(source_kernel, out_shape=(jax.ShapeDtypeStruct((ROWS, owne...]
  transfers between devices with their start and end apart: 5 -> 5, of which waited for: 2 -> 2; matrix products, arithmetic and copies ran while one was open for 0% -> 0% of each run, Pallas kernels for 18% -> 17%
where the time goes in v6:
time: 35.8 us; the launch traced here: 35.5 us
  blocking collectives  14.5 us (41%)
  Pallas kernels  10.1 us (28%)
  starting transfers between devices  7.49 us (21%)
  waiting for transfers between devices  2.64 us (7%)
  between operations  0.68 us (2%)
    all_to_all x1, blocking collectives, shards(): lax.all_to_all(packed, 'wide', split_axis=0, concat_axis=0, tiled=True)  14.5 us
    ppermute x5, starting transfers between devices, swap(): return lax.ppermute(x, 'wide', [(i, i ^ bit) for i in range(nwide)])  7.49 us
    pallas_call x1, Pallas kernels, second_sums(): pl.pallas_call(kernel, out_shape=jax.ShapeDtypeStruct((nwide, rows + 8, l...  2.77 us
    pallas_call x1, Pallas kernels, first_sums(): pl.pallas_call(first_kernel, out_shape=jax.ShapeDtypeStruct((devices, 2 *...  2.75 us
    ppermute x5, waiting for transfers between devices, swap(): return lax.ppermute(x, 'wide', [(i, i ^ bit) for i in range(nwide)])  2.64 us
    pallas_call x1, Pallas kernels, sources(): pl.pallas_call(source_kernel, out_shape=(jax.ShapeDtypeStruct((ROWS, owne...  1.6 us
    pallas_call x1, Pallas kernels, pack(): pl.pallas_call(body, out_shape=(jax.ShapeDtypeStruct((nwide, ROWS * subs,...  1.51 us
    pallas_call x1, Pallas kernels, place(): pl.pallas_call(body, out_shape=(jax.ShapeDtypeStruct((ROWS, owned), BF16)...  1.48 us
  transfers between devices with their start and end apart: 5, of which 2 were waited for; matrix products, arithmetic and copies ran while one was open for 0% of the time, Pallas kernels for 17%

profile of v6, /device:TPU:0, one launch (start us, length us, event | category | flops | bytes accessed | tf_op | source)
XLA Modules:
  0.0 35.5 jit_solution(15265789880746898526)
XLA Ops:
  0.6 0.5 %collective-permute-start = (f32[2,16]{1,0:T(2,128)}, f32[2,16]{1,0:T(2,128)S(1)}, u32[]{:S(2)}, u32[]{:S(2)}) collective-permute-start(f32[2,16]{1,0:T(2,128)} %over_hbm.1), channel_id=1, source_target_pairs={{0,1},{1,0},{2,3},{3,2},{4,5},{5,4},{6,7},{7,6},{8,9},{9,8},{10,11... | collective-permute-start | bytes 392 | tf_op jit(solution)/shard_map/ppermute | solution.py:435
  1.1 2.6 %collective-permute-start.2 = (f32[2,16]{1,0:T(2,128)}, f32[2,16]{1,0:T(2,128)S(1)}, u32[]{:S(2)}, u32[]{:S(2)}) collective-permute-start(f32[2,16]{1,0:T(2,128)} %over_hbm.1), channel_id=1, source_target_pairs={{0,3},{1,2},{2,1},{3,0},{4,7},{5,6},{6,5},{7,4},{8,11},{9,10},{10,... | collective-permute-start | bytes 392 | tf_op jit(solution)/shard_map/ppermute | solution.py:435
  3.8 0.0 collective-permute-start.1
  3.8 1.6 %shard_map.77 = (bf16[32,2048]{1,0:T(8,128)(2,1)S(1)}, bf16[4,16,2048]{2,1,0:T(8,128)(2,1)S(1)}, bf16[2048,16]{1,0:T(8,128)(2,1)S(1)}, s32[1,2048]{1,0:T(1,128)S(1)}, f32[2,16]{1,0:T(2,128)S(1)}) custom-call(bf16[5,16,2048]{2,1,0:T(8,128)(2,1)} %flow_hbm.1, bf16[3,2048]{1,0:T(4,128)(2,1)} %normals_hbm.1, bf16[3,2048]{1,0:T(4,128)(2,1)} %place_hbm.1, ...), custom_call_target="tpu_custom_call" | custom-call | tf_op jit(solution)/shard_map/pallas_call | solution.py:137
  5.4 0.0 collective-permute-done
  5.5 0.0 collective-permute-done.2
  5.5 2.1 %collective-permute-done.1 = f32[2,16]{1,0:T(2,128)S(1)} collective-permute-done((f32[2,16]{1,0:T(2,128)}, f32[2,16]{1,0:T(2,128)S(1)}, u32[]{:S(2)}, u32[]{:S(2)}) %collective-permute-start.1) | collective-permute-done | bytes 160 | tf_op jit(solution)/shard_map/ppermute | solution.py:435
  7.6 1.6 %collective-permute-start.3 = (f32[8,16]{1,0:T(8,128)S(1)}, f32[8,16]{1,0:T(8,128)S(1)}, u32[]{:S(2)}, u32[]{:S(2)}) collective-permute-start(f32[8,16]{1,0:T(8,128)S(1)} %pad_maximum_fusion), channel_id=1, source_target_pairs={{0,4},{1,5},{2,6},{3,7},{4,0},{5,1},{6,2},{7,3},{8,12},{9,13},{10,... | collective-permute-start | bytes 1544 | tf_op jit(solution)/shard_map/ppermute | solution.py:435
  9.2 1.5 %shard_map.78 = (bf16[16,64,128]{2,1,0:T(8,128)(2,1)S(1)}, f32[16,8,128]{2,1,0:T(8,128)S(1)}) custom-call(bf16[32,2048]{1,0:T(8,128)(2,1)S(1)} %get-tuple-element.24.refs_0_, s32[1,2048]{1,0:T(1,128)S(1)} %get-tuple-element.25.refs_1_), custom_call_target="tpu_custom_call" | custom-call | tf_op jit(solution)/shard_map/pallas_call | solution.py:213
  10.7 0.5 %collective-permute-done.3 = f32[8,16]{1,0:T(8,128)S(1)} collective-permute-done((f32[8,16]{1,0:T(8,128)S(1)}, f32[8,16]{1,0:T(8,128)S(1)}, u32[]{:S(2)}, u32[]{:S(2)}) %collective-permute-start.3) | collective-permute-done | bytes 544 | tf_op jit(solution)/shard_map/ppermute | solution.py:435
  11.3 2.6 %collective-permute-start.4 = (f32[16,16]{1,0:T(8,128)S(1)}, f32[16,16]{1,0:T(8,128)S(1)}, u32[]{:S(2)}, u32[]{:S(2)}) collective-permute-start(f32[16,16]{1,0:T(8,128)S(1)} %concatenate.8.lines_ref), channel_id=1, source_target_pairs={{0,8},{1,9},{2,10},{3,11},{4,12},{5,13},{6,14},{7,15},{8,0},{9,1},... | collective-permute-start | bytes 3080 | tf_op jit(solution)/shard_map/ppermute | solution.py:435
  13.9 2.8 %shard_map.79.refs_4_ = f32[8,8,128]{2,1,0:T(8,128)S(1)} custom-call(f32[16,16]{1,0:T(8,128)S(1)} %concatenate.8.lines_ref, bf16[4,16,2048]{2,1,0:T(8,128)(2,1)S(1)} %get-tuple-element.28.weights_ref.refs_2_, bf16[2048,16]{1,0:T(8,128)(2,1)S(1)} %get-tuple-element.29.points_ref.refs_3_), custom_call_target="tpu_custom_call" | custom-call | flops 524288000 | bytes 143360 | tf_op jit(solution)/shard_map/pallas_call | solution.py:404
  16.7 0.0 collective-permute-done.4.refs_1_
  16.7 2.8 %shard_map.80 = bf16[16,72,128]{2,1,0:T(8,128)(2,1)S(1)} custom-call(s32[1]{0:T(128)} %bitcast.refs_0_, f32[16,16]{1,0:T(8,128)S(1)} %collective-permute-done.4.refs_1_, bf16[4,16,2048]{2,1,0:T(8,128)(2,1)S(1)} %get-tuple-element.28.weights_ref.refs_2_, bf16[2048,16]{1,0:T(8,128)(2,1)S(1)} %get-tuple-element.29.points_ref.refs_3_, ...), custom_call_target="tpu_custom_call" | custom-call | flops 524288000 | bytes 143360 | tf_op jit(solution)/shard_map/pallas_call | solution.py:424
  19.5 14.5 %all_to_all.5.refs_0_ = bf16[16,72,128]{2,1,0:T(8,128)(2,1)S(1)} all-to-all(bf16[16,72,128]{2,1,0:T(8,128)(2,1)S(1)} %shard_map.80), channel_id=1, replica_groups=mesh['case'=2,'wide'=16] {'wide'}, dimensions={0} | all-to-all | bytes 589824 | tf_op jit(solution)/shard_map/all_to_all | solution.py:456
  34.0 1.5 %shard_map.81 = (bf16[32,2048]{1,0:T(8,128)(2,1)}, f32[8,16]{1,0:T(8,128)}) custom-call(bf16[16,72,128]{2,1,0:T(8,128)(2,1)S(1)} %all_to_all.5.refs_0_), custom_call_target="tpu_custom_call" | custom-call | tf_op jit(solution)/shard_map/pallas_call | solution.py:272
  (2 shorter events, 0.0 us)
Async XLA Ops:
  0.6 4.8 %collective-permute-start = (f32[2,16]{1,0:T(2,128)}, f32[2,16]{1,0:T(2,128)S(1)}, u32[]{:S(2)}, u32[]{:S(2)}) collective-permute-start(f32[2,16]{1,0:T(2,128)} %over_hbm.1), channel_id=1, source_target_pairs={{0,1},{1,0},{2,3},{3,2},{4,5},{5,4},{6,7},{7,6},{8,9},{9,8},{10,11... | collective-permute-start | bytes 392 | tf_op jit(solution)/shard_map/ppermute | solution.py:435
  1.1 4.3 %collective-permute-start.2 = (f32[2,16]{1,0:T(2,128)}, f32[2,16]{1,0:T(2,128)S(1)}, u32[]{:S(2)}, u32[]{:S(2)}) collective-permute-start(f32[2,16]{1,0:T(2,128)} %over_hbm.1), channel_id=1, source_target_pairs={{0,3},{1,2},{2,1},{3,0},{4,7},{5,6},{6,5},{7,4},{8,11},{9,10},{10,... | collective-permute-start | bytes 392 | tf_op jit(solution)/shard_map/ppermute | solution.py:435
  3.8 3.8 %collective-permute-start.1 = (f32[2,16]{1,0:T(2,128)}, f32[2,16]{1,0:T(2,128)S(1)}, u32[]{:S(2)}, u32[]{:S(2)}) collective-permute-start(f32[2,16]{1,0:T(2,128)} %over_hbm.1), channel_id=1, source_target_pairs={{0,2},{1,3},{2,0},{3,1},{4,6},{5,7},{6,4},{7,5},{8,10},{9,11},{10,... | collective-permute-start | bytes 392 | tf_op jit(solution)/shard_map/ppermute | solution.py:435
  7.6 3.7 %collective-permute-start.3 = (f32[8,16]{1,0:T(8,128)S(1)}, f32[8,16]{1,0:T(8,128)S(1)}, u32[]{:S(2)}, u32[]{:S(2)}) collective-permute-start(f32[8,16]{1,0:T(8,128)S(1)} %pad_maximum_fusion), channel_id=1, source_target_pairs={{0,4},{1,5},{2,6},{3,7},{4,0},{5,1},{6,2},{7,3},{8,12},{9,13},{10,... | collective-permute-start | bytes 1544 | tf_op jit(solution)/shard_map/ppermute | solution.py:435
  11.3 5.4 %collective-permute-start.4 = (f32[16,16]{1,0:T(8,128)S(1)}, f32[16,16]{1,0:T(8,128)S(1)}, u32[]{:S(2)}, u32[]{:S(2)}) collective-permute-start(f32[16,16]{1,0:T(8,128)S(1)} %concatenate.8.lines_ref), channel_id=1, source_target_pairs={{0,8},{1,9},{2,10},{3,11},{4,12},{5,13},{6,14},{7,15},{8,0},{9,1},... | collective-permute-start | bytes 3080 | tf_op jit(solution)/shard_map/ppermute | solution.py:435

commit v7 on v6

--- a/solution.py
+++ b/solution.py
@@ -348,20 +348,14 @@
         for h in range(HARM):
             wavenum = WAVENUMBER * (h + 1)
             totals[h] = [half for both in totals[h] for half in (both[:, :width], both[:, width:])]
-            cos_sum, sin_sum = totals[h][0], totals[h][1]
-
-            def loads(m):
-                t = totals[h][m]
-                return [
-                    ox * t[2 + c : 3 + c] + oy * t[4 + c : 5 + c] + (t[8 + c : 9 + c] + t[10 + c : 11 + c])
-                    for c in (0, 1)
-                ]
-
-            (dr, di), (er, ei), (ur, ui), (vr, vi) = loads(2), loads(3), loads(4), loads(5)
-            real = wavenum * (er - di) + TURN * (ur + vi)
-            imag = wavenum * (ei + dr) + TURN * (ui - vr)
-            rows.append(TURN * (wavenum * (sin_sum[0:1] - cos_sum[1:2]) + TURN * real))
-            rows.append(TURN * (wavenum * (cos_sum[0:1] + sin_sum[1:2]) + TURN * imag))
+            cos_sum, sin_sum, d, e, u, v = totals[h]
+
+            def loads(t):
+                return ox * t[2:4] + oy * t[4:6] + (t[8:10] + t[10:12])
+
+            plain = wavenum * sin_sum[:2] + loads((wavenum * TURN) * e + (TURN * TURN) * u)
+            turned = wavenum * cos_sum[:2] + loads((wavenum * TURN) * d - (TURN * TURN) * v)
+            rows.append(TURN * (plain + jnp.concatenate([-turned[1:2], turned[0:1]], axis=0)))
         made.append(jnp.concatenate(rows, axis=0))
     return made
 

time: 35.8 us -> 35.8 us (level)
  transfers between devices with their start and end apart: 5 -> 5, of which waited for: 2 -> 2; matrix products, arithmetic and copies ran while one was open for 0% -> 0% of each run, Pallas kernels for 17% -> 16%
where the time goes in v7:
time: 35.8 us; the launch traced here: 35.5 us
  blocking collectives  14.6 us (41%)
  Pallas kernels  10.1 us (28%)
  starting transfers between devices  7.49 us (21%)
  waiting for transfers between devices  2.64 us (7%)
  between operations  0.68 us (2%)
    all_to_all x1, blocking collectives, shards(): lax.all_to_all(packed, 'wide', split_axis=0, concat_axis=0, tiled=True)  14.6 us
    ppermute x5, starting transfers between devices, swap(): return lax.ppermute(x, 'wide', [(i, i ^ bit) for i in range(nwide)])  7.49 us
    pallas_call x1, Pallas kernels, second_sums(): pl.pallas_call(kernel, out_shape=jax.ShapeDtypeStruct((nwide, rows + 8, l...  2.76 us
    pallas_call x1, Pallas kernels, first_sums(): pl.pallas_call(first_kernel, out_shape=jax.ShapeDtypeStruct((devices, 2 *...  2.75 us
    ppermute x5, waiting for transfers between devices, swap(): return lax.ppermute(x, 'wide', [(i, i ^ bit) for i in range(nwide)])  2.64 us
    pallas_call x1, Pallas kernels, sources(): pl.pallas_call(source_kernel, out_shape=(jax.ShapeDtypeStruct((ROWS, owne...  1.6 us
    pallas_call x1, Pallas kernels, pack(): pl.pallas_call(body, out_shape=(jax.ShapeDtypeStruct((nwide, ROWS * subs,...  1.51 us
    pallas_call x1, Pallas kernels, place(): pl.pallas_call(body, out_shape=(jax.ShapeDtypeStruct((ROWS, owned), BF16)...  1.49 us
  transfers between devices with their start and end apart: 5, of which 2 were waited for; matrix products, arithmetic and copies ran while one was open for 0% of the time, Pallas kernels for 16%

profile of v7, /device:TPU:0, one launch (start us, length us, event | category | flops | bytes accessed | tf_op | source)
XLA Modules:
  0.0 35.5 jit_solution(5481957586257688121)
XLA Ops:
  0.6 0.5 %collective-permute-start = (f32[2,16]{1,0:T(2,128)}, f32[2,16]{1,0:T(2,128)S(1)}, u32[]{:S(2)}, u32[]{:S(2)}) collective-permute-start(f32[2,16]{1,0:T(2,128)} %over_hbm.1), channel_id=1, source_target_pairs={{0,1},{1,0},{2,3},{3,2},{4,5},{5,4},{6,7},{7,6},{8,9},{9,8},{10,11... | collective-permute-start | bytes 392 | tf_op jit(solution)/shard_map/ppermute | solution.py:429
  1.1 2.6 %collective-permute-start.2 = (f32[2,16]{1,0:T(2,128)}, f32[2,16]{1,0:T(2,128)S(1)}, u32[]{:S(2)}, u32[]{:S(2)}) collective-permute-start(f32[2,16]{1,0:T(2,128)} %over_hbm.1), channel_id=1, source_target_pairs={{0,3},{1,2},{2,1},{3,0},{4,7},{5,6},{6,5},{7,4},{8,11},{9,10},{10,... | collective-permute-start | bytes 392 | tf_op jit(solution)/shard_map/ppermute | solution.py:429
  3.8 0.0 collective-permute-start.1
  3.8 1.6 %shard_map.77 = (bf16[32,2048]{1,0:T(8,128)(2,1)S(1)}, bf16[4,16,2048]{2,1,0:T(8,128)(2,1)S(1)}, bf16[2048,16]{1,0:T(8,128)(2,1)S(1)}, s32[1,2048]{1,0:T(1,128)S(1)}, f32[2,16]{1,0:T(2,128)S(1)}) custom-call(bf16[5,16,2048]{2,1,0:T(8,128)(2,1)} %flow_hbm.1, bf16[3,2048]{1,0:T(4,128)(2,1)} %normals_hbm.1, bf16[3,2048]{1,0:T(4,128)(2,1)} %place_hbm.1, ...), custom_call_target="tpu_custom_call" | custom-call | tf_op jit(solution)/shard_map/pallas_call | solution.py:137
  5.4 0.0 collective-permute-done
  5.5 0.0 collective-permute-done.2
  5.5 2.1 %collective-permute-done.1 = f32[2,16]{1,0:T(2,128)S(1)} collective-permute-done((f32[2,16]{1,0:T(2,128)}, f32[2,16]{1,0:T(2,128)S(1)}, u32[]{:S(2)}, u32[]{:S(2)}) %collective-permute-start.1) | collective-permute-done | bytes 160 | tf_op jit(solution)/shard_map/ppermute | solution.py:429
  7.6 1.6 %collective-permute-start.3 = (f32[8,16]{1,0:T(8,128)S(1)}, f32[8,16]{1,0:T(8,128)S(1)}, u32[]{:S(2)}, u32[]{:S(2)}) collective-permute-start(f32[8,16]{1,0:T(8,128)S(1)} %pad_maximum_fusion), channel_id=1, source_target_pairs={{0,4},{1,5},{2,6},{3,7},{4,0},{5,1},{6,2},{7,3},{8,12},{9,13},{10,... | collective-permute-start | bytes 1544 | tf_op jit(solution)/shard_map/ppermute | solution.py:429
  9.2 1.5 %shard_map.78 = (bf16[16,64,128]{2,1,0:T(8,128)(2,1)S(1)}, f32[16,8,128]{2,1,0:T(8,128)S(1)}) custom-call(bf16[32,2048]{1,0:T(8,128)(2,1)S(1)} %get-tuple-element.24.refs_0_, s32[1,2048]{1,0:T(1,128)S(1)} %get-tuple-element.25.refs_1_), custom_call_target="tpu_custom_call" | custom-call | tf_op jit(solution)/shard_map/pallas_call | solution.py:213
  10.7 0.5 %collective-permute-done.3 = f32[8,16]{1,0:T(8,128)S(1)} collective-permute-done((f32[8,16]{1,0:T(8,128)S(1)}, f32[8,16]{1,0:T(8,128)S(1)}, u32[]{:S(2)}, u32[]{:S(2)}) %collective-permute-start.3) | collective-permute-done | bytes 544 | tf_op jit(solution)/shard_map/ppermute | solution.py:429
  11.3 2.6 %collective-permute-start.4 = (f32[16,16]{1,0:T(8,128)S(1)}, f32[16,16]{1,0:T(8,128)S(1)}, u32[]{:S(2)}, u32[]{:S(2)}) collective-permute-start(f32[16,16]{1,0:T(8,128)S(1)} %concatenate.8.lines_ref), channel_id=1, source_target_pairs={{0,8},{1,9},{2,10},{3,11},{4,12},{5,13},{6,14},{7,15},{8,0},{9,1},... | collective-permute-start | bytes 3080 | tf_op jit(solution)/shard_map/ppermute | solution.py:429
  13.9 2.7 %shard_map.79.refs_4_ = f32[8,8,128]{2,1,0:T(8,128)S(1)} custom-call(f32[16,16]{1,0:T(8,128)S(1)} %concatenate.8.lines_ref, bf16[4,16,2048]{2,1,0:T(8,128)(2,1)S(1)} %get-tuple-element.28.weights_ref.refs_2_, bf16[2048,16]{1,0:T(8,128)(2,1)S(1)} %get-tuple-element.29.points_ref.refs_3_), custom_call_target="tpu_custom_call" | custom-call | flops 524288000 | bytes 143360 | tf_op jit(solution)/shard_map/pallas_call | solution.py:398
  16.7 0.0 collective-permute-done.4.refs_1_
  16.7 2.8 %shard_map.80 = bf16[16,72,128]{2,1,0:T(8,128)(2,1)S(1)} custom-call(s32[1]{0:T(128)} %bitcast.refs_0_, f32[16,16]{1,0:T(8,128)S(1)} %collective-permute-done.4.refs_1_, bf16[4,16,2048]{2,1,0:T(8,128)(2,1)S(1)} %get-tuple-element.28.weights_ref.refs_2_, bf16[2048,16]{1,0:T(8,128)(2,1)S(1)} %get-tuple-element.29.points_ref.refs_3_, ...), custom_call_target="tpu_custom_call" | custom-call | flops 524288000 | bytes 143360 | tf_op jit(solution)/shard_map/pallas_call | solution.py:418
  19.5 14.6 %all_to_all.5.refs_0_ = bf16[16,72,128]{2,1,0:T(8,128)(2,1)S(1)} all-to-all(bf16[16,72,128]{2,1,0:T(8,128)(2,1)S(1)} %shard_map.80), channel_id=1, replica_groups=mesh['case'=2,'wide'=16] {'wide'}, dimensions={0} | all-to-all | bytes 589824 | tf_op jit(solution)/shard_map/all_to_all | solution.py:450
  34.0 1.5 %shard_map.81 = (bf16[32,2048]{1,0:T(8,128)(2,1)}, f32[8,16]{1,0:T(8,128)}) custom-call(bf16[16,72,128]{2,1,0:T(8,128)(2,1)S(1)} %all_to_all.5.refs_0_), custom_call_target="tpu_custom_call" | custom-call | tf_op jit(solution)/shard_map/pallas_call | solution.py:272
  (2 shorter events, 0.0 us)
Async XLA Ops:
  0.6 4.8 %collective-permute-start = (f32[2,16]{1,0:T(2,128)}, f32[2,16]{1,0:T(2,128)S(1)}, u32[]{:S(2)}, u32[]{:S(2)}) collective-permute-start(f32[2,16]{1,0:T(2,128)} %over_hbm.1), channel_id=1, source_target_pairs={{0,1},{1,0},{2,3},{3,2},{4,5},{5,4},{6,7},{7,6},{8,9},{9,8},{10,11... | collective-permute-start | bytes 392 | tf_op jit(solution)/shard_map/ppermute | solution.py:429
  1.1 4.3 %collective-permute-start.2 = (f32[2,16]{1,0:T(2,128)}, f32[2,16]{1,0:T(2,128)S(1)}, u32[]{:S(2)}, u32[]{:S(2)}) collective-permute-start(f32[2,16]{1,0:T(2,128)} %over_hbm.1), channel_id=1, source_target_pairs={{0,3},{1,2},{2,1},{3,0},{4,7},{5,6},{6,5},{7,4},{8,11},{9,10},{10,... | collective-permute-start | bytes 392 | tf_op jit(solution)/shard_map/ppermute | solution.py:429
  3.8 3.8 %collective-permute-start.1 = (f32[2,16]{1,0:T(2,128)}, f32[2,16]{1,0:T(2,128)S(1)}, u32[]{:S(2)}, u32[]{:S(2)}) collective-permute-start(f32[2,16]{1,0:T(2,128)} %over_hbm.1), channel_id=1, source_target_pairs={{0,2},{1,3},{2,0},{3,1},{4,6},{5,7},{6,4},{7,5},{8,10},{9,11},{10,... | collective-permute-start | bytes 392 | tf_op jit(solution)/shard_map/ppermute | solution.py:429
  7.6 3.7 %collective-permute-start.3 = (f32[8,16]{1,0:T(8,128)S(1)}, f32[8,16]{1,0:T(8,128)S(1)}, u32[]{:S(2)}, u32[]{:S(2)}) collective-permute-start(f32[8,16]{1,0:T(8,128)S(1)} %pad_maximum_fusion), channel_id=1, source_target_pairs={{0,4},{1,5},{2,6},{3,7},{4,0},{5,1},{6,2},{7,3},{8,12},{9,13},{10,... | collective-permute-start | bytes 1544 | tf_op jit(solution)/shard_map/ppermute | solution.py:429
  11.3 5.4 %collective-permute-start.4 = (f32[16,16]{1,0:T(8,128)S(1)}, f32[16,16]{1,0:T(8,128)S(1)}, u32[]{:S(2)}, u32[]{:S(2)}) collective-permute-start(f32[16,16]{1,0:T(8,128)S(1)} %concatenate.8.lines_ref), channel_id=1, source_target_pairs={{0,8},{1,9},{2,10},{3,11},{4,12},{5,13},{6,14},{7,15},{8,0},{9,1},... | collective-permute-start | bytes 3080 | tf_op jit(solution)/shard_map/ppermute | solution.py:429

commit v8 on v7

--- a/solution.py
+++ b/solution.py
@@ -235,7 +235,7 @@
     group = max(1, 256 // (lanes * subs))
     width = lanes * subs * group
     lows = lax.broadcasted_iota(jnp.int32, (LOW, width), 0).astype(F32)
-    total = jnp.zeros((heights * ROWS, LOW), F32)
+    all_picked, all_spread = [], []
     sums = jnp.zeros((2 * HARM, lanes), F32)
     lower = lax.broadcasted_iota(jnp.int32, (1, lanes), 1) < lanes // 2
     for first in range(0, nwide, group):
@@ -252,10 +252,17 @@
         high = jnp.concatenate(high, axis=1)
         low = jnp.concatenate(low, axis=1)
         spread = (lows == low).astype(F32).astype(BF16)
-        picked = jnp.concatenate(
-            [jnp.where(high == h + 1.0, values, jnp.zeros_like(values)) for h in range(heights)], axis=0
-        )
-        total = total + lax.dot_general(picked, spread, NT_DIMS, preferred_element_type=F32)
+        masks = (lax.broadcasted_iota(jnp.int32, (heights, width), 0).astype(F32) + 1.0 == high).astype(F32)
+        picked = []
+        for h in range(heights):
+            mask = jnp.broadcast_to(masks[h : h + 1], (16, width)).astype(BF16)
+            picked += [values[16 * p : 16 * p + 16] * mask for p in range(ROWS // 16)]
+        picked = jnp.concatenate(picked, axis=0)
+        all_picked.append(picked)
+        all_spread.append(spread)
+    total = lax.dot_general(
+        jnp.concatenate(all_picked, axis=1), jnp.concatenate(all_spread, axis=1), NT_DIMS, preferred_element_type=F32
+    )
     for h in range(heights):
         spectra_ref[:, LOW * h : LOW * h + LOW] = total[ROWS * h : ROWS * h + ROWS].astype(BF16)
     pressure_ref[...] = scale * (sums[:, listeners : 2 * listeners] + sums[:, :listeners])

time: 35.8 us -> 35.8 us (level)
  no operation moved by 1% of the time
where the time goes in v8:
time: 35.8 us; the launch traced here: 35.5 us
  blocking collectives  14.6 us (41%)
  Pallas kernels  10.1 us (28%)
  starting transfers between devices  7.49 us (21%)
  waiting for transfers between devices  2.64 us (7%)
  between operations  0.68 us (2%)
    all_to_all x1, blocking collectives, shards(): lax.all_to_all(packed, 'wide', split_axis=0, concat_axis=0, tiled=True)  14.6 us
    ppermute x5, starting transfers between devices, swap(): return lax.ppermute(x, 'wide', [(i, i ^ bit) for i in range(nwide)])  7.49 us
    pallas_call x1, Pallas kernels, second_sums(): pl.pallas_call(kernel, out_shape=jax.ShapeDtypeStruct((nwide, rows + 8, l...  2.76 us
    pallas_call x1, Pallas kernels, first_sums(): pl.pallas_call(first_kernel, out_shape=jax.ShapeDtypeStruct((devices, 2 *...  2.75 us
    ppermute x5, waiting for transfers between devices, swap(): return lax.ppermute(x, 'wide', [(i, i ^ bit) for i in range(nwide)])  2.64 us
    pallas_call x1, Pallas kernels, sources(): pl.pallas_call(source_kernel, out_shape=(jax.ShapeDtypeStruct((ROWS, owne...  1.6 us
    pallas_call x1, Pallas kernels, pack(): pl.pallas_call(body, out_shape=(jax.ShapeDtypeStruct((nwide, ROWS * subs,...  1.51 us
    pallas_call x1, Pallas kernels, place(): pl.pallas_call(body, out_shape=(jax.ShapeDtypeStruct((ROWS, owned), BF16)...  1.48 us
  transfers between devices with their start and end apart: 5, of which 2 were waited for; matrix products, arithmetic and copies ran while one was open for 0% of the time, Pallas kernels for 16%

profile of v8, /device:TPU:0, one launch (start us, length us, event | category | flops | bytes accessed | tf_op | source)
XLA Modules:
  0.0 35.5 jit_solution(18188567011195425508)
XLA Ops:
  0.6 0.5 %collective-permute-start = (f32[2,16]{1,0:T(2,128)}, f32[2,16]{1,0:T(2,128)S(1)}, u32[]{:S(2)}, u32[]{:S(2)}) collective-permute-start(f32[2,16]{1,0:T(2,128)} %over_hbm.1), channel_id=1, source_target_pairs={{0,1},{1,0},{2,3},{3,2},{4,5},{5,4},{6,7},{7,6},{8,9},{9,8},{10,11... | collective-permute-start | bytes 392 | tf_op jit(solution)/shard_map/ppermute | solution.py:436
  1.1 2.6 %collective-permute-start.2 = (f32[2,16]{1,0:T(2,128)}, f32[2,16]{1,0:T(2,128)S(1)}, u32[]{:S(2)}, u32[]{:S(2)}) collective-permute-start(f32[2,16]{1,0:T(2,128)} %over_hbm.1), channel_id=1, source_target_pairs={{0,3},{1,2},{2,1},{3,0},{4,7},{5,6},{6,5},{7,4},{8,11},{9,10},{10,... | collective-permute-start | bytes 392 | tf_op jit(solution)/shard_map/ppermute | solution.py:436
  3.8 0.0 collective-permute-start.1
  3.8 1.6 %shard_map.77 = (bf16[32,2048]{1,0:T(8,128)(2,1)S(1)}, bf16[4,16,2048]{2,1,0:T(8,128)(2,1)S(1)}, bf16[2048,16]{1,0:T(8,128)(2,1)S(1)}, s32[1,2048]{1,0:T(1,128)S(1)}, f32[2,16]{1,0:T(2,128)S(1)}) custom-call(bf16[5,16,2048]{2,1,0:T(8,128)(2,1)} %flow_hbm.1, bf16[3,2048]{1,0:T(4,128)(2,1)} %normals_hbm.1, bf16[3,2048]{1,0:T(4,128)(2,1)} %place_hbm.1, ...), custom_call_target="tpu_custom_call" | custom-call | tf_op jit(solution)/shard_map/pallas_call | solution.py:137
  5.4 0.0 collective-permute-done
  5.5 0.0 collective-permute-done.2
  5.5 2.1 %collective-permute-done.1 = f32[2,16]{1,0:T(2,128)S(1)} collective-permute-done((f32[2,16]{1,0:T(2,128)}, f32[2,16]{1,0:T(2,128)S(1)}, u32[]{:S(2)}, u32[]{:S(2)}) %collective-permute-start.1) | collective-permute-done | bytes 160 | tf_op jit(solution)/shard_map/ppermute | solution.py:436
  7.6 1.6 %collective-permute-start.3 = (f32[8,16]{1,0:T(8,128)S(1)}, f32[8,16]{1,0:T(8,128)S(1)}, u32[]{:S(2)}, u32[]{:S(2)}) collective-permute-start(f32[8,16]{1,0:T(8,128)S(1)} %pad_maximum_fusion), channel_id=1, source_target_pairs={{0,4},{1,5},{2,6},{3,7},{4,0},{5,1},{6,2},{7,3},{8,12},{9,13},{10,... | collective-permute-start | bytes 1544 | tf_op jit(solution)/shard_map/ppermute | solution.py:436
  9.2 1.5 %shard_map.78 = (bf16[16,64,128]{2,1,0:T(8,128)(2,1)S(1)}, f32[16,8,128]{2,1,0:T(8,128)S(1)}) custom-call(bf16[32,2048]{1,0:T(8,128)(2,1)S(1)} %get-tuple-element.24.refs_0_, s32[1,2048]{1,0:T(1,128)S(1)} %get-tuple-element.25.refs_1_), custom_call_target="tpu_custom_call" | custom-call | tf_op jit(solution)/shard_map/pallas_call | solution.py:213
  10.7 0.5 %collective-permute-done.3 = f32[8,16]{1,0:T(8,128)S(1)} collective-permute-done((f32[8,16]{1,0:T(8,128)S(1)}, f32[8,16]{1,0:T(8,128)S(1)}, u32[]{:S(2)}, u32[]{:S(2)}) %collective-permute-start.3) | collective-permute-done | bytes 544 | tf_op jit(solution)/shard_map/ppermute | solution.py:436
  11.3 2.6 %collective-permute-start.4 = (f32[16,16]{1,0:T(8,128)S(1)}, f32[16,16]{1,0:T(8,128)S(1)}, u32[]{:S(2)}, u32[]{:S(2)}) collective-permute-start(f32[16,16]{1,0:T(8,128)S(1)} %concatenate.8.lines_ref), channel_id=1, source_target_pairs={{0,8},{1,9},{2,10},{3,11},{4,12},{5,13},{6,14},{7,15},{8,0},{9,1},... | collective-permute-start | bytes 3080 | tf_op jit(solution)/shard_map/ppermute | solution.py:436
  13.9 2.7 %shard_map.79.refs_4_ = f32[8,8,128]{2,1,0:T(8,128)S(1)} custom-call(f32[16,16]{1,0:T(8,128)S(1)} %concatenate.8.lines_ref, bf16[4,16,2048]{2,1,0:T(8,128)(2,1)S(1)} %get-tuple-element.28.weights_ref.refs_2_, bf16[2048,16]{1,0:T(8,128)(2,1)S(1)} %get-tuple-element.29.points_ref.refs_3_), custom_call_target="tpu_custom_call" | custom-call | flops 524288000 | bytes 143360 | tf_op jit(solution)/shard_map/pallas_call | solution.py:405
  16.7 0.0 collective-permute-done.4.refs_1_
  16.7 2.8 %shard_map.80 = bf16[16,72,128]{2,1,0:T(8,128)(2,1)S(1)} custom-call(s32[1]{0:T(128)} %bitcast.refs_0_, f32[16,16]{1,0:T(8,128)S(1)} %collective-permute-done.4.refs_1_, bf16[4,16,2048]{2,1,0:T(8,128)(2,1)S(1)} %get-tuple-element.28.weights_ref.refs_2_, bf16[2048,16]{1,0:T(8,128)(2,1)S(1)} %get-tuple-element.29.points_ref.refs_3_, ...), custom_call_target="tpu_custom_call" | custom-call | flops 524288000 | bytes 143360 | tf_op jit(solution)/shard_map/pallas_call | solution.py:425
  19.5 14.6 %all_to_all.5.refs_0_ = bf16[16,72,128]{2,1,0:T(8,128)(2,1)S(1)} all-to-all(bf16[16,72,128]{2,1,0:T(8,128)(2,1)S(1)} %shard_map.80), channel_id=1, replica_groups=mesh['case'=2,'wide'=16] {'wide'}, dimensions={0} | all-to-all | bytes 589824 | tf_op jit(solution)/shard_map/all_to_all | solution.py:457
  34.0 1.5 %shard_map.81 = (bf16[32,2048]{1,0:T(8,128)(2,1)}, f32[8,16]{1,0:T(8,128)}) custom-call(bf16[16,72,128]{2,1,0:T(8,128)(2,1)S(1)} %all_to_all.5.refs_0_), custom_call_target="tpu_custom_call" | custom-call | tf_op jit(solution)/shard_map/pallas_call | solution.py:279
  (2 shorter events, 0.0 us)
Async XLA Ops:
  0.6 4.8 %collective-permute-start = (f32[2,16]{1,0:T(2,128)}, f32[2,16]{1,0:T(2,128)S(1)}, u32[]{:S(2)}, u32[]{:S(2)}) collective-permute-start(f32[2,16]{1,0:T(2,128)} %over_hbm.1), channel_id=1, source_target_pairs={{0,1},{1,0},{2,3},{3,2},{4,5},{5,4},{6,7},{7,6},{8,9},{9,8},{10,11... | collective-permute-start | bytes 392 | tf_op jit(solution)/shard_map/ppermute | solution.py:436
  1.1 4.3 %collective-permute-start.2 = (f32[2,16]{1,0:T(2,128)}, f32[2,16]{1,0:T(2,128)S(1)}, u32[]{:S(2)}, u32[]{:S(2)}) collective-permute-start(f32[2,16]{1,0:T(2,128)} %over_hbm.1), channel_id=1, source_target_pairs={{0,3},{1,2},{2,1},{3,0},{4,7},{5,6},{6,5},{7,4},{8,11},{9,10},{10,... | collective-permute-start | bytes 392 | tf_op jit(solution)/shard_map/ppermute | solution.py:436
  3.8 3.8 %collective-permute-start.1 = (f32[2,16]{1,0:T(2,128)}, f32[2,16]{1,0:T(2,128)S(1)}, u32[]{:S(2)}, u32[]{:S(2)}) collective-permute-start(f32[2,16]{1,0:T(2,128)} %over_hbm.1), channel_id=1, source_target_pairs={{0,2},{1,3},{2,0},{3,1},{4,6},{5,7},{6,4},{7,5},{8,10},{9,11},{10,... | collective-permute-start | bytes 392 | tf_op jit(solution)/shard_map/ppermute | solution.py:436
  7.6 3.7 %collective-permute-start.3 = (f32[8,16]{1,0:T(8,128)S(1)}, f32[8,16]{1,0:T(8,128)S(1)}, u32[]{:S(2)}, u32[]{:S(2)}) collective-permute-start(f32[8,16]{1,0:T(8,128)S(1)} %pad_maximum_fusion), channel_id=1, source_target_pairs={{0,4},{1,5},{2,6},{3,7},{4,0},{5,1},{6,2},{7,3},{8,12},{9,13},{10,... | collective-permute-start | bytes 1544 | tf_op jit(solution)/shard_map/ppermute | solution.py:436
  11.3 5.4 %collective-permute-start.4 = (f32[16,16]{1,0:T(8,128)S(1)}, f32[16,16]{1,0:T(8,128)S(1)}, u32[]{:S(2)}, u32[]{:S(2)}) collective-permute-start(f32[16,16]{1,0:T(8,128)S(1)} %concatenate.8.lines_ref), channel_id=1, source_target_pairs={{0,8},{1,9},{2,10},{3,11},{4,12},{5,13},{6,14},{7,15},{8,0},{9,1},... | collective-permute-start | bytes 3080 | tf_op jit(solution)/shard_map/ppermute | solution.py:436
